TPU v7x, 512 devices: a whole 4x4x16 slice. The times are simulated.
512 devices in a mesh: dp: 8 (over x, z_hi), layer: 4 (over y), tensor: 16 (over z_lo, core).
Axes of the slice: x: 4, y: 4, z: 16 (z_hi: 2, z_lo: 8; z = z_hi * 8 + z_lo), core: 2. Of those that a mesh axis runs over, the one named last changes fastest.
Arguments:
- hidden: bfloat16 [4, 1024, 4096], P('layer', 'dp'), may hold values from -120 to 120
- target: bfloat16 [4, 1024, 1024], P('layer', 'dp'), may hold values from -6 to 6
- value_weight: bfloat16 [4, 4096, 1024], P('layer', None, 'dp'), may hold values from -0.09375 to 0.09375
- quant_scale: float32 [4, 1024], P('layer', 'dp'), may hold values from 0.005 to 0.05
- head_rotation: float32 [4, 128, 128], P('layer'), may hold values from -2.5 to 2.5
- rotation: float32 [4096, 4096], P(('dp', 'layer'), 'tensor'), may hold values from -2.5 to 2.5
Outputs:
- new_rotation: float32 [4096, 4096], P(('dp', 'layer'), 'tensor')
- new_head_rotation: float32 [4, 128, 128], P('layer')
All inputs are finite; a program needn't handle non-finite values.
Results may differ from a plain program's by a relative error of at most 0.022.
Values may be sent and summed in bfloat16 or wider, within the bound.
No kernel may reach another device: no remote copies, remote signals or barrier semaphores. Data moves between devices by JAX's collectives and lax.ppermute only.
A program may use at most 64 MiB of HBM per device.

v0:
```python
import math

import jax
import jax.numpy as jnp
from jax import lax
from jax.sharding import PartitionSpec as P

D = 4096
HEAD = 128


precise = lax.Precision.HIGHEST
contract_first = (((0,), (0,)), ((), ()))
contract_second = (((1,), (1,)), ((), ()))


def apply_heads(matrix, head_matrix):
    height = matrix.shape[0]
    width_head = head_matrix.shape[0]
    groups = matrix.shape[1] // width_head
    shaped = matrix.reshape(height, groups, width_head)
    turned = jnp.einsum("jhp,pq->jhq", shaped, head_matrix, precision=precise)
    return turned.reshape(height, matrix.shape[1])


def head_update(stored, gradient):
    root_head = math.sqrt(stored.shape[0])
    head_skew = (
        jnp.dot(gradient, stored.T, precision=precise)
        - jnp.dot(stored, gradient.T, precision=precise)
    ) / root_head
    head_step = 4.0 / jnp.sqrt(jnp.sum(head_skew * head_skew) + 1e-12)
    head_base = jnp.dot(head_skew, stored, precision=precise)
    iterate = stored - head_step * head_base
    iterate = stored - 0.5 * head_step * (
        head_base + jnp.dot(head_skew, iterate, precision=precise)
    )
    return iterate


def body(hidden, target, value_weight, quant_scale, head_rotation, rotation):
    root_width = math.sqrt(D)
    hidden_rows = hidden[0]
    weights = value_weight[0]
    scales = quant_scale[0][None, :]
    stored = head_rotation[0]
    head_matrix = stored / math.sqrt(HEAD)
    token_count = hidden_rows.shape[0] * lax.axis_size("dp")
    col_block = rotation.shape[1]
    block_low = rotation.astype(jnp.bfloat16)
    rotation_cols = lax.all_gather(block_low, ("dp", "layer"), axis=0, tiled=True)
    rotated = (
        jnp.dot(hidden_rows, rotation_cols, preferred_element_type=jnp.float32) / root_width
    ).astype(jnp.bfloat16)
    unmixed = (
        lax.dot_general(rotation_cols, weights, contract_first, preferred_element_type=jnp.float32)
        / root_width
    )
    mixed = apply_heads(unmixed, head_matrix)
    tangent = jnp.tanh(mixed / scales)
    quantized = (scales * tangent).astype(jnp.bfloat16)
    all_heads = lax.all_gather(quantized, "dp", axis=1, tiled=True)
    values = lax.psum(
        jnp.dot(rotated, all_heads, preferred_element_type=jnp.float32).astype(jnp.bfloat16),
        "tensor",
    ).astype(jnp.float32)
    value_grad = (2.0 * (values - target[0].astype(jnp.float32)) / token_count).astype(jnp.bfloat16)
    rotated_grad = lax.dot_general(
        value_grad, all_heads, contract_second, preferred_element_type=jnp.float32
    ).astype(jnp.bfloat16)
    quant_part = lax.dot_general(
        rotated, value_grad, contract_first, preferred_element_type=jnp.float32
    )
    quant_grad = lax.psum_scatter(
        quant_part.astype(jnp.bfloat16), "dp", scatter_dimension=1, tiled=True
    ).astype(jnp.float32)
    mixed_grad = quant_grad * (1.0 - tangent * tangent)
    mixed_low = mixed_grad.astype(jnp.bfloat16)
    heads_here = weights.shape[1] // HEAD
    folded_rows = jnp.einsum(
        "pq,jhp->hqj",
        head_matrix,
        weights.reshape(D, heads_here, HEAD).astype(jnp.float32),
        precision=precise,
    )
    folded_rows = folded_rows.astype(jnp.bfloat16).reshape(weights.shape[1], D)
    head_part = jnp.einsum(
        "jhp,jhq->pq",
        unmixed.reshape(col_block, heads_here, HEAD),
        mixed_grad.reshape(col_block, heads_here, HEAD),
        precision=precise,
    )
    head_grad = lax.psum(head_part, ("dp", "tensor"))
    left_factors = jnp.concatenate([hidden_rows, folded_rows], 0)
    right_factors = jnp.concatenate([rotated_grad, mixed_low.T], 0)
    columns = lax.all_to_all(left_factors, ("dp", "layer"), split_axis=1, concat_axis=0, tiled=True)
    gradient = lax.dot_general(
        columns,
        lax.all_gather(right_factors, ("dp", "layer"), axis=0, tiled=True),
        contract_first,
        preferred_element_type=jnp.float32,
    )
    gradient_low = gradient.astype(jnp.bfloat16)
    gradient_cols = lax.all_gather(gradient_low, ("dp", "layer"), axis=0, tiled=True)
    first_term = lax.dot_general(
        rotation_cols, gradient_low, contract_second, preferred_element_type=jnp.float32
    )
    second_term = lax.dot_general(
        gradient_cols, block_low, contract_second, preferred_element_type=jnp.float32
    )
    skew_cols = lax.psum_scatter(
        ((first_term - second_term) / root_width).astype(jnp.bfloat16),
        "tensor",
        scatter_dimension=0,
        tiled=True,
    ).astype(jnp.float32)
    skew = skew_cols.T
    square_part = jnp.sum(skew * skew)
    square_sum = lax.psum(square_part, ("dp", "layer", "tensor"))
    step_size = 16.0 / jnp.sqrt(square_sum + 1e-12)
    skew_full_rows = lax.all_gather(skew.astype(jnp.bfloat16), "tensor", axis=1, tiled=True)
    base_term = jnp.dot(skew_full_rows, rotation_cols, preferred_element_type=jnp.float32)
    iterate = rotation - step_size * base_term
    iterate_cols = lax.all_gather(iterate.astype(jnp.bfloat16), ("dp", "layer"), axis=0, tiled=True)
    iterate = rotation - 0.5 * step_size * (
        base_term + jnp.dot(skew_full_rows, iterate_cols, preferred_element_type=jnp.float32)
    )
    return (iterate, head_update(stored, head_grad)[None])


def solution(mesh):
    in_specs = (
        P("layer", "dp", None),
        P("layer", "dp", None),
        P("layer", None, "dp"),
        P("layer", "dp"),
        P("layer", None, None),
        P(("dp", "layer"), "tensor"),
    )
    out_specs = (P(("dp", "layer"), "tensor"), P("layer", None, None))
    return jax.shard_map(body, mesh=mesh, in_specs=in_specs, out_specs=out_specs, check_vma=False)
```

profile of v0, /device:TPU:1, one launch (start us, length us, event | category | flops | bytes accessed | tf_op | source)
XLA Modules:
  0.0 1525.2 jit_solution(14361094586554635549)
XLA Ops:
  7.2 0.0 copy-start
  7.2 0.0 copy-start.5
  7.2 0.0 copy-start.9
  7.2 0.0 all-gather.6.cloned.1.call-start
  7.2 1.6 convert_element_type.69
  8.9 0.0 all-gather.6.cloned.1.call-update
  8.9 0.0 all-reduce.3.cloned.1.call-start
  8.9 139.8 %all-gather.6.cloned.1.call-done = bf16[4096,256]{1,0:T(8,128)(2,1)} async-done(((bf16[128,256]{1,0:T(8,128)(2,1)}), bf16[4096,256]{1,0:T(8,128)(2,1)}) %all-gather.6.cloned.1.call-update) | async-done | bytes 2097168 | tf_op jit(solution)/shard_map/all_gather | solution.py:51
  148.7 0.0 copy-done
  148.7 2.5 convolution_multiply_fusion
  151.2 0.0 copy-start.7
  151.2 0.0 copy-done.5
  151.2 1.0 multiply_convert_fusion
  152.2 69.3 %all_gather.19 = bf16[256,1024]{0,1:T(8,128)(2,1)S(1)} all-gather(bf16[256,128]{0,1:T(8,128)(2,1)S(1)} %get-tuple-element.2), channel_id=1, replica_groups=mesh['dp'=8,'layer'=4,'tensor'=16] {'dp'}, dimensions={1}, use_global_device_ids=true | all-gather | bytes 589824 | tf_op jit(solution)/shard_map/all_gather | solution.py:62
  221.5 1.9 fusion.6
  223.4 1.0 convolution_convert_fusion.2
  224.4 0.0 all-reduce.3.cloned.1.call-update
  224.4 0.0 reduce-scatter.3.cloned.1.call-start
  224.5 199.8 %all-reduce.3.cloned.1.call-done = bf16[128,1024]{1,0:T(8,128)(2,1)} async-done(((bf16[128,1024]{1,0:T(8,128)(2,1)}), bf16[128,1024]{1,0:T(8,128)(2,1)}) %all-reduce.3.cloned.1.call-update) | async-done | bytes 262160 | tf_op jit(solution)/shard_map/psum | solution.py:63
  424.3 2.1 convolution_convert_fusion.1
  426.4 0.0 reduce-scatter.3.cloned.1.call-update
  426.4 2.3 copy.15
  428.7 2.0 fusion.2
  430.7 2.3 copy.23
  433.0 3.2 pad_maximum_fusion
  436.1 9.8 all-to-all-start
  445.9 0.0 all-gather.8.cloned.1.call-start
  446.0 1.4 convolution_convert_fusion.4
  447.4 156.8 %reduce-scatter.3.cloned.1.call-done = bf16[256,128]{0,1:T(8,128)(2,1)} async-done(((bf16[256,1024]{0,1:T(8,128)(2,1)}), bf16[256,128]{0,1:T(8,128)(2,1)}) %reduce-scatter.3.cloned.1.call-update) | async-done | bytes 65552 | tf_op jit(solution)/shard_map/reduce_scatter | solution.py:74
  604.2 0.9 fusion.19
  605.1 0.7 pad_maximum_fusion.1
  605.8 0.0 all-gather.8.cloned.1.call-update
  605.8 0.0 all-gather.10.cloned.1.call-start
  605.8 0.0 all-to-all-done
  605.8 4.1 copy.17
  609.9 151.1 %all-gather.8.cloned.1.call-done = bf16[8192,256]{1,0:T(8,128)(2,1)} async-done(((bf16[256,256]{1,0:T(8,128)(2,1)}), bf16[8192,256]{1,0:T(8,128)(2,1)}) %all-gather.8.cloned.1.call-update) | async-done | bytes 4194320 | tf_op jit(solution)/shard_map/all_gather | solution.py:99
  761.0 4.4 convolution_convert_fusion.3
  765.5 0.0 all-gather.10.cloned.1.call-update
  765.5 0.0 copy-start.6
  765.5 0.0 reduce-scatter.5.cloned.1.call-start
  765.5 3.0 convolution_bitcast_fusion
  768.5 128.6 %all-gather.10.cloned.1.call-done = bf16[4096,256]{1,0:T(8,128)(2,1)} async-done(((bf16[128,256]{1,0:T(8,128)(2,1)}), bf16[4096,256]{1,0:T(8,128)(2,1)}) %all-gather.10.cloned.1.call-update) | async-done | bytes 2097168 | tf_op jit(solution)/shard_map/all_gather | solution.py:104
  897.1 4.0 fusion.1
  901.1 0.0 reduce-scatter.5.cloned.1.call-update
  901.1 0.0 all-gather.12.cloned.1.call-start
  901.2 89.7 %reduce-scatter.5.cloned.1.call-done = bf16[256,128]{0,1:T(8,128)(2,1)} async-done(((bf16[4096,128]{0,1:T(8,128)(2,1)}), bf16[256,128]{0,1:T(8,128)(2,1)}) %reduce-scatter.5.cloned.1.call-update) | async-done | bytes 65552 | tf_op jit(solution)/shard_map/reduce_scatter | solution.py:111
  990.9 0.0 all-gather.12.cloned.1.call-update
  990.9 0.0 all-reduce.5.cloned.1.call-start
  991.0 2.0 fusion.15
  993.0 1.5 multiply_reduce_fusion
  994.4 0.0 all-reduce.5.cloned.1.call-update
  994.5 0.0 all-gather.14.cloned.1.call-start
  994.5 111.9 %psum.22 = f32[]{:T(128)} all-reduce(f32[]{:T(128)} %multiply_reduce_fusion), channel_id=1, replica_groups=mesh['dp'=8,'layer'=4,'tensor'=16] {'dp','layer','tensor'}, use_global_device_ids=true, to_apply=%region_4.0 | all-reduce | flops 1 | bytes 8 | tf_op jit(solution)/shard_map/psum | solution.py:119
  1107.1 0.0 all-gather.12.cloned.1.call-done
  1107.1 2.3 subtract_convert_fusion
  1109.5 0.0 all-gather.14.cloned.1.call-update
  1109.5 278.3 %all-reduce.5.cloned.1.call-done = f32[128,128]{1,0:T(8,128)} async-done(((f32[128,128]{1,0:T(8,128)}), f32[128,128]{1,0:T(8,128)}) %all-reduce.5.cloned.1.call-update) | async-done | bytes 65552 | tf_op jit(solution)/shard_map/psum | solution.py:93
  1387.8 1.1 fusion.23
  1388.9 0.1 copy.20
  1389.0 0.6 multiply_reduce_fusion.1
  1390.3 0.2 fusion.21
  1390.5 0.8 fusion.9
  1391.3 124.4 %all-gather.14.cloned.1.call-done = bf16[4096,256]{1,0:T(8,128)(2,1)} async-done(((bf16[128,256]{1,0:T(8,128)(2,1)}), bf16[4096,256]{1,0:T(8,128)(2,1)}) %all-gather.14.cloned.1.call-update) | async-done | bytes 2097168 | tf_op jit(solution)/shard_map/all_gather | solution.py:124
  1515.7 3.0 fusion.5
  (13 shorter events, 0.0 us)
Async XLA Ops:
  7.2 141.5 %copy-start = (bf16[1,4096,128]{2,1,0:T(8,128)(2,1)S(1)}, bf16[1,4096,128]{2,1,0:T(8,128)(2,1)}, u32[]{:S(2)}) copy-start(bf16[1,4096,128]{2,1,0:T(8,128)(2,1)} %param.8) | copy-start | bytes 3145732
  7.2 144.0 %copy-start.5 = (f32[1,128,128]{2,1,0:T(8,128)S(1)}, f32[1,128,128]{2,1,0:T(8,128)}, u32[]{:S(2)}) copy-start(f32[1,128,128]{2,1,0:T(8,128)} %param.10) | copy-start | bytes 196612
  7.2 144.0 %copy-start.9 = (f32[1,128]{1,0:T(1,128)S(1)}, f32[1,128]{1,0:T(1,128)}, u32[]{:S(2)}) copy-start(f32[1,128]{1,0:T(1,128)} %param.9) | copy-start | bytes 1540
  7.2 141.5 %all-gather.6.cloned.1.call-start = ((), (), s32[]{:S(2)}) async-start(), calls=%async_computation.3 | async-start | bytes 2162688 | tf_op jit(solution)/shard_map/all_gather | solution.py:51
  8.9 415.4 %all-reduce.3.cloned.1.call-start = ((), (), s32[]{:S(2)}) async-start(), calls=%async_computation.4 | async-start | bytes 524288 | tf_op jit(solution)/shard_map/psum | solution.py:63
  148.7 72.8 %copy-start.1 = (bf16[4096,256]{1,0:T(8,128)(2,1)S(1)}, bf16[4096,256]{1,0:T(8,128)(2,1)}, u32[]{:S(2)}) copy-start(bf16[4096,256]{1,0:T(8,128)(2,1)} %all-gather.6.cloned.1.call-done) | copy-start | bytes 6291460
  151.2 1.0 copy-start.7
  221.5 1.9 copy-start.2
  221.5 202.8 %copy-start.4 = (bf16[1,128,1024]{2,1,0:T(8,128)(2,1)S(1)}, bf16[1,128,1024]{2,1,0:T(8,128)(2,1)}, u32[]{:S(2)}) copy-start(bf16[1,128,1024]{2,1,0:T(8,128)(2,1)} %param.7) | copy-start | bytes 786436
  224.4 379.7 %reduce-scatter.3.cloned.1.call-start = ((), (), s32[]{:S(2)}) async-start(), calls=%async_computation.5 | async-start | bytes 589824 | tf_op jit(solution)/shard_map/reduce_scatter | solution.py:74
  436.1 169.7 %all-to-all-start = ((bf16[256,32,128]{0,2,1:T(8,128)(2,1)}), bf16[256,32,128]{0,2,1:T(8,128)(2,1)}, u32[]{:S(2)}, u32[]{:S(2)}) async-start(bf16[256,32,128]{0,2,1:T(8,128)(2,1)} %pad_maximum_fusion), calls=%async_computation | async-start | bytes 4194304 | tf_op jit(solution)/shard_map/all_to_all | solution.py:96
  445.9 315.1 %all-gather.8.cloned.1.call-start = ((), (), s32[]{:S(2)}) async-start(), calls=%async_computation.6 | async-start | bytes 4325376 | tf_op jit(solution)/shard_map/all_gather | solution.py:99
  605.8 291.3 %all-gather.10.cloned.1.call-start = ((), (), s32[]{:S(2)}) async-start(), calls=%async_computation.7 | async-start | bytes 2162688 | tf_op jit(solution)/shard_map/all_gather | solution.py:104
  765.5 131.6 %copy-start.6 = (bf16[128,256]{1,0:T(8,128)(2,1)S(1)}, bf16[128,256]{1,0:T(8,128)(2,1)}, u32[]{:S(2)}) copy-start(bf16[128,256]{1,0:T(8,128)(2,1)} %convert_element_type.69) | copy-start | bytes 196612
  765.5 225.4 %reduce-scatter.5.cloned.1.call-start = ((), (), s32[]{:S(2)}) async-start(), calls=%async_computation.8 | async-start | bytes 1114112 | tf_op jit(solution)/shard_map/reduce_scatter | solution.py:111
  768.5 222.5 %copy-start.8 = (bf16[256,128]{0,1:T(8,128)(2,1)S(1)}, bf16[256,128]{0,1:T(8,128)(2,1)}, u32[]{:S(2)}) copy-start(bf16[256,128]{0,1:T(8,128)(2,1)} %reduce-scatter.3.cloned.1.call-done) | copy-start | bytes 196612
  768.5 338.6 %copy-start.3 = (f32[128,256]{1,0:T(8,128)S(1)}, f32[128,256]{1,0:T(8,128)}, u32[]{:S(2)}) copy-start(f32[128,256]{1,0:T(8,128)} %param.11) | copy-start | bytes 393220
  901.1 206.0 %all-gather.12.cloned.1.call-start = ((), (), s32[]{:S(2)}) async-start(), calls=%async_computation.9 | async-start | bytes 1114112 | tf_op jit(solution)/shard_map/all_gather | solution.py:121
  990.9 396.8 %all-reduce.5.cloned.1.call-start = ((), (), s32[]{:S(2)}) async-start(), calls=%async_computation.11 | async-start | bytes 131072 | tf_op jit(solution)/shard_map/psum | solution.py:93
  994.5 521.3 %all-gather.14.cloned.1.call-start = ((), (), s32[]{:S(2)}) async-start(), calls=%async_computation.10 | async-start | bytes 2162688 | tf_op jit(solution)/shard_map/all_gather | solution.py:124
Sparse Core Ops, SparseCore 0:
  13.0 135.6 all-gather.5
  224.5 199.6 all-reduce.2
  429.4 174.7 reduce-scatter.2
  608.4 152.5 all-gather.7
  765.6 131.4 all-gather.9
  901.3 89.5 reduce-scatter.4
  993.1 80.8 all-gather.11
  1078.4 309.2 all-reduce.4
  1393.0 122.7 all-gather.13
where the time goes:
time: 1530 us
  waiting for transfers between devices  1270 us (83%)
  blocking collectives  181 us (12%)
  matrix products  32.7 us (2%)
  between operations  15.4 us (1%)
    psum x1, waiting for transfers between devices, body(): head_grad = lax.psum(head_part, ('dp', 'tensor'))  278 us
    psum x1, waiting for transfers between devices, body(): lax.psum(jnp.dot(rotated, all_heads, preferred_element_type=jnp.float32)....  200 us
    reduce_scatter x1, waiting for transfers between devices, body(): lax.psum_scatter(quant_part.astype(jnp.bfloat16), 'dp', scatter_dimension...  157 us
    all_gather x1, waiting for transfers between devices, body(): lax.all_gather(right_factors, ('dp', 'layer'), axis=0, tiled=True)  151 us
    all_gather x1, waiting for transfers between devices, body(): lax.all_gather(block_low, ('dp', 'layer'), axis=0, tiled=True)  140 us
    all_gather x1, waiting for transfers between devices, body(): lax.all_gather(gradient_low, ('dp', 'layer'), axis=0, tiled=True)  129 us
    all_gather x1, waiting for transfers between devices, body(): lax.all_gather(iterate.astype(jnp.bfloat16), ('dp', 'layer'), axis=0, til...  124 us
    psum x1, blocking collectives, body(): square_sum = lax.psum(square_part, ('dp', 'layer', 'tensor'))  112 us
  transfers between devices with their start and end apart: 10, of which 8 were waited for; matrix products, arithmetic and copies ran while one was open for 2% of the time, Pallas kernels for 0%

commit v1 on v0

v1 whole, which is shorter than its diff:
```python
import math

import jax
import jax.numpy as jnp
from jax import lax
from jax.sharding import Mesh, PartitionSpec as P

D = 4096
HEAD = 128
SIZES = {"x": 4, "zh": 2, "y": 4, "zl": 8, "c": 2}
ALL = tuple(SIZES)
ROWS = 128
COLS = 256

precise = lax.Precision.HIGHEST
first = (((0,), (0,)), ((), ()))
second = (((1,), (1,)), ((), ()))
plain = (((1,), (0,)), ((), ()))


def mul(a, b, dims=plain, precision=None):
    return lax.dot_general(a, b, dims, precision=precision, preferred_element_type=jnp.float32)


def count(axes):
    return math.prod(SIZES[a] for a in axes)


def exchange(blocks, axes):
    n = count(axes)
    flat = blocks.reshape((n * blocks.shape[1],) + blocks.shape[2:])
    out = lax.all_to_all(flat, axes, split_axis=0, concat_axis=0, tiled=True)
    return out.reshape(blocks.shape)


def gather(block, axes):
    return exchange(jnp.broadcast_to(block[None], (count(axes),) + block.shape), axes)


def swap(block, axis):
    return lax.ppermute(block, axis, [(0, 1), (1, 0)])


def added(blocks):
    return jnp.sum(blocks.astype(jnp.float32), 0)


def split_at(array, axis, index):
    mine = lax.dynamic_index_in_dim(array, index, axis, keepdims=False)
    other = lax.dynamic_index_in_dim(array, 1 - index, axis, keepdims=False)
    return mine, other


def head_update(stored, gradient):
    root_head = math.sqrt(stored.shape[0])
    head_skew = (
        jnp.dot(gradient, stored.T, precision=precise)
        - jnp.dot(stored, gradient.T, precision=precise)
    ) / root_head
    head_step = 4.0 / jnp.sqrt(jnp.sum(head_skew * head_skew) + 1e-12)
    head_base = jnp.dot(head_skew, stored, precision=precise)
    iterate = stored - head_step * head_base
    iterate = stored - 0.5 * head_step * (
        head_base + jnp.dot(head_skew, iterate, precision=precise)
    )
    return iterate


def body(hidden, target, value_weight, quant_scale, head_rotation, rotation):
    root_width = math.sqrt(D)
    zh, core = lax.axis_index("zh"), lax.axis_index("c")
    tensor = lax.axis_index(("zl", "c"))
    plane, line = ("x", "y"), ("zl",)
    low = jnp.bfloat16
    rows = hidden[0]
    weights = value_weight[0]
    stored = head_rotation[0]
    head_matrix = stored / math.sqrt(HEAD)
    scales = quant_scale[0][:, None]

    block_low = rotation.astype(low)
    block_far = swap(block_low, "zh")
    panel_own = gather(block_low, plane).reshape(D // 2, COLS)
    panel_far = gather(block_far, plane).reshape(D // 2, COLS)

    rows_own, rows_far = split_at(rows.reshape(ROWS, 4, 2, D // 8), 2, zh)
    weights_own, weights_far = split_at(weights.reshape(4, 2, D // 8, HEAD), 1, zh)
    folded = mul(head_matrix, weights.astype(jnp.float32), (((0,), (1,)), ((), ())), precise)
    left = jnp.concatenate([rows, folded.astype(low)], 0)
    left_own, left_far = split_at(left.reshape(2 * ROWS, 4, 2, D // 8), 2, zh)
    target_own, target_far = split_at(target[0].reshape(ROWS, 4, 2, HEAD), 2, zh)
    target_here = jnp.concatenate(
        [target_own.reshape(ROWS, 4 * HEAD), target_far.reshape(ROWS, 4 * HEAD)], 1
    )
    target_here = lax.dynamic_slice_in_dim(target_here, tensor * 8, 8, 0)

    unmixed = (
        mul(weights_own.reshape(D // 2, HEAD), panel_own, first)
        + mul(weights_far.reshape(D // 2, HEAD), panel_far, first)
    ) / root_width
    mixed = mul(head_matrix, unmixed, first, precise)
    tangent = jnp.tanh(mixed / scales)
    quantized = (scales * tangent).astype(low)
    quantized_far = swap(quantized, "zh")
    heads_own = gather(quantized, ("x",)).reshape(4 * HEAD, COLS)
    heads_far = gather(quantized_far, ("x",)).reshape(4 * HEAD, COLS)
    rotated = (
        (
            mul(rows_own.reshape(ROWS, D // 2), panel_own)
            + mul(rows_far.reshape(ROWS, D // 2), panel_far)
        )
        / root_width
    ).astype(low)
    heads = jnp.concatenate([heads_own, heads_far], 0)

    part = mul(rotated, heads, second).astype(low)
    values = added(exchange(part.reshape(16, 8, 8 * HEAD), ("zl", "c")))
    value_grad = (2.0 * (values - target_here.astype(jnp.float32)) / 1024).astype(low)
    value_grad = gather(value_grad, ("zl", "c")).reshape(ROWS, 8 * HEAD)

    grad_own, grad_far = value_grad[:, : 4 * HEAD], value_grad[:, 4 * HEAD :]
    quant_far = mul(grad_far, rotated, first).astype(low)
    quant_far = added(exchange(quant_far.reshape(4, HEAD, COLS), ("x",))).astype(low)
    quant_far = swap(quant_far, "zh")
    quant_own = mul(grad_own, rotated, first).astype(low)
    quant_own = added(exchange(quant_own.reshape(4, HEAD, COLS), ("x",)))
    quant_grad = quant_own + quant_far.astype(jnp.float32)
    mixed_grad = quant_grad * (1.0 - tangent * tangent)
    rotated_grad = mul(value_grad, heads).astype(low)

    right = jnp.concatenate([rotated_grad, mixed_grad.astype(low)], 0)
    part_far = mul(left_far.reshape(2 * ROWS, D // 2), right, first).astype(low)
    part_far = added(exchange(part_far.reshape(16, ROWS, COLS), plane)).astype(low)
    part_far = swap(part_far, "zh")
    part_own = mul(left_own.reshape(2 * ROWS, D // 2), right, first).astype(low)
    part_own = added(exchange(part_own.reshape(16, ROWS, COLS), plane))
    gradient = (part_own + part_far.astype(jnp.float32)).astype(low)

    head_part = mul(unmixed, mixed_grad, second, precise)
    head_part = added(exchange(head_part.reshape(16, 8, HEAD), ("zl", "c")))
    head_grad = lax.all_gather(head_part, ("x", "zh", "zl", "c"), axis=0, tiled=False)
    head_grad = jnp.sum(head_grad.reshape(8, HEAD, HEAD), 0)
    new_head = head_update(stored, head_grad)

    panels = jnp.stack(
        [jnp.where(zh == 0, panel_own, panel_far), jnp.where(zh == 0, panel_far, panel_own)]
    ).reshape(2, 4, 2, 2, ROWS, COLS)
    panels = panels.transpose(1, 0, 2, 3, 4, 5).reshape(8, 2, COLS, COLS)
    panel_core, panel_mate = split_at(panels, 1, core)
    panel_core = panel_core.reshape(D // 2, COLS)
    panel_mate = panel_mate.reshape(D // 2, COLS)

    product_mate = (mul(panel_mate, gradient, second) / root_width).astype(low)
    product_mate = swap(product_mate, "c")
    product_core = mul(panel_core, gradient, second) / root_width
    product = (product_core + product_mate.astype(jnp.float32)).astype(low)
    product = added(exchange(product.reshape(8, COLS, ROWS), line))
    odd = lax.axis_index("y") % 2
    halves = product.reshape(2, ROWS, ROWS)
    mirrored = []
    for turn in range(2):
        pairs = [
            (p * 16 + k, (2 * k + (turn ^ (p & 1))) * 16 + p // 2)
            for p in range(32)
            for k in range(16)
        ]
        piece = jnp.where(odd == turn, halves[0], halves[1])
        mirrored.append(lax.ppermute(piece, ALL, pairs))
    mirror = jnp.concatenate(
        [
            jnp.where(odd == 0, mirrored[0], mirrored[1]),
            jnp.where(odd == 0, mirrored[1], mirrored[0]),
        ],
        1,
    )
    skew = product.T - mirror
    skew_low = skew.astype(low)

    skew_core = gather(skew_low, line)
    skew_mate = swap(skew_core, "c")
    wide_core = skew_core.transpose(1, 0, 2)
    wide_mate = skew_mate.transpose(1, 0, 2)
    base = mul(wide_core.reshape(ROWS, D // 2), panel_core) + mul(
        wide_mate.reshape(ROWS, D // 2), panel_mate
    )

    square = jnp.sum(jnp.square(skew_core.astype(jnp.float32))) + jnp.sum(
        jnp.square(skew_mate.astype(jnp.float32))
    )
    high = square.astype(low)
    rest = square - high.astype(jnp.float32)
    middle = rest.astype(low)
    least = (rest - middle.astype(jnp.float32)).astype(low)
    terms = jnp.stack([high, middle, least])[:, None]
    extra = jnp.pad(jnp.broadcast_to(terms, (3, COLS)), ((0, 13), (0, 0)))
    message = jnp.concatenate([base.astype(low), extra], 0)
    message_far = swap(message, "zh")
    all_own = gather(message, plane)
    all_far = gather(message_far, plane)

    wide = jnp.where(
        core == 0,
        jnp.stack([wide_core, wide_mate], 2),
        jnp.stack([wide_mate, wide_core], 2),
    )
    wide_own, wide_far = split_at(wide.reshape(ROWS, 4, 2, D // 8), 2, zh)
    twice = mul(
        wide_own.reshape(ROWS, D // 2), all_own[:, :ROWS].reshape(D // 2, COLS)
    ) + mul(wide_far.reshape(ROWS, D // 2), all_far[:, :ROWS].reshape(D // 2, COLS))
    square_sum = jnp.sum(all_own[:, ROWS : ROWS + 3, 0].astype(jnp.float32)) + jnp.sum(
        all_far[:, ROWS : ROWS + 3, 0].astype(jnp.float32)
    )
    step_size = 16.0 / jnp.sqrt(square_sum + 1e-12)
    iterate = rotation - step_size * base + 0.5 * step_size * step_size * twice
    return (iterate, new_head[None])


def solution(mesh):
    split = Mesh(mesh.devices.reshape(tuple(SIZES.values())), ALL)
    dp, tensor = ("x", "zh"), ("zl", "c")
    in_specs = (
        P("y", dp, None),
        P("y", dp, None),
        P("y", None, dp),
        P("y", dp),
        P("y", None, None),
        P(("x", "zh", "y"), tensor),
    )
    out_specs = (P(("x", "zh", "y"), tensor), P("y", None, None))
    return jax.shard_map(body, mesh=split, in_specs=in_specs, out_specs=out_specs, check_vma=False)
```

time: 1530 us -> 464 us (0.30)
  waiting for transfers between devices: 1270 us -> 121 us
  starting transfers between devices: 10.1 us -> 145 us
  blocking collectives: 181 us -> 130 us
  local copies, waits for them, and re-layouts: 8.78 us -> 24.5 us
    all_gather x5 -> x0, waiting for transfers between devices: 544 us -> none  [the longest x1 151 us: body(): lax.all_gather(right_factors, ('dp', 'layer'), axis=0, tiled=True)]
    psum x2 -> x0, waiting for transfers between devices: 478 us -> none  [the longest x1 278 us: body(): head_grad = lax.psum(head_part, ('dp', 'tensor'))]
    reduce_scatter x2 -> x0, waiting for transfers between devices: 247 us -> none  [the longest x1 157 us: body(): lax.psum_scatter(quant_part.astype(jnp.bfloat16), 'dp', scatter_dimension...]
    psum x1 -> x0, blocking collectives: 112 us -> none  [body(): square_sum = lax.psum(square_part, ('dp', 'layer', 'tensor'))]
    all_to_all x1 -> x14, waiting for transfers between devices: 0.01 us -> 100 us  [exchange(): out = lax.all_to_all(flat, axes, split_axis=0, concat_axis=0, tiled=True)]
    all_to_all x1 -> x14, starting transfers between devices: 9.78 us -> 79 us  [exchange(): out = lax.all_to_all(flat, axes, split_axis=0, concat_axis=0, tiled=True)]
    ppermute x0 -> x9, starting transfers between devices: none -> 65.9 us  [the longest x7 50.7 us: swap(): return lax.ppermute(block, axis, [(0, 1), (1, 0)])]
    all_to_all x0 -> x1, blocking collectives: none -> 45.9 us  [exchange(): out = lax.all_to_all(flat, axes, split_axis=0, concat_axis=0, tiled=True)]
  transfers between devices with their start and end apart: 10 -> 23, of which waited for: 8 -> 16; matrix products, arithmetic and copies ran while one was open for 2% -> 8% of each run, Pallas kernels for 0% -> 0%
where the time goes in v1:
time: 464 us; the launch traced here: 461 us
  starting transfers between devices  145 us (31%)
  blocking collectives  130 us (28%)
  waiting for transfers between devices  121 us (26%)
  matrix products  25.8 us (6%)
  local copies, waits for them, and re-layouts  24.5 us (5%)
  other arithmetic  10 us (2%)
  between operations  4.67 us (1%)
    all_to_all x14, waiting for transfers between devices, exchange(): out = lax.all_to_all(flat, axes, split_axis=0, concat_axis=0, tiled=True)  100 us
    all_gather x1, blocking collectives, body(): lax.all_gather(head_part, ('x', 'zh', 'zl', 'c'), axis=0, tiled=False)  83.9 us
    all_to_all x14, starting transfers between devices, exchange(): out = lax.all_to_all(flat, axes, split_axis=0, concat_axis=0, tiled=True)  79 us
    ppermute x7, starting transfers between devices, swap(): return lax.ppermute(block, axis, [(0, 1), (1, 0)])  50.7 us
    all_to_all x1, blocking collectives, exchange(): out = lax.all_to_all(flat, axes, split_axis=0, concat_axis=0, tiled=True)  45.9 us
    dot_general x19, matrix products, mul(): lax.dot_general(a, b, dims, precision=precision, preferred_element_type=j...  24.4 us
    ppermute x7, waiting for transfers between devices, swap(): return lax.ppermute(block, axis, [(0, 1), (1, 0)])  16.3 us
    ppermute x2, starting transfers between devices, body(): mirrored.append(lax.ppermute(piece, ALL, pairs))  15.2 us
  transfers between devices with their start and end apart: 23, of which 16 were waited for; matrix products, arithmetic and copies ran while one was open for 8% of the time, Pallas kernels for 0%

profile of v1, /device:TPU:1, one launch (start us, length us, event | category | flops | bytes accessed | tf_op | source)
XLA Modules:
  0.0 461.1 jit_solution(8045671255430228584)
XLA Ops:
  1.5 1.1 broadcast_in_dim.18
  2.7 7.6 %all-to-all-start = ((bf16[16,128,256]{2,1,0:T(8,128)(2,1)}), bf16[16,128,256]{2,1,0:T(8,128)(2,1)S(1)}, u32[]{:S(2)}, u32[]{:S(2)}) async-start(bf16[16,128,256]{2,1,0:T(8,128)(2,1)} %broadcast_in_dim.18), calls=%async_computation | async-start | bytes 2097152 | tf_op jit(solution)/shard_map/all_to_all | solution.py:32
  10.2 15.4 %collective-permute-start = (bf16[128,256]{1,0:T(8,128)(2,1)S(1)}, bf16[128,256]{1,0:T(8,128)(2,1)S(1)}, u32[]{:S(2)}, u32[]{:S(2)}) collective-permute-start(bf16[128,256]{1,0:T(8,128)(2,1)S(1)} %convert_element_type.113), channel_id=1, source_target_pairs={{0,64},{64,0},{1,65},{65,1},{2,66},{66,2},{3,67},{67,3},{4,68},{68... | collective-permute-start | bytes 196616 | tf_op jit(solution)/shard_map/ppermute | solution.py:41
  25.7 1.8 collective-permute-done
  27.5 1.1 broadcast_in_dim.19
  28.6 6.8 %all-to-all-start.1 = ((bf16[16,128,256]{2,1,0:T(8,128)(2,1)}), bf16[16,128,256]{2,1,0:T(8,128)(2,1)S(1)}, u32[]{:S(2)}, u32[]{:S(2)}) async-start(bf16[16,128,256]{2,1,0:T(8,128)(2,1)} %broadcast_in_dim.19), calls=%async_computation.1 | async-start | bytes 2097152 | tf_op jit(solution)/shard_map/all_to_all | solution.py:32
  35.4 1.6 copy.62
  39.9 7.3 %all-to-all-done.1 = bf16[16,128,256]{2,1,0:T(8,128)(2,1)S(1)} async-done(((bf16[16,128,256]{2,1,0:T(8,128)(2,1)}), bf16[16,128,256]{2,1,0:T(8,128)(2,1)S(1)}, u32[]{:S(2)}, u32[]{:S(2)}) %all-to-all-start.1) | async-done | bytes 1048608 | tf_op jit(solution)/shard_map/all_to_all | solution.py:32
  47.2 1.4 fusion.7
  49.7 12.9 %collective-permute-start.1 = (bf16[128,256]{1,0:T(8,128)(2,1)}, bf16[128,256]{1,0:T(8,128)(2,1)S(1)}, u32[]{:S(2)}, u32[]{:S(2)}) collective-permute-start(bf16[128,256]{1,0:T(8,128)(2,1)} %get-tuple-element.20), channel_id=1, source_target_pairs={{0,64},{64,0},{1,65},{65,1},{2,66},{66,2},{3,67},{67,3},{4,68},{68... | collective-permute-start | bytes 196616 | tf_op jit(solution)/shard_map/ppermute | solution.py:41
  62.6 1.6 broadcast_in_dim.20
  64.1 4.0 all-to-all-start.2
  68.2 1.4 fusion.43
  69.6 4.2 all-to-all-done.2
  74.5 4.0 all-to-all-start.3
  78.5 1.4 fusion.9
  80.0 4.2 all-to-all-done.3
  84.1 2.0 fusion.3
  86.1 15.8 %all-to-all-start.4 = ((bf16[16,8,1024]{2,1,0:T(8,128)(2,1)}), bf16[16,8,1024]{2,1,0:T(8,128)(2,1)S(1)}, u32[]{:S(2)}, u32[]{:S(2)}) async-start(bf16[16,8,1024]{2,1,0:T(8,128)(2,1)} %fusion.3), calls=%async_computation.4 | async-start | bytes 524288 | tf_op jit(solution)/shard_map/all_to_all | solution.py:32
  101.9 1.8 copy.64
  103.7 1.7 constant_dynamic-slice_fusion.3
  105.4 1.7 copy.65
  107.0 1.7 copy.66
  108.7 10.2 %all-to-all-done.4 = bf16[16,8,1024]{2,1,0:T(8,128)(2,1)S(1)} async-done(((bf16[16,8,1024]{2,1,0:T(8,128)(2,1)}), bf16[16,8,1024]{2,1,0:T(8,128)(2,1)S(1)}, u32[]{:S(2)}, u32[]{:S(2)}) %all-to-all-start.4) | async-done | bytes 262176 | tf_op jit(solution)/shard_map/all_to_all | solution.py:32
  120.4 5.3 %all-to-all-start.5 = ((bf16[16,8,1024]{2,1,0:T(8,128)(2,1)}), bf16[16,8,1024]{2,1,0:T(8,128)(2,1)S(1)}, u32[]{:S(2)}, u32[]{:S(2)}) async-start(bf16[16,8,1024]{2,1,0:T(8,128)(2,1)} %broadcast_in_dim.22), calls=%async_computation.5 | async-start | bytes 524288 | tf_op jit(solution)/shard_map/all_to_all | solution.py:32
  125.7 3.3 convolution_convert_fusion
  129.0 2.3 copy.73
  131.2 2.8 fusion.13
  134.0 8.7 %all-to-all-done.5 = bf16[16,8,1024]{2,1,0:T(8,128)(2,1)S(1)} async-done(((bf16[16,8,1024]{2,1,0:T(8,128)(2,1)}), bf16[16,8,1024]{2,1,0:T(8,128)(2,1)S(1)}, u32[]{:S(2)}, u32[]{:S(2)}) %all-to-all-start.5) | async-done | bytes 262176 | tf_op jit(solution)/shard_map/all_to_all | solution.py:32
  143.6 3.4 all-to-all-start.7
  148.0 4.6 all-to-all-done.7
  152.6 3.4 all-to-all-start.6
  156.0 1.3 convolution_convert_fusion.6
  157.3 6.5 %collective-permute-start.2 = (bf16[128,256]{1,0:T(8,128)(2,1)S(1)}, bf16[128,256]{1,0:T(8,128)(2,1)S(1)}, u32[]{:S(2)}, u32[]{:S(2)}) collective-permute-start(bf16[128,256]{1,0:T(8,128)(2,1)S(1)} %reduce_sum.125), channel_id=1, source_target_pairs={{0,64},{64,0},{1,65},{65,1},{2,66},{66,2},{3,67},{67,3},{4,68},{68... | collective-permute-start | bytes 196616 | tf_op jit(solution)/shard_map/ppermute | solution.py:41
  163.8 10.6 %collective-permute-done.2 = bf16[128,256]{1,0:T(8,128)(2,1)S(1)} collective-permute-done((bf16[128,256]{1,0:T(8,128)(2,1)S(1)}, bf16[128,256]{1,0:T(8,128)(2,1)S(1)}, u32[]{:S(2)}, u32[]{:S(2)}) %collective-permute-start.2) | collective-permute-done | bytes 65568 | tf_op jit(solution)/shard_map/ppermute | solution.py:41
  174.5 2.7 convolution_convert_fusion.1
  177.2 4.9 %all-to-all-start.9 = ((bf16[16,128,256]{2,1,0:T(8,128)(2,1)}), bf16[16,128,256]{2,1,0:T(8,128)(2,1)}, u32[]{:S(2)}, u32[]{:S(2)}) async-start(bf16[16,128,256]{2,1,0:T(8,128)(2,1)} %bitcast.131), calls=%async_computation.9 | async-start | bytes 2097152 | tf_op jit(solution)/shard_map/all_to_all | solution.py:32
  182.2 1.4 convolution_convert_fusion.2
  183.6 13.9 %all-to-all-done.9 = bf16[16,128,256]{2,1,0:T(8,128)(2,1)} async-done(((bf16[16,128,256]{2,1,0:T(8,128)(2,1)}), bf16[16,128,256]{2,1,0:T(8,128)(2,1)}, u32[]{:S(2)}, u32[]{:S(2)}) %all-to-all-start.9) | async-done | bytes 1048608 | tf_op jit(solution)/shard_map/all_to_all | solution.py:32
  197.5 4.4 all-to-all-start.8
  202.5 1.4 reduce_sum.127
  203.8 3.6 collective-permute-start.3
  207.5 9.0 %all-to-all-done.8 = bf16[16,128,256]{2,1,0:T(8,128)(2,1)S(1)} async-done(((bf16[16,128,256]{2,1,0:T(8,128)(2,1)}), bf16[16,128,256]{2,1,0:T(8,128)(2,1)S(1)}, u32[]{:S(2)}, u32[]{:S(2)}) %all-to-all-start.8) | async-done | bytes 1048608 | tf_op jit(solution)/shard_map/all_to_all | solution.py:32
  216.7 2.4 collective-permute-done.3
  219.5 4.2 collective-permute-start.4
  223.7 1.5 collective-permute-done.4
  225.2 1.3 fusion.1
  226.5 4.9 %all-to-all-start.10 = ((bf16[8,256,128]{2,1,0:T(8,128)(2,1)}), bf16[8,256,128]{2,1,0:T(8,128)(2,1)S(1)}, u32[]{:S(2)}, u32[]{:S(2)}) async-start(bf16[8,256,128]{2,1,0:T(8,128)(2,1)} %bitcast.33), calls=%async_computation.10 | async-start | bytes 1048576 | tf_op jit(solution)/shard_map/all_to_all | solution.py:32
  231.4 21.2 %all-to-all-done.10 = bf16[8,256,128]{2,1,0:T(8,128)(2,1)S(1)} async-done(((bf16[8,256,128]{2,1,0:T(8,128)(2,1)}), bf16[8,256,128]{2,1,0:T(8,128)(2,1)S(1)}, u32[]{:S(2)}, u32[]{:S(2)}) %all-to-all-start.10) | async-done | bytes 524320 | tf_op jit(solution)/shard_map/all_to_all | solution.py:32
  252.7 13.3 %collective-permute-start.5 = (f32[128,128]{1,0:T(8,128)S(1)}, f32[128,128]{1,0:T(8,128)S(1)}, u32[]{:S(2)}, u32[]{:S(2)}) collective-permute-start(f32[128,128]{1,0:T(8,128)S(1)} %get-tuple-element.18), channel_id=1, source_target_pairs={{0,0},{1,32},{2,64},{3,96},{4,128},{5,160},{6,192},{7,224},{8,256}... | collective-permute-start | bytes 196616 | tf_op jit(solution)/shard_map/ppermute | solution.py:168
  266.0 1.9 collective-permute-start.6
  268.0 4.8 %collective-permute-done.6 = f32[128,128]{1,0:T(8,128)S(1)} collective-permute-done((f32[128,128]{1,0:T(8,128)S(1)}, f32[128,128]{1,0:T(8,128)S(1)}, u32[]{:S(2)}, u32[]{:S(2)}) %collective-permute-start.6) | collective-permute-done | bytes 65568 | tf_op jit(solution)/shard_map/ppermute | solution.py:168
  273.0 45.9 %all_to_all.126 = bf16[8,128,256]{1,2,0:T(8,128)(2,1)S(1)} all-to-all(bf16[8,128,256]{1,2,0:T(8,128)(2,1)S(1)} %broadcast_in_dim.23), channel_id=1, replica_groups=mesh['x'=4,'zh'=2,'y'=4,'zl'=8,'c'=2] {'zl'}, dimensions={0} | all-to-all | bytes 1048576 | tf_op jit(solution)/shard_map/all_to_all | solution.py:32
  319.0 1.9 collective-permute-start.7
  320.9 1.8 convolution_bitcast_fusion
  322.7 4.9 %all-to-all-start.14 = ((f32[16,8,128]{2,1,0:T(8,128)}), f32[16,8,128]{2,1,0:T(8,128)S(1)}, u32[]{:S(2)}, u32[]{:S(2)}) async-start(f32[16,8,128]{2,1,0:T(8,128)} %convolution_bitcast_fusion), calls=%async_computation.14 | async-start | bytes 131072 | tf_op jit(solution)/shard_map/all_to_all | solution.py:32
  332.3 5.4 %all-to-all-done.14 = f32[16,8,128]{2,1,0:T(8,128)S(1)} async-done(((f32[16,8,128]{2,1,0:T(8,128)}), f32[16,8,128]{2,1,0:T(8,128)S(1)}, u32[]{:S(2)}, u32[]{:S(2)}) %all-to-all-start.14) | async-done | bytes 65568 | tf_op jit(solution)/shard_map/all_to_all | solution.py:32
  337.7 1.1 broadcast_in_dim.24
  338.8 3.7 all-to-all-start.12
  342.5 6.1 %collective-permute-start.8 = (bf16[144,256]{1,0:T(8,128)(2,1)S(1)}, bf16[144,256]{1,0:T(8,128)(2,1)S(1)}, u32[]{:S(2)}, u32[]{:S(2)}) collective-permute-start(bf16[144,256]{1,0:T(8,128)(2,1)S(1)} %pad_maximum_fusion.7), channel_id=1, source_target_pairs={{0,64},{64,0},{1,65},{65,1},{2,66},{66,2},{3,67},{67,3},{4,68},{68... | collective-permute-start | bytes 221192 | tf_op jit(solution)/shard_map/ppermute | solution.py:41
  348.7 83.9 %all-gather = f32[1024,128]{1,0:T(8,128)S(1)} all-gather(f32[8,128]{1,0:T(8,128)S(1)} %reduce_sum.133), channel_id=2, replica_groups=mesh['x'=4,'zh'=2,'y'=4,'zl'=8,'c'=2] {'x','zh','zl','c'}, dimensions={0}, use_global_device_ids=true | all-gather | bytes 528384 | tf_op jit(solution)/shard_map/all_gather | solution.py:141
  432.6 1.2 broadcast_in_dim.25
  434.1 5.9 %all-to-all-start.13 = ((bf16[16,144,256]{2,1,0:T(8,128)(2,1)}), bf16[16,144,256]{2,1,0:T(8,128)(2,1)S(1)}, u32[]{:S(2)}, u32[]{:S(2)}) async-start(bf16[16,144,256]{2,1,0:T(8,128)(2,1)} %broadcast_in_dim.25), calls=%async_computation.13 | async-start | bytes 2359296 | tf_op jit(solution)/shard_map/all_to_all | solution.py:32
  446.1 11.6 %all-to-all-done.13 = bf16[16,144,256]{2,1,0:T(8,128)(2,1)S(1)} async-done(((bf16[16,144,256]{2,1,0:T(8,128)(2,1)}), bf16[16,144,256]{2,1,0:T(8,128)(2,1)S(1)}, u32[]{:S(2)}, u32[]{:S(2)}) %all-to-all-start.13) | async-done | bytes 1179680 | tf_op jit(solution)/shard_map/all_to_all | solution.py:32
  (90 shorter events, 21.3 us)
Async XLA Ops:
  2.7 24.8 %all-to-all-start = ((bf16[16,128,256]{2,1,0:T(8,128)(2,1)}), bf16[16,128,256]{2,1,0:T(8,128)(2,1)S(1)}, u32[]{:S(2)}, u32[]{:S(2)}) async-start(bf16[16,128,256]{2,1,0:T(8,128)(2,1)} %broadcast_in_dim.18), calls=%async_computation | async-start | bytes 2097152 | tf_op jit(solution)/shard_map/all_to_all | solution.py:32
  10.2 17.2 %collective-permute-start = (bf16[128,256]{1,0:T(8,128)(2,1)S(1)}, bf16[128,256]{1,0:T(8,128)(2,1)S(1)}, u32[]{:S(2)}, u32[]{:S(2)}) collective-permute-start(bf16[128,256]{1,0:T(8,128)(2,1)S(1)} %convert_element_type.113), channel_id=1, source_target_pairs={{0,64},{64,0},{1,65},{65,1},{2,66},{66,2},{3,67},{67,3},{4,68},{68... | collective-permute-start | bytes 196616 | tf_op jit(solution)/shard_map/ppermute | solution.py:41
  28.6 18.6 %all-to-all-start.1 = ((bf16[16,128,256]{2,1,0:T(8,128)(2,1)}), bf16[16,128,256]{2,1,0:T(8,128)(2,1)S(1)}, u32[]{:S(2)}, u32[]{:S(2)}) async-start(bf16[16,128,256]{2,1,0:T(8,128)(2,1)} %broadcast_in_dim.19), calls=%async_computation.1 | async-start | bytes 2097152 | tf_op jit(solution)/shard_map/all_to_all | solution.py:32
  37.0 1.6 copy-start.3
  39.5 9.1 %copy-start.6 = (f32[1,128,128]{2,1,0:T(8,128)S(1)}, f32[1,128,128]{2,1,0:T(8,128)}, u32[]{:S(2)}) copy-start(f32[1,128,128]{2,1,0:T(8,128)} %param.10) | copy-start | bytes 196612
  39.5 9.1 %copy-start.14 = (f32[1,128]{1,0:T(1,128)S(1)}, f32[1,128]{1,0:T(1,128)}, u32[]{:S(2)}) copy-start(f32[1,128]{1,0:T(1,128)} %param.9) | copy-start | bytes 1540
  48.6 31.3 %copy-start.7 = (f32[128,256]{1,0:T(8,128)}, f32[128,256]{1,0:T(8,128)S(1)}, u32[]{:S(2)}) copy-start(f32[128,256]{1,0:T(8,128)S(1)} %fusion.7) | copy-start | bytes 393220
  49.7 19.9 %collective-permute-start.1 = (bf16[128,256]{1,0:T(8,128)(2,1)}, bf16[128,256]{1,0:T(8,128)(2,1)S(1)}, u32[]{:S(2)}, u32[]{:S(2)}) collective-permute-start(bf16[128,256]{1,0:T(8,128)(2,1)} %get-tuple-element.20), channel_id=1, source_target_pairs={{0,64},{64,0},{1,65},{65,1},{2,66},{66,2},{3,67},{67,3},{4,68},{68... | collective-permute-start | bytes 196616 | tf_op jit(solution)/shard_map/ppermute | solution.py:41
  64.1 9.6 %all-to-all-start.2 = ((bf16[4,128,256]{2,1,0:T(8,128)(2,1)}), bf16[4,128,256]{2,1,0:T(8,128)(2,1)}, u32[]{:S(2)}, u32[]{:S(2)}) async-start(bf16[4,128,256]{2,1,0:T(8,128)(2,1)} %broadcast_in_dim.20), calls=%async_computation.2 | async-start | bytes 524288 | tf_op jit(solution)/shard_map/all_to_all | solution.py:32
  74.5 9.6 %all-to-all-start.3 = ((bf16[4,128,256]{2,1,0:T(8,128)(2,1)}), bf16[4,128,256]{2,1,0:T(8,128)(2,1)}, u32[]{:S(2)}, u32[]{:S(2)}) async-start(bf16[4,128,256]{2,1,0:T(8,128)(2,1)} %broadcast_in_dim.21), calls=%async_computation.3 | async-start | bytes 524288 | tf_op jit(solution)/shard_map/all_to_all | solution.py:32
  86.1 32.8 %all-to-all-start.4 = ((bf16[16,8,1024]{2,1,0:T(8,128)(2,1)}), bf16[16,8,1024]{2,1,0:T(8,128)(2,1)S(1)}, u32[]{:S(2)}, u32[]{:S(2)}) async-start(bf16[16,8,1024]{2,1,0:T(8,128)(2,1)} %fusion.3), calls=%async_computation.4 | async-start | bytes 524288 | tf_op jit(solution)/shard_map/all_to_all | solution.py:32
  120.4 22.3 %all-to-all-start.5 = ((bf16[16,8,1024]{2,1,0:T(8,128)(2,1)}), bf16[16,8,1024]{2,1,0:T(8,128)(2,1)S(1)}, u32[]{:S(2)}, u32[]{:S(2)}) async-start(bf16[16,8,1024]{2,1,0:T(8,128)(2,1)} %broadcast_in_dim.22), calls=%async_computation.5 | async-start | bytes 524288 | tf_op jit(solution)/shard_map/all_to_all | solution.py:32
  134.0 40.5 %copy-start.9 = (f32[128,256]{1,0:T(8,128)S(1)}, f32[128,256]{1,0:T(8,128)}, u32[]{:S(2)}) copy-start(f32[128,256]{1,0:T(8,128)} %get-tuple-element.21) | copy-start | bytes 393220
  143.6 9.0 %all-to-all-start.7 = ((bf16[4,128,256]{2,1,0:T(8,128)(2,1)}), bf16[4,128,256]{2,1,0:T(8,128)(2,1)S(1)}, u32[]{:S(2)}, u32[]{:S(2)}) async-start(bf16[4,128,256]{2,1,0:T(8,128)(2,1)} %bitcast.27), calls=%async_computation.7 | async-start | bytes 524288 | tf_op jit(solution)/shard_map/all_to_all | solution.py:32
  152.6 11.2 %all-to-all-start.6 = ((bf16[4,128,256]{2,1,0:T(8,128)(2,1)}), bf16[4,128,256]{2,1,0:T(8,128)(2,1)S(1)}, u32[]{:S(2)}, u32[]{:S(2)}) async-start(bf16[4,128,256]{2,1,0:T(8,128)(2,1)} %bitcast.26), calls=%async_computation.6 | async-start | bytes 524288 | tf_op jit(solution)/shard_map/all_to_all | solution.py:32
  157.3 17.1 %collective-permute-start.2 = (bf16[128,256]{1,0:T(8,128)(2,1)S(1)}, bf16[128,256]{1,0:T(8,128)(2,1)S(1)}, u32[]{:S(2)}, u32[]{:S(2)}) collective-permute-start(bf16[128,256]{1,0:T(8,128)(2,1)S(1)} %reduce_sum.125), channel_id=1, source_target_pairs={{0,64},{64,0},{1,65},{65,1},{2,66},{66,2},{3,67},{67,3},{4,68},{68... | collective-permute-start | bytes 196616 | tf_op jit(solution)/shard_map/ppermute | solution.py:41
  174.4 2.8 copy-start.12
  174.5 7.7 %copy-start.2 = (bf16[256,4,1,512]{0,3,2,1:T(8,128)(2,1)S(1)}, bf16[256,4,1,512]{0,3,2,1:T(8,128)(2,1)}, u32[]{:S(2)}) copy-start(bf16[256,4,1,512]{0,3,2,1:T(8,128)(2,1)} %get-tuple-element.3) | copy-start | bytes 3145732
  177.2 20.3 %all-to-all-start.9 = ((bf16[16,128,256]{2,1,0:T(8,128)(2,1)}), bf16[16,128,256]{2,1,0:T(8,128)(2,1)}, u32[]{:S(2)}, u32[]{:S(2)}) async-start(bf16[16,128,256]{2,1,0:T(8,128)(2,1)} %bitcast.131), calls=%async_computation.9 | async-start | bytes 2097152 | tf_op jit(solution)/shard_map/all_to_all | solution.py:32
  197.5 19.0 %all-to-all-start.8 = ((bf16[16,128,256]{2,1,0:T(8,128)(2,1)}), bf16[16,128,256]{2,1,0:T(8,128)(2,1)S(1)}, u32[]{:S(2)}, u32[]{:S(2)}) async-start(bf16[16,128,256]{2,1,0:T(8,128)(2,1)} %bitcast.130), calls=%async_computation.8 | async-start | bytes 2097152 | tf_op jit(solution)/shard_map/all_to_all | solution.py:32
  203.8 15.2 %collective-permute-start.3 = (bf16[128,256]{1,0:T(8,128)(2,1)S(1)}, bf16[128,256]{1,0:T(8,128)(2,1)S(1)}, u32[]{:S(2)}, u32[]{:S(2)}) collective-permute-start(bf16[128,256]{1,0:T(8,128)(2,1)S(1)} %reduce_sum.127), channel_id=1, source_target_pairs={{0,64},{64,0},{1,65},{65,1},{2,66},{66,2},{3,67},{67,3},{4,68},{68... | collective-permute-start | bytes 196616 | tf_op jit(solution)/shard_map/ppermute | solution.py:41
  219.5 5.8 %collective-permute-start.4 = (bf16[2048,128]{1,0:T(8,128)(2,1)S(1)}, bf16[2048,128]{1,0:T(8,128)(2,1)S(1)}, u32[]{:S(2)}, u32[]{:S(2)}) collective-permute-start(bf16[2048,128]{1,0:T(8,128)(2,1)S(1)} %fusion.2), channel_id=1, source_target_pairs={{0,1},{1,0},{2,3},{3,2},{4,5},{5,4},{6,7},{7,6},{8,9},{9,8},{10,11... | collective-permute-start | bytes 1572872 | tf_op jit(solution)/shard_map/ppermute | solution.py:41
  226.5 94.4 %copy-start.8 = (f32[128,256]{1,0:T(8,128)S(1)}, f32[128,256]{1,0:T(8,128)}, u32[]{:S(2)}) copy-start(f32[128,256]{1,0:T(8,128)} %copy-done.7) | copy-start | bytes 393220
  226.5 94.4 %copy-start.13 = (bf16[128,256]{1,0:T(8,128)(2,1)S(1)}, bf16[128,256]{1,0:T(8,128)(2,1)}, u32[]{:S(2)}) copy-start(bf16[128,256]{1,0:T(8,128)(2,1)} %copy-done.12) | copy-start | bytes 196612
  226.5 26.1 %all-to-all-start.10 = ((bf16[8,256,128]{2,1,0:T(8,128)(2,1)}), bf16[8,256,128]{2,1,0:T(8,128)(2,1)S(1)}, u32[]{:S(2)}, u32[]{:S(2)}) async-start(bf16[8,256,128]{2,1,0:T(8,128)(2,1)} %bitcast.33), calls=%async_computation.10 | async-start | bytes 1048576 | tf_op jit(solution)/shard_map/all_to_all | solution.py:32
  252.7 15.3 %collective-permute-start.5 = (f32[128,128]{1,0:T(8,128)S(1)}, f32[128,128]{1,0:T(8,128)S(1)}, u32[]{:S(2)}, u32[]{:S(2)}) collective-permute-start(f32[128,128]{1,0:T(8,128)S(1)} %get-tuple-element.18), channel_id=1, source_target_pairs={{0,0},{1,32},{2,64},{3,96},{4,128},{5,160},{6,192},{7,224},{8,256}... | collective-permute-start | bytes 196616 | tf_op jit(solution)/shard_map/ppermute | solution.py:168
  266.0 6.8 %collective-permute-start.6 = (f32[128,128]{1,0:T(8,128)S(1)}, f32[128,128]{1,0:T(8,128)S(1)}, u32[]{:S(2)}, u32[]{:S(2)}) collective-permute-start(f32[128,128]{1,0:T(8,128)S(1)} %get-tuple-element.19), channel_id=1, source_target_pairs={{0,16},{1,48},{2,80},{3,112},{4,144},{5,176},{6,208},{7,240},{8,27... | collective-permute-start | bytes 196616 | tf_op jit(solution)/shard_map/ppermute | solution.py:168
  319.0 9.8 %collective-permute-start.7 = (bf16[8,128,256]{1,2,0:T(8,128)(2,1)S(1)}, bf16[8,128,256]{1,2,0:T(8,128)(2,1)S(1)}, u32[]{:S(2)}, u32[]{:S(2)}) collective-permute-start(bf16[8,128,256]{1,2,0:T(8,128)(2,1)S(1)} %all_to_all.126), channel_id=1, source_target_pairs={{0,1},{1,0},{2,3},{3,2},{4,5},{5,4},{6,7},{7,6},{8,9},{9,8},{10,11... | collective-permute-start | bytes 1572872 | tf_op jit(solution)/shard_map/ppermute | solution.py:41
  322.7 14.9 %all-to-all-start.14 = ((f32[16,8,128]{2,1,0:T(8,128)}), f32[16,8,128]{2,1,0:T(8,128)S(1)}, u32[]{:S(2)}, u32[]{:S(2)}) async-start(f32[16,8,128]{2,1,0:T(8,128)} %convolution_bitcast_fusion), calls=%async_computation.14 | async-start | bytes 131072 | tf_op jit(solution)/shard_map/all_to_all | solution.py:32
  338.8 93.8 %all-to-all-start.12 = ((bf16[16,144,256]{2,1,0:T(8,128)(2,1)}), bf16[16,144,256]{2,1,0:T(8,128)(2,1)S(1)}, u32[]{:S(2)}, u32[]{:S(2)}) async-start(bf16[16,144,256]{2,1,0:T(8,128)(2,1)} %broadcast_in_dim.24), calls=%async_computation.12 | async-start | bytes 2359296 | tf_op jit(solution)/shard_map/all_to_all | solution.py:32
  342.5 90.1 %collective-permute-start.8 = (bf16[144,256]{1,0:T(8,128)(2,1)S(1)}, bf16[144,256]{1,0:T(8,128)(2,1)S(1)}, u32[]{:S(2)}, u32[]{:S(2)}) collective-permute-start(bf16[144,256]{1,0:T(8,128)(2,1)S(1)} %pad_maximum_fusion.7), channel_id=1, source_target_pairs={{0,64},{64,0},{1,65},{65,1},{2,66},{66,2},{3,67},{67,3},{4,68},{68... | collective-permute-start | bytes 221192 | tf_op jit(solution)/shard_map/ppermute | solution.py:41
  432.6 1.4 copy-start
  434.1 23.7 %all-to-all-start.13 = ((bf16[16,144,256]{2,1,0:T(8,128)(2,1)}), bf16[16,144,256]{2,1,0:T(8,128)(2,1)S(1)}, u32[]{:S(2)}, u32[]{:S(2)}) async-start(bf16[16,144,256]{2,1,0:T(8,128)(2,1)} %broadcast_in_dim.25), calls=%async_computation.13 | async-start | bytes 2359296 | tf_op jit(solution)/shard_map/all_to_all | solution.py:32
  442.9 1.6 copy-start.1
  443.0 1.9 slice-start
  444.7 1.1 copy-start.4
  444.7 15.4 %copy-start.5 = (bf16[128,4,1,512]{0,3,2,1:T(8,128)(2,1)S(1)}, bf16[128,4,1,512]{0,3,2,1:T(8,128)(2,1)}, u32[]{:S(2)}) copy-start(bf16[128,4,1,512]{0,3,2,1:T(8,128)(2,1)} %get-tuple-element.8) | copy-start | bytes 1572868
  444.7 15.4 %copy-start.10 = (f32[128,256]{1,0:T(8,128)S(1)}, f32[128,256]{1,0:T(8,128)}, u32[]{:S(2)}) copy-start(f32[128,256]{1,0:T(8,128)} %param.11) | copy-start | bytes 393220
  444.7 15.4 %copy-start.11 = (f32[128,256]{1,0:T(8,128)S(1)}, f32[128,256]{1,0:T(8,128)}, u32[]{:S(2)}) copy-start(f32[128,256]{1,0:T(8,128)} %get-tuple-element.23) | copy-start | bytes 393220

commit v2 on v1

v2 whole, which is shorter than its diff:
```python
import math

import jax
import jax.numpy as jnp
from jax import lax
from jax.sharding import Mesh, PartitionSpec as P

D = 4096
HEAD = 128
SIZES = {"x": 4, "zh": 2, "y": 4, "zq": 4, "z1": 2, "c": 2}
ALL = tuple(SIZES)
ROWS = 128
COLS = 256
HALF = D // 2
LONG = COLS + 40
DP = ("x", "zh")
PLANE = ("x", "y")
TENSOR = ("zq", "z1", "c")

precise = lax.Precision.HIGHEST
first = (((0,), (0,)), ((), ()))
second = (((1,), (1,)), ((), ()))
plain = (((1,), (0,)), ((), ()))


def mul(a, b, dims=plain, precision=None):
    return lax.dot_general(a, b, dims, precision=precision, preferred_element_type=jnp.float32)


def count(axes):
    return math.prod(SIZES[a] for a in axes)


def exchange(blocks, axes):
    n = count(axes)
    flat = blocks.reshape((n * blocks.shape[1],) + blocks.shape[2:])
    out = lax.all_to_all(flat, axes, split_axis=0, concat_axis=0, tiled=True)
    return out.reshape(blocks.shape)


def copies(block, axes):
    return jnp.broadcast_to(block[None], (count(axes),) + block.shape)


def gather(block, axes):
    return exchange(copies(block, axes), axes)


hold = lax.optimization_barrier


def swap(block, axis, bit=1):
    n = SIZES[axis]
    return lax.ppermute(block, axis, [(i, i ^ bit) for i in range(n)])


def added(blocks):
    return jnp.sum(blocks.astype(jnp.float32), 0)


def split_at(array, axis, index):
    zero = lax.index_in_dim(array, 0, axis, keepdims=False)
    one = lax.index_in_dim(array, 1, axis, keepdims=False)
    return jnp.where(index == 0, zero, one), jnp.where(index == 0, one, zero)


def in_order(index, mine, other, axis):
    return jnp.where(
        index == 0, jnp.stack([mine, other], axis), jnp.stack([other, mine], axis)
    )


def terms_of(array, axis=-1):
    high = array.astype(jnp.bfloat16)
    rest = (array - high.astype(jnp.float32)).astype(jnp.bfloat16)
    return jnp.concatenate([high, rest], axis)


def three_terms(array):
    high = array.astype(jnp.bfloat16)
    rest = array - high.astype(jnp.float32)
    middle = rest.astype(jnp.bfloat16)
    least = (rest - middle.astype(jnp.float32)).astype(jnp.bfloat16)
    return jnp.stack([high, middle, least])


def value_of(pair):
    pair = pair.astype(jnp.float32)
    return pair[..., :HEAD] + pair[..., HEAD:]


def head_update(stored, gradient):
    root_head = math.sqrt(stored.shape[0])
    head_skew = (
        jnp.dot(gradient, stored.T, precision=precise)
        - jnp.dot(stored, gradient.T, precision=precise)
    ) / root_head
    head_step = 4.0 / jnp.sqrt(jnp.sum(head_skew * head_skew) + 1e-12)
    head_base = jnp.dot(head_skew, stored, precision=precise)
    iterate = stored - head_step * head_base
    iterate = stored - 0.5 * head_step * (
        head_base + jnp.dot(head_skew, iterate, precision=precise)
    )
    return iterate


def body(hidden, target, value_weight, quant_scale, head_rotation, rotation):
    root_width = math.sqrt(D)
    zh, core, stride = lax.axis_index("zh"), lax.axis_index("c"), lax.axis_index("z1")
    tensor = lax.axis_index(TENSOR)
    low = jnp.bfloat16
    rows = hidden[0]
    weights = value_weight[0]
    stored = head_rotation[0]
    head_matrix = stored / math.sqrt(HEAD)
    scales = quant_scale[0][:, None]

    block_low = rotation.astype(low)
    spread, block_low = hold((copies(block_low, PLANE), block_low))
    block_far = swap(block_low, "zh")
    panel_own = exchange(spread, PLANE)
    spread, panel_own = hold((copies(block_far, PLANE), panel_own))
    panel_own = panel_own.reshape(HALF, COLS)
    panel_far = exchange(spread, PLANE)

    rows_own, rows_far = split_at(rows.reshape(ROWS, 4, 2, D // 8), 2, zh)
    rows_own, rows_far = rows_own.reshape(ROWS, HALF), rows_far.reshape(ROWS, HALF)
    weights_own, weights_far = split_at(weights.reshape(4, 2, D // 8, HEAD), 1, zh)
    weights_own, weights_far = weights_own.reshape(HALF, HEAD), weights_far.reshape(HALF, HEAD)
    panel_far, rows_own, rows_far, weights_own, weights_far = hold(
        (panel_far, rows_own, rows_far, weights_own, weights_far)
    )
    panel_far = panel_far.reshape(HALF, COLS)

    unmixed = (mul(weights_own, panel_own, first) + mul(weights_far, panel_far, first)) / root_width
    tangent = jnp.tanh(mul(head_matrix, unmixed, first, precise) / scales)
    quantized = (scales * tangent).astype(low)
    spread, quantized = hold((copies(quantized, ("x",)), quantized))
    heads_own = exchange(spread, ("x",))
    spread, heads_own = hold((copies(swap(quantized, "zh"), ("x",)), heads_own))
    heads_far = exchange(spread, ("x",))
    heads = in_order(zh, heads_own, heads_far, 1).reshape(8 * HEAD, COLS)
    rotated = ((mul(rows_own, panel_own) + mul(rows_far, panel_far)) / root_width).astype(low)

    turned = (((0,), (1,)), ((), ()))
    left_own, left_far = (
        jnp.concatenate(
            [tokens, mul(head_matrix, head.astype(jnp.float32), turned, precise).astype(low)], 0
        )
        for tokens, head in ((rows_own, weights_own), (rows_far, weights_far))
    )
    target_here = lax.dynamic_slice_in_dim(target[0], tensor * 8, 8, 0)

    part = mul(rotated, heads, second).astype(low)
    part = exchange(part.reshape(16, 8, 8 * HEAD), TENSOR)
    part, left_own, left_far, target_here = hold((part, left_own, left_far, target_here))
    values = added(part)
    value_grad = (2.0 * (values - target_here.astype(jnp.float32)) / 1024).astype(low)
    value_grad = gather(value_grad, TENSOR)

    own_core, own_mate = split_at(panel_own.reshape(4, 2, COLS, COLS), 1, core)
    far_core, far_mate = split_at(panel_far.reshape(4, 2, COLS, COLS), 1, core)
    same = stride == zh
    panel_core = jnp.where(
        same, jnp.stack([own_core, far_core]), jnp.stack([far_core, own_core])
    )
    panel_mate = jnp.where(
        same, jnp.stack([own_mate, far_mate]), jnp.stack([far_mate, own_mate])
    )
    value_grad, panel_core, panel_mate = hold((value_grad, panel_core, panel_mate))
    value_grad = value_grad.reshape(ROWS, 8 * HEAD)
    tail = ((0, 0), (0, 0), (0, LONG - COLS), (0, 0))
    padded_core, padded_mate = jnp.pad(panel_core, tail), jnp.pad(panel_mate, tail)
    panel_core, panel_mate = panel_core.reshape(HALF, COLS), panel_mate.reshape(HALF, COLS)

    quant_part = mul(value_grad, rotated, first).astype(low)
    quant_grad = added(exchange(quant_part.reshape(8, HEAD, COLS), DP))
    mixed_grad = quant_grad * (1.0 - tangent * tangent)
    rotated_grad = mul(value_grad, heads).astype(low)

    head_part = terms_of(mul(unmixed, mixed_grad, second, precise))
    head_own, head_far = split_at(head_part.reshape(2, 64, COLS), 0, zh)

    right = jnp.concatenate([rotated_grad, mixed_grad.astype(low)], 0)

    def spread_out(left, heads):
        part = mul(left, right, first).astype(low).reshape(16, ROWS, COLS)
        return jnp.concatenate([part, heads.reshape(16, 4, COLS)], 1)

    far = exchange(spread_out(left_far, head_far), PLANE)
    far, own = hold((far, spread_out(left_own, head_own)))
    heads = jnp.sum(value_of(far[:, ROWS:]).reshape(4, 4, 4, HEAD), 0).reshape(16, HEAD)
    back = swap(jnp.concatenate([added(far[:, :ROWS]).astype(low), terms_of(heads)], 0), "zh")
    own = exchange(own, PLANE)
    gradient = (added(own[:, :ROWS]) + back[:ROWS].astype(jnp.float32)).astype(low)
    heads = jnp.sum(value_of(own[:, ROWS:]).reshape(4, 4, 4, HEAD), 0).reshape(16, HEAD)
    head_part = heads + value_of(back[ROWS:])

    product_mate = swap((mul(panel_mate, gradient, second) / root_width).astype(low), "c")
    product = mul(panel_core, gradient, second) / root_width + product_mate.astype(jnp.float32)
    near, next_to = product[: HALF // 2], product[HALF // 2 :]
    near = (near + swap(next_to.astype(low), "z1").astype(jnp.float32)).astype(low)
    product = added(exchange(near.reshape(4, COLS, ROWS), ("zq",)))
    odd = lax.axis_index("y") % 2
    pairs = [
        (p * 16 + k, (2 * k + p % 2) * 16 + p // 2) for p in range(32) for k in range(16)
    ]
    mirror = lax.ppermute(product, ALL, pairs)
    mine, other = split_at(mirror.reshape(2, ROWS, ROWS), 0, odd)
    other = swap(other, "y")
    mirror = in_order(odd, mine.T, other.T, 0).reshape(COLS, ROWS)
    skew = product - mirror
    square = jnp.broadcast_to(three_terms(jnp.sum(skew * skew))[:, None], (3, ROWS))

    message = jnp.concatenate(
        [skew.astype(low), terms_of(head_part, 0), jnp.pad(square, ((0, 5), (0, 0)))], 0
    )
    near = gather(message, ("zq",))
    far = swap(near, "z1")
    near_mate, far_mate = swap(near, "c"), swap(far, "c")
    base = 0.0
    for block, panel in (
        (near, padded_core[0]),
        (near_mate, padded_mate[0]),
        (far, padded_core[1]),
        (far_mate, padded_mate[1]),
    ):
        base += mul(block.reshape(4 * LONG, ROWS), panel.reshape(4 * LONG, COLS), first)
    rest = sum(added(block[:, COLS:]) for block in (near, near_mate, far, far_mate))
    head_part = rest[:16] + rest[16:32]
    square = jnp.sum(rest[32:35, 0])

    extra = jnp.pad(jnp.broadcast_to(three_terms(square)[:, None], (3, COLS)), ((0, 5), (0, 0)))
    message = jnp.concatenate([base.astype(low), terms_of(head_part), extra], 0)
    message_far = swap(message, "zh")
    all_own = gather(message, PLANE)
    all_far = gather(message_far, PLANE)

    near = in_order(core, near[:, :COLS], near_mate[:, :COLS], 1)
    far = in_order(core, far[:, :COLS], far_mate[:, :COLS], 1)
    skew_own, skew_far = jnp.where(same, near, far), jnp.where(same, far, near)
    twice = mul(
        skew_own.reshape(HALF, ROWS), all_own[:, :ROWS].reshape(HALF, COLS), first
    ) + mul(skew_far.reshape(HALF, ROWS), all_far[:, :ROWS].reshape(HALF, COLS), first)
    square_sum = jnp.sum(all_own[:, ROWS + 16 : ROWS + 19, 0].astype(jnp.float32)) + jnp.sum(
        all_far[:, ROWS + 16 : ROWS + 19, 0].astype(jnp.float32)
    )
    step_size = 16.0 / jnp.sqrt(square_sum + 1e-12)
    iterate = rotation - step_size * base + 0.5 * step_size * step_size * twice

    layer = lax.axis_index("y")
    heads_own = all_own[:, ROWS : ROWS + 16].reshape(16, 4, 4, COLS)
    heads_far = all_far[:, ROWS : ROWS + 16].reshape(16, 4, 4, COLS)
    heads_own = lax.dynamic_index_in_dim(heads_own, layer, 1, keepdims=False)
    heads_far = lax.dynamic_index_in_dim(heads_far, layer, 1, keepdims=False)
    head_grad = value_of(in_order(zh, heads_own, heads_far, 0)).reshape(HEAD, HEAD)
    return (iterate, head_update(stored, head_grad)[None])


def solution(mesh):
    split = Mesh(mesh.devices.reshape(tuple(SIZES.values())), ALL)
    in_specs = (
        P("y", DP, None),
        P("y", DP, None),
        P("y", None, DP),
        P("y", DP),
        P("y", None, None),
        P(("x", "zh", "y"), TENSOR),
    )
    out_specs = (P(("x", "zh", "y"), TENSOR), P("y", None, None))
    return jax.shard_map(body, mesh=split, in_specs=in_specs, out_specs=out_specs, check_vma=False)
```

time: 464 us -> 406 us (0.88)
  blocking collectives: 130 us -> 0 us
  waiting for transfers between devices: 121 us -> 154 us
  starting transfers between devices: 145 us -> 166 us
  other arithmetic: 10 us -> 24.8 us
    all_gather x1 -> x0, blocking collectives: 83.9 us -> none  [body(): lax.all_gather(head_part, ('x', 'zh', 'zl', 'c'), axis=0, tiled=False)]
    all_to_all x1 -> x0, blocking collectives: 45.9 us -> none  [exchange(): out = lax.all_to_all(flat, axes, split_axis=0, concat_axis=0, tiled=True)]
    all_to_all x14 -> x13, waiting for transfers between devices: 100 us -> 119 us  [exchange(): out = lax.all_to_all(flat, axes, split_axis=0, concat_axis=0, tiled=True)]
    all_to_all x14 -> x13, starting transfers between devices: 79 us -> 95.2 us  [exchange(): out = lax.all_to_all(flat, axes, split_axis=0, concat_axis=0, tiled=True)]
    ppermute x9 -> x11, waiting for transfers between devices: 21 us -> 34.7 us  [the longest x10 32.8 us: swap(): return lax.ppermute(block, axis, [(i, i ^ bit) for i in range(n)])]
    ppermute x9 -> x11, starting transfers between devices: 65.9 us -> 71.2 us  [the longest x10 63.5 us: swap(): return lax.ppermute(block, axis, [(i, i ^ bit) for i in range(n)])]
    dot_general x19 -> x21, matrix products: 24.4 us -> 21.5 us  [mul(): lax.dot_general(a, b, dims, precision=precision, preferred_element_type=j...]
  transfers between devices with their start and end apart: 23 -> 24, of which waited for: 16 -> 21; matrix products, arithmetic and copies ran while one was open for 8% -> 9% of each run, Pallas kernels for 0% -> 0%
where the time goes in v2:
time: 406 us; the launch traced here: 401 us
  starting transfers between devices  166 us (41%)
  waiting for transfers between devices  154 us (38%)
  local copies, waits for them, and re-layouts  27.4 us (7%)
  other arithmetic  24.8 us (6%)
  matrix products  22.8 us (6%)
  between operations  6.14 us (2%)
    all_to_all x13, waiting for transfers between devices, exchange(): out = lax.all_to_all(flat, axes, split_axis=0, concat_axis=0, tiled=True)  119 us
    all_to_all x13, starting transfers between devices, exchange(): out = lax.all_to_all(flat, axes, split_axis=0, concat_axis=0, tiled=True)  95.2 us
    ppermute x10, starting transfers between devices, swap(): return lax.ppermute(block, axis, [(i, i ^ bit) for i in range(n)])  63.5 us
    ppermute x10, waiting for transfers between devices, swap(): return lax.ppermute(block, axis, [(i, i ^ bit) for i in range(n)])  32.8 us
    dot_general x21, matrix products, mul(): lax.dot_general(a, b, dims, precision=precision, preferred_element_type=j...  21.5 us
    broadcast_in_dim x8, local copies, waits for them, and re-layouts, copies(): return jnp.broadcast_to(block[None], (count(axes),) + block.shape)  8.24 us
  transfers between devices with their start and end apart: 24, of which 21 were waited for; matrix products, arithmetic and copies ran while one was open for 9% of the time, Pallas kernels for 0%

profile of v2, /device:TPU:1, one launch (start us, length us, event | category | flops | bytes accessed | tf_op | source)
XLA Modules:
  0.0 401.2 jit_solution(5140029696618777008)
XLA Ops:
  2.7 7.6 %all-to-all-start = ((bf16[16,128,256]{2,1,0:T(8,128)(2,1)}), bf16[16,128,256]{2,1,0:T(8,128)(2,1)S(1)}, u32[]{:S(2)}, u32[]{:S(2)}) async-start(bf16[16,128,256]{2,1,0:T(8,128)(2,1)} %broadcast_in_dim.18), calls=%async_computation | async-start | bytes 2097152 | tf_op jit(solution)/shard_map/all_to_all | solution.py:37
  10.3 15.4 %collective-permute-start = (bf16[128,256]{1,0:T(8,128)(2,1)S(1)}, bf16[128,256]{1,0:T(8,128)(2,1)S(1)}, u32[]{:S(2)}, u32[]{:S(2)}) collective-permute-start(bf16[128,256]{1,0:T(8,128)(2,1)S(1)} %convert_element_type.185), channel_id=1, source_target_pairs={{0,64},{64,0},{1,65},{65,1},{2,66},{66,2},{3,67},{67,3},{4,68},{68... | collective-permute-start | bytes 196616 | tf_op jit(solution)/shard_map/ppermute | solution.py:54
  25.7 1.8 collective-permute-done
  28.6 6.8 %all-to-all-start.1 = ((bf16[16,128,256]{2,1,0:T(8,128)(2,1)}), bf16[16,128,256]{2,1,0:T(8,128)(2,1)S(1)}, u32[]{:S(2)}, u32[]{:S(2)}) async-start(bf16[16,128,256]{2,1,0:T(8,128)(2,1)} %broadcast_in_dim.19), calls=%async_computation.1 | async-start | bytes 2097152 | tf_op jit(solution)/shard_map/all_to_all | solution.py:37
  35.4 1.8 reshape_squeeze.18
  37.3 1.5 fusion.43
  41.2 6.0 %all-to-all-done.1 = bf16[16,128,256]{2,1,0:T(8,128)(2,1)S(1)} async-done(((bf16[16,128,256]{2,1,0:T(8,128)(2,1)}), bf16[16,128,256]{2,1,0:T(8,128)(2,1)S(1)}, u32[]{:S(2)}, u32[]{:S(2)}) %all-to-all-start.1) | async-done | bytes 1048608 | tf_op jit(solution)/shard_map/all_to_all | solution.py:37
  49.6 1.6 broadcast_in_dim.20
  51.2 12.9 %collective-permute-start.1 = (bf16[128,256]{1,0:T(8,128)(2,1)}, bf16[128,256]{1,0:T(8,128)(2,1)S(1)}, u32[]{:S(2)}, u32[]{:S(2)}) collective-permute-start(bf16[128,256]{1,0:T(8,128)(2,1)} %get-tuple-element.33), channel_id=1, source_target_pairs={{0,64},{64,0},{1,65},{65,1},{2,66},{66,2},{3,67},{67,3},{4,68},{68... | collective-permute-start | bytes 196616 | tf_op jit(solution)/shard_map/ppermute | solution.py:54
  64.1 4.0 %all-to-all-start.2 = ((bf16[4,128,256]{2,1,0:T(8,128)(2,1)}), bf16[4,128,256]{2,1,0:T(8,128)(2,1)}, u32[]{:S(2)}, u32[]{:S(2)}) async-start(bf16[4,128,256]{2,1,0:T(8,128)(2,1)} %broadcast_in_dim.20), calls=%async_computation.2 | async-start | bytes 524288 | tf_op jit(solution)/shard_map/all_to_all | solution.py:37
  68.1 2.0 fusion.46
  70.1 3.6 all-to-all-done.2
  74.4 4.0 %all-to-all-start.3 = ((bf16[4,128,256]{2,1,0:T(8,128)(2,1)}), bf16[4,128,256]{2,1,0:T(8,128)(2,1)}, u32[]{:S(2)}, u32[]{:S(2)}) async-start(bf16[4,128,256]{2,1,0:T(8,128)(2,1)} %broadcast_in_dim.21), calls=%async_computation.3 | async-start | bytes 524288 | tf_op jit(solution)/shard_map/all_to_all | solution.py:37
  78.5 1.4 fusion.7
  79.9 4.2 %all-to-all-done.3 = bf16[4,128,256]{2,1,0:T(8,128)(2,1)} async-done(((bf16[4,128,256]{2,1,0:T(8,128)(2,1)}), bf16[4,128,256]{2,1,0:T(8,128)(2,1)}, u32[]{:S(2)}, u32[]{:S(2)}) %all-to-all-start.3) | async-done | bytes 262176 | tf_op jit(solution)/shard_map/all_to_all | solution.py:37
  84.1 1.3 maximum_select_fusion.2
  87.2 15.8 %all-to-all-start.4 = ((bf16[16,8,1024]{2,1,0:T(8,128)(2,1)}), bf16[16,8,1024]{2,1,0:T(8,128)(2,1)}, u32[]{:S(2)}, u32[]{:S(2)}) async-start(bf16[16,8,1024]{2,1,0:T(8,128)(2,1)} %fusion.2), calls=%async_computation.4 | async-start | bytes 524288 | tf_op jit(solution)/shard_map/all_to_all | solution.py:37
  104.3 1.5 pad_maximum_fusion.2
  105.7 14.3 %all-to-all-done.4 = bf16[16,8,1024]{2,1,0:T(8,128)(2,1)} async-done(((bf16[16,8,1024]{2,1,0:T(8,128)(2,1)}), bf16[16,8,1024]{2,1,0:T(8,128)(2,1)}, u32[]{:S(2)}, u32[]{:S(2)}) %all-to-all-start.4) | async-done | bytes 262176 | tf_op jit(solution)/shard_map/all_to_all | solution.py:37
  121.8 5.3 %all-to-all-start.5 = ((bf16[16,8,1024]{2,1,0:T(8,128)(2,1)}), bf16[16,8,1024]{2,1,0:T(8,128)(2,1)S(1)}, u32[]{:S(2)}, u32[]{:S(2)}) async-start(bf16[16,8,1024]{2,1,0:T(8,128)(2,1)} %broadcast_in_dim.22), calls=%async_computation.5 | async-start | bytes 524288 | tf_op jit(solution)/shard_map/all_to_all | solution.py:37
  127.6 16.5 %all-to-all-done.5 = bf16[16,8,1024]{2,1,0:T(8,128)(2,1)S(1)} async-done(((bf16[16,8,1024]{2,1,0:T(8,128)(2,1)}), bf16[16,8,1024]{2,1,0:T(8,128)(2,1)S(1)}, u32[]{:S(2)}, u32[]{:S(2)}) %all-to-all-start.5) | async-done | bytes 262176 | tf_op jit(solution)/shard_map/all_to_all | solution.py:37
  145.2 6.4 %all-to-all-start.6 = ((bf16[8,128,256]{2,1,0:T(8,128)(2,1)}), bf16[8,128,256]{2,1,0:T(8,128)(2,1)}, u32[]{:S(2)}, u32[]{:S(2)}) async-start(bf16[8,128,256]{2,1,0:T(8,128)(2,1)} %bitcast.203), calls=%async_computation.6 | async-start | bytes 1048576 | tf_op jit(solution)/shard_map/all_to_all | solution.py:37
  152.5 17.6 %all-to-all-done.6 = bf16[8,128,256]{2,1,0:T(8,128)(2,1)} async-done(((bf16[8,128,256]{2,1,0:T(8,128)(2,1)}), bf16[8,128,256]{2,1,0:T(8,128)(2,1)}, u32[]{:S(2)}, u32[]{:S(2)}) %all-to-all-start.6) | async-done | bytes 524320 | tf_op jit(solution)/shard_map/all_to_all | solution.py:37
  172.2 1.3 fusion.44
  174.2 1.5 copy.53
  175.8 1.4 reshape.333
  177.2 1.3 convolution_convert_fusion.1
  179.6 13.7 %all-to-all-start.7 = ((bf16[16,132,256]{2,1,0:T(8,128)(2,1)}), bf16[16,132,256]{2,1,0:T(8,128)(2,1)S(1)}, u32[]{:S(2)}, u32[]{:S(2)}) async-start(bf16[16,132,256]{2,1,0:T(8,128)(2,1)} %pad_maximum_fusion), calls=%async_computation.7 | async-start | bytes 2228224 | tf_op jit(solution)/shard_map/all_to_all | solution.py:37
  193.3 1.5 copy.54
  194.9 1.4 reshape.335
  196.3 1.7 convolution_convert_fusion
  199.1 6.4 %all-to-all-done.7 = bf16[16,132,256]{2,1,0:T(8,128)(2,1)S(1)} async-done(((bf16[16,132,256]{2,1,0:T(8,128)(2,1)}), bf16[16,132,256]{2,1,0:T(8,128)(2,1)S(1)}, u32[]{:S(2)}, u32[]{:S(2)}) %all-to-all-start.7) | async-done | bytes 1081376 | tf_op jit(solution)/shard_map/all_to_all | solution.py:37
  206.5 3.7 all-to-all-start.8
  212.4 1.4 slice_reduce_fusion
  214.4 2.4 collective-permute-start.2
  216.9 5.3 %all-to-all-done.8 = bf16[16,132,256]{2,1,0:T(8,128)(2,1)S(1)} async-done(((bf16[16,132,256]{2,1,0:T(8,128)(2,1)}), bf16[16,132,256]{2,1,0:T(8,128)(2,1)S(1)}, u32[]{:S(2)}, u32[]{:S(2)}) %all-to-all-start.8) | async-done | bytes 1081376 | tf_op jit(solution)/shard_map/all_to_all | solution.py:37
  222.4 6.2 %collective-permute-done.2 = bf16[144,256]{1,0:T(8,128)(2,1)} collective-permute-done((bf16[144,256]{1,0:T(8,128)(2,1)}, bf16[144,256]{1,0:T(8,128)(2,1)}, u32[]{:S(2)}, u32[]{:S(2)}) %collective-permute-start.2) | collective-permute-done | bytes 73760 | tf_op jit(solution)/shard_map/ppermute | solution.py:54
  228.6 1.3 fusion.1
  229.8 1.9 collective-permute-start.3
  231.8 1.9 collective-permute-done.3
  233.6 1.3 fusion
  235.0 17.9 %collective-permute-start.4 = (bf16[1024,128]{1,0:T(8,128)(2,1)S(1)}, bf16[1024,128]{1,0:T(8,128)(2,1)S(1)}, u32[]{:S(2)}, u32[]{:S(2)}) collective-permute-start(bf16[1024,128]{1,0:T(8,128)(2,1)S(1)} %slice.331), channel_id=1, source_target_pairs={{0,2},{2,0},{1,3},{3,1},{4,6},{6,4},{5,7},{7,5},{8,10},{10,8},{9,1... | collective-permute-start | bytes 786440 | tf_op jit(solution)/shard_map/ppermute | solution.py:54
  252.8 6.4 %collective-permute-done.4 = bf16[1024,128]{1,0:T(8,128)(2,1)S(1)} collective-permute-done((bf16[1024,128]{1,0:T(8,128)(2,1)S(1)}, bf16[1024,128]{1,0:T(8,128)(2,1)S(1)}, u32[]{:S(2)}, u32[]{:S(2)}) %collective-permute-start.4) | collective-permute-done | bytes 262176 | tf_op jit(solution)/shard_map/ppermute | solution.py:54
  260.0 4.0 %all-to-all-start.9 = ((bf16[4,256,128]{2,1,0:T(8,128)(2,1)}), bf16[4,256,128]{2,1,0:T(8,128)(2,1)}, u32[]{:S(2)}, u32[]{:S(2)}) async-start(bf16[4,256,128]{2,1,0:T(8,128)(2,1)} %bitcast.210), calls=%async_computation.9 | async-start | bytes 524288 | tf_op jit(solution)/shard_map/all_to_all | solution.py:37
  265.4 14.3 %all-to-all-done.9 = bf16[4,256,128]{2,1,0:T(8,128)(2,1)} async-done(((bf16[4,256,128]{2,1,0:T(8,128)(2,1)}), bf16[4,256,128]{2,1,0:T(8,128)(2,1)}, u32[]{:S(2)}, u32[]{:S(2)}) %all-to-all-start.9) | async-done | bytes 262176 | tf_op jit(solution)/shard_map/all_to_all | solution.py:37
  280.7 7.7 %collective-permute-start.5 = (f32[256,128]{1,0:T(8,128)S(1)}, f32[256,128]{1,0:T(8,128)S(1)}, u32[]{:S(2)}, u32[]{:S(2)}) collective-permute-start(f32[256,128]{1,0:T(8,128)S(1)} %convert_reduce_fusion.2), channel_id=1, source_target_pairs={{0,0},{1,32},{2,64},{3,96},{4,128},{5,160},{6,192},{7,224},{8,256}... | collective-permute-start | bytes 393224 | tf_op jit(solution)/shard_map/ppermute | solution.py:208
  289.2 1.9 collective-permute-done.5
  291.1 2.3 collective-permute-start.6
  293.4 2.7 collective-permute-done.6
  299.2 14.1 %all-to-all-start.10 = ((bf16[4,296,128]{2,1,0:T(8,128)(2,1)}), bf16[4,296,128]{2,1,0:T(8,128)(2,1)S(1)}, u32[]{:S(2)}, u32[]{:S(2)}) async-start(bf16[4,296,128]{2,1,0:T(8,128)(2,1)} %broadcast_in_dim.23), calls=%async_computation.10 | async-start | bytes 606208 | tf_op jit(solution)/shard_map/all_to_all | solution.py:37
  315.3 15.5 %all-to-all-done.10 = bf16[4,296,128]{2,1,0:T(8,128)(2,1)S(1)} async-done(((bf16[4,296,128]{2,1,0:T(8,128)(2,1)}), bf16[4,296,128]{2,1,0:T(8,128)(2,1)S(1)}, u32[]{:S(2)}, u32[]{:S(2)}) %all-to-all-start.10) | async-done | bytes 303136 | tf_op jit(solution)/shard_map/all_to_all | solution.py:37
  330.8 1.9 collective-permute-start.8
  332.7 2.8 collective-permute-start.7
  335.5 1.4 fusion.48
  336.9 1.4 convolution_add_fusion.2
  338.3 2.2 collective-permute-done.8
  340.5 3.7 collective-permute-start.9
  349.7 4.8 %all-to-all-start.11 = ((bf16[16,152,256]{2,1,0:T(8,128)(2,1)}), bf16[16,152,256]{2,1,0:T(8,128)(2,1)S(1)}, u32[]{:S(2)}, u32[]{:S(2)}) async-start(bf16[16,152,256]{2,1,0:T(8,128)(2,1)} %broadcast_in_dim.24), calls=%async_computation.11 | async-start | bytes 2490368 | tf_op jit(solution)/shard_map/all_to_all | solution.py:37
  355.2 2.3 collective-permute-start.10
  358.2 10.9 %collective-permute-done.10 = bf16[152,256]{1,0:T(8,128)(2,1)S(1)} collective-permute-done((bf16[152,256]{1,0:T(8,128)(2,1)S(1)}, bf16[152,256]{1,0:T(8,128)(2,1)S(1)}, u32[]{:S(2)}, u32[]{:S(2)}) %collective-permute-start.10) | collective-permute-done | bytes 77856 | tf_op jit(solution)/shard_map/ppermute | solution.py:54
  369.1 3.1 all-to-all-done.11
  373.3 5.0 %all-to-all-start.12 = ((bf16[16,152,256]{2,1,0:T(8,128)(2,1)}), bf16[16,152,256]{2,1,0:T(8,128)(2,1)S(1)}, u32[]{:S(2)}, u32[]{:S(2)}) async-start(bf16[16,152,256]{2,1,0:T(8,128)(2,1)} %broadcast_in_dim.25), calls=%async_computation.12 | async-start | bytes 2490368 | tf_op jit(solution)/shard_map/all_to_all | solution.py:37
  378.3 1.1 pad_maximum_fusion.4
  382.9 12.2 %all-to-all-done.12 = bf16[16,152,256]{2,1,0:T(8,128)(2,1)S(1)} async-done(((bf16[16,152,256]{2,1,0:T(8,128)(2,1)}), bf16[16,152,256]{2,1,0:T(8,128)(2,1)S(1)}, u32[]{:S(2)}, u32[]{:S(2)}) %all-to-all-start.12) | async-done | bytes 1245216 | tf_op jit(solution)/shard_map/all_to_all | solution.py:37
  (139 shorter events, 46.9 us)
Async XLA Ops:
  0.6 102.3 %copy-start = (bf16[1,128,1024]{2,1,0:T(8,128)(2,1)S(1)}, bf16[1,128,1024]{2,1,0:T(8,128)(2,1)}, u32[]{:S(2)}) copy-start(bf16[1,128,1024]{2,1,0:T(8,128)(2,1)} %param.7) | copy-start | bytes 786436
  2.7 24.8 %all-to-all-start = ((bf16[16,128,256]{2,1,0:T(8,128)(2,1)}), bf16[16,128,256]{2,1,0:T(8,128)(2,1)S(1)}, u32[]{:S(2)}, u32[]{:S(2)}) async-start(bf16[16,128,256]{2,1,0:T(8,128)(2,1)} %broadcast_in_dim.18), calls=%async_computation | async-start | bytes 2097152 | tf_op jit(solution)/shard_map/all_to_all | solution.py:37
  10.3 17.2 %collective-permute-start = (bf16[128,256]{1,0:T(8,128)(2,1)S(1)}, bf16[128,256]{1,0:T(8,128)(2,1)S(1)}, u32[]{:S(2)}, u32[]{:S(2)}) collective-permute-start(bf16[128,256]{1,0:T(8,128)(2,1)S(1)} %convert_element_type.185), channel_id=1, source_target_pairs={{0,64},{64,0},{1,65},{65,1},{2,66},{66,2},{3,67},{67,3},{4,68},{68... | collective-permute-start | bytes 196616 | tf_op jit(solution)/shard_map/ppermute | solution.py:54
  28.6 18.6 %all-to-all-start.1 = ((bf16[16,128,256]{2,1,0:T(8,128)(2,1)}), bf16[16,128,256]{2,1,0:T(8,128)(2,1)S(1)}, u32[]{:S(2)}, u32[]{:S(2)}) async-start(bf16[16,128,256]{2,1,0:T(8,128)(2,1)} %broadcast_in_dim.19), calls=%async_computation.1 | async-start | bytes 2097152 | tf_op jit(solution)/shard_map/all_to_all | solution.py:37
  39.3 1.8 copy-start.12
  47.6 1.0 copy-start.9
  47.6 1.0 copy-start.20
  48.0 0.7 copy-start.15
  51.2 19.0 %collective-permute-start.1 = (bf16[128,256]{1,0:T(8,128)(2,1)}, bf16[128,256]{1,0:T(8,128)(2,1)S(1)}, u32[]{:S(2)}, u32[]{:S(2)}) collective-permute-start(bf16[128,256]{1,0:T(8,128)(2,1)} %get-tuple-element.33), channel_id=1, source_target_pairs={{0,64},{64,0},{1,65},{65,1},{2,66},{66,2},{3,67},{67,3},{4,68},{68... | collective-permute-start | bytes 196616 | tf_op jit(solution)/shard_map/ppermute | solution.py:54
  64.1 9.6 %all-to-all-start.2 = ((bf16[4,128,256]{2,1,0:T(8,128)(2,1)}), bf16[4,128,256]{2,1,0:T(8,128)(2,1)}, u32[]{:S(2)}, u32[]{:S(2)}) async-start(bf16[4,128,256]{2,1,0:T(8,128)(2,1)} %broadcast_in_dim.20), calls=%async_computation.2 | async-start | bytes 524288 | tf_op jit(solution)/shard_map/all_to_all | solution.py:37
  74.4 9.6 %all-to-all-start.3 = ((bf16[4,128,256]{2,1,0:T(8,128)(2,1)}), bf16[4,128,256]{2,1,0:T(8,128)(2,1)}, u32[]{:S(2)}, u32[]{:S(2)}) async-start(bf16[4,128,256]{2,1,0:T(8,128)(2,1)} %broadcast_in_dim.21), calls=%async_computation.3 | async-start | bytes 524288 | tf_op jit(solution)/shard_map/all_to_all | solution.py:37
  85.4 0.8 copy-start.1
  87.2 32.9 %all-to-all-start.4 = ((bf16[16,8,1024]{2,1,0:T(8,128)(2,1)}), bf16[16,8,1024]{2,1,0:T(8,128)(2,1)}, u32[]{:S(2)}, u32[]{:S(2)}) async-start(bf16[16,8,1024]{2,1,0:T(8,128)(2,1)} %fusion.2), calls=%async_computation.4 | async-start | bytes 524288 | tf_op jit(solution)/shard_map/all_to_all | solution.py:37
  102.9 1.3 copy-start.3
  103.0 1.3 copy-start.4
  121.8 22.3 %all-to-all-start.5 = ((bf16[16,8,1024]{2,1,0:T(8,128)(2,1)}), bf16[16,8,1024]{2,1,0:T(8,128)(2,1)S(1)}, u32[]{:S(2)}, u32[]{:S(2)}) async-start(bf16[16,8,1024]{2,1,0:T(8,128)(2,1)} %broadcast_in_dim.22), calls=%async_computation.5 | async-start | bytes 524288 | tf_op jit(solution)/shard_map/all_to_all | solution.py:37
  127.6 24.0 %copy-start.2 = (bf16[4,2,128,256]{3,2,1,0:T(8,128)(2,1)S(1)}, bf16[4,2,128,256]{3,2,1,0:T(8,128)(2,1)}, u32[]{:S(2)}) copy-start(bf16[4,2,128,256]{3,2,1,0:T(8,128)(2,1)} %copy-done.1) | copy-start | bytes 1572868
  145.2 24.9 %all-to-all-start.6 = ((bf16[8,128,256]{2,1,0:T(8,128)(2,1)}), bf16[8,128,256]{2,1,0:T(8,128)(2,1)}, u32[]{:S(2)}, u32[]{:S(2)}) async-start(bf16[8,128,256]{2,1,0:T(8,128)(2,1)} %bitcast.203), calls=%async_computation.6 | async-start | bytes 1048576 | tf_op jit(solution)/shard_map/all_to_all | solution.py:37
  152.5 24.7 %copy-start.6 = (bf16[256,2048]{1,0:T(8,128)(2,1)S(1)}, bf16[256,2048]{1,0:T(8,128)(2,1)}, u32[]{:S(2)}) copy-start(bf16[256,2048]{1,0:T(8,128)(2,1)} %get-tuple-element.40) | copy-start | bytes 3145732
  172.2 6.3 %copy-start.14 = (bf16[128,256]{1,0:T(8,128)(2,1)}, bf16[128,256]{1,0:T(8,128)(2,1)S(1)}, u32[]{:S(2)}) copy-start(bf16[128,256]{1,0:T(8,128)(2,1)S(1)} %fusion.25) | copy-start | bytes 196612
  177.2 1.4 copy-start.19
  179.6 25.9 %all-to-all-start.7 = ((bf16[16,132,256]{2,1,0:T(8,128)(2,1)}), bf16[16,132,256]{2,1,0:T(8,128)(2,1)S(1)}, u32[]{:S(2)}, u32[]{:S(2)}) async-start(bf16[16,132,256]{2,1,0:T(8,128)(2,1)} %pad_maximum_fusion), calls=%async_computation.7 | async-start | bytes 2228224 | tf_op jit(solution)/shard_map/all_to_all | solution.py:37
  196.3 1.7 copy-start.18
  205.5 1.0 copy-start.5
  206.5 15.8 %all-to-all-start.8 = ((bf16[16,132,256]{2,1,0:T(8,128)(2,1)}), bf16[16,132,256]{2,1,0:T(8,128)(2,1)S(1)}, u32[]{:S(2)}, u32[]{:S(2)}) async-start(bf16[16,132,256]{2,1,0:T(8,128)(2,1)} %pad_maximum_fusion.1), calls=%async_computation.8 | async-start | bytes 2228224 | tf_op jit(solution)/shard_map/all_to_all | solution.py:37
  214.4 14.1 %collective-permute-start.2 = (bf16[144,256]{1,0:T(8,128)(2,1)}, bf16[144,256]{1,0:T(8,128)(2,1)}, u32[]{:S(2)}, u32[]{:S(2)}) collective-permute-start(bf16[144,256]{1,0:T(8,128)(2,1)} %maximum_maximum_fusion.2), channel_id=1, source_target_pairs={{0,64},{64,0},{1,65},{65,1},{2,66},{66,2},{3,67},{67,3},{4,68},{68... | collective-permute-start | bytes 221192 | tf_op jit(solution)/shard_map/ppermute | solution.py:54
  229.8 3.8 collective-permute-start.3
  235.0 24.2 %collective-permute-start.4 = (bf16[1024,128]{1,0:T(8,128)(2,1)S(1)}, bf16[1024,128]{1,0:T(8,128)(2,1)S(1)}, u32[]{:S(2)}, u32[]{:S(2)}) collective-permute-start(bf16[1024,128]{1,0:T(8,128)(2,1)S(1)} %slice.331), channel_id=1, source_target_pairs={{0,2},{2,0},{1,3},{3,1},{4,6},{6,4},{5,7},{7,5},{8,10},{10,8},{9,1... | collective-permute-start | bytes 786440 | tf_op jit(solution)/shard_map/ppermute | solution.py:54
  260.0 19.7 %all-to-all-start.9 = ((bf16[4,256,128]{2,1,0:T(8,128)(2,1)}), bf16[4,256,128]{2,1,0:T(8,128)(2,1)}, u32[]{:S(2)}, u32[]{:S(2)}) async-start(bf16[4,256,128]{2,1,0:T(8,128)(2,1)} %bitcast.210), calls=%async_computation.9 | async-start | bytes 524288 | tf_op jit(solution)/shard_map/all_to_all | solution.py:37
  280.7 10.4 %collective-permute-start.5 = (f32[256,128]{1,0:T(8,128)S(1)}, f32[256,128]{1,0:T(8,128)S(1)}, u32[]{:S(2)}, u32[]{:S(2)}) collective-permute-start(f32[256,128]{1,0:T(8,128)S(1)} %convert_reduce_fusion.2), channel_id=1, source_target_pairs={{0,0},{1,32},{2,64},{3,96},{4,128},{5,160},{6,192},{7,224},{8,256}... | collective-permute-start | bytes 393224 | tf_op jit(solution)/shard_map/ppermute | solution.py:208
  291.1 5.0 %collective-permute-start.6 = (f32[128,128]{1,0:T(8,128)S(1)}, f32[128,128]{1,0:T(8,128)S(1)}, u32[]{:S(2)}, u32[]{:S(2)}) collective-permute-start(f32[128,128]{1,0:T(8,128)S(1)} %get-tuple-element.71), channel_id=1, source_target_pairs={{0,16},{16,0},{32,48},{48,32},{1,17},{17,1},{33,49},{49,33},{2,18}... | collective-permute-start | bytes 196616 | tf_op jit(solution)/shard_map/ppermute | solution.py:54
  299.2 31.6 %all-to-all-start.10 = ((bf16[4,296,128]{2,1,0:T(8,128)(2,1)}), bf16[4,296,128]{2,1,0:T(8,128)(2,1)S(1)}, u32[]{:S(2)}, u32[]{:S(2)}) async-start(bf16[4,296,128]{2,1,0:T(8,128)(2,1)} %broadcast_in_dim.23), calls=%async_computation.10 | async-start | bytes 606208 | tf_op jit(solution)/shard_map/all_to_all | solution.py:37
  315.3 29.0 %copy-start.7 = (bf16[1,4,296,256]{3,2,1,0:T(8,128)(2,1)S(1)}, bf16[1,4,296,256]{3,2,1,0:T(8,128)(2,1)}, u32[]{:S(2)}) copy-start(bf16[1,4,296,256]{3,2,1,0:T(8,128)(2,1)} %get-tuple-element.58) | copy-start | bytes 1818628
  330.8 9.7 %collective-permute-start.8 = (bf16[4,296,128]{2,1,0:T(8,128)(2,1)S(1)}, bf16[4,296,128]{2,1,0:T(8,128)(2,1)S(1)}, u32[]{:S(2)}, u32[]{:S(2)}) collective-permute-start(bf16[4,296,128]{2,1,0:T(8,128)(2,1)S(1)} %all-to-all-done.10), channel_id=1, source_target_pairs={{0,2},{2,0},{1,3},{3,1},{4,6},{6,4},{5,7},{7,5},{8,10},{10,8},{9,1... | collective-permute-start | bytes 909320 | tf_op jit(solution)/shard_map/ppermute | solution.py:54
  332.7 4.2 %collective-permute-start.7 = (bf16[4,296,128]{2,1,0:T(8,128)(2,1)S(1)}, bf16[4,296,128]{2,1,0:T(8,128)(2,1)S(1)}, u32[]{:S(2)}, u32[]{:S(2)}) collective-permute-start(bf16[4,296,128]{2,1,0:T(8,128)(2,1)S(1)} %all-to-all-done.10), channel_id=1, source_target_pairs={{0,1},{1,0},{2,3},{3,2},{4,5},{5,4},{6,7},{7,6},{8,9},{9,8},{10,11... | collective-permute-start | bytes 909320 | tf_op jit(solution)/shard_map/ppermute | solution.py:54
  340.5 4.9 %collective-permute-start.9 = (bf16[4,296,128]{2,1,0:T(8,128)(2,1)S(1)}, bf16[4,296,128]{2,1,0:T(8,128)(2,1)S(1)}, u32[]{:S(2)}, u32[]{:S(2)}) collective-permute-start(bf16[4,296,128]{2,1,0:T(8,128)(2,1)S(1)} %collective-permute-done.8), channel_id=1, source_target_pairs={{0,1},{1,0},{2,3},{3,2},{4,5},{5,4},{6,7},{7,6},{8,9},{9,8},{10,11... | collective-permute-start | bytes 909320 | tf_op jit(solution)/shard_map/ppermute | solution.py:54
  345.4 4.3 %copy-start.10 = (bf16[4,296,128]{2,1,0:T(8,128)(2,1)}, bf16[4,296,128]{2,1,0:T(8,128)(2,1)S(1)}, u32[]{:S(2)}) copy-start(bf16[4,296,128]{2,1,0:T(8,128)(2,1)S(1)} %collective-permute-done.9) | copy-start | bytes 909316
  349.7 22.5 %all-to-all-start.11 = ((bf16[16,152,256]{2,1,0:T(8,128)(2,1)}), bf16[16,152,256]{2,1,0:T(8,128)(2,1)S(1)}, u32[]{:S(2)}, u32[]{:S(2)}) async-start(bf16[16,152,256]{2,1,0:T(8,128)(2,1)} %broadcast_in_dim.24), calls=%async_computation.11 | async-start | bytes 2490368 | tf_op jit(solution)/shard_map/all_to_all | solution.py:37
  355.2 13.8 %collective-permute-start.10 = (bf16[152,256]{1,0:T(8,128)(2,1)S(1)}, bf16[152,256]{1,0:T(8,128)(2,1)S(1)}, u32[]{:S(2)}, u32[]{:S(2)}) collective-permute-start(bf16[152,256]{1,0:T(8,128)(2,1)S(1)} %maximum_maximum_fusion), channel_id=1, source_target_pairs={{0,64},{64,0},{1,65},{65,1},{2,66},{66,2},{3,67},{67,3},{4,68},{68... | collective-permute-start | bytes 233480 | tf_op jit(solution)/shard_map/ppermute | solution.py:54
  373.3 5.0 %copy-start.11 = (bf16[4,296,128]{2,1,0:T(8,128)(2,1)S(1)}, bf16[4,296,128]{2,1,0:T(8,128)(2,1)}, u32[]{:S(2)}) copy-start(bf16[4,296,128]{2,1,0:T(8,128)(2,1)} %copy-done.10) | copy-start | bytes 909316
  373.3 21.8 %all-to-all-start.12 = ((bf16[16,152,256]{2,1,0:T(8,128)(2,1)}), bf16[16,152,256]{2,1,0:T(8,128)(2,1)S(1)}, u32[]{:S(2)}, u32[]{:S(2)}) async-start(bf16[16,152,256]{2,1,0:T(8,128)(2,1)} %broadcast_in_dim.25), calls=%async_computation.12 | async-start | bytes 2490368 | tf_op jit(solution)/shard_map/all_to_all | solution.py:37
  378.2 1.2 copy-start.13
  396.5 3.7 copy-start.8
  396.5 3.7 copy-start.16
  396.5 3.7 copy-start.17

commit v3 on v2

--- a/solution.py
+++ b/solution.py
@@ -127,20 +127,24 @@
     rows_own, rows_far = rows_own.reshape(ROWS, HALF), rows_far.reshape(ROWS, HALF)
     weights_own, weights_far = split_at(weights.reshape(4, 2, D // 8, HEAD), 1, zh)
     weights_own, weights_far = weights_own.reshape(HALF, HEAD), weights_far.reshape(HALF, HEAD)
-    panel_far, rows_own, rows_far, weights_own, weights_far = hold(
-        (panel_far, rows_own, rows_far, weights_own, weights_far)
+    target_own, target_far = split_at(target[0].reshape(ROWS, 4, 2, HEAD), 2, zh)
+    target_own, target_far = (
+        lax.dynamic_slice_in_dim(half.reshape(ROWS, 4 * HEAD), tensor % 8 * 16, 16, 0)
+        for half in (target_own, target_far)
+    )
+    panel_far, rows_own, rows_far, weights_own, weights_far, target_far = hold(
+        (panel_far, rows_own, rows_far, weights_own, weights_far, target_far)
     )
     panel_far = panel_far.reshape(HALF, COLS)
 
+    rotated = ((mul(rows_own, panel_own) + mul(rows_far, panel_far)) / root_width).astype(low)
+    message = swap(jnp.concatenate([rotated, target_far.reshape(32, COLS)], 0), "zh")
+    tokens = jnp.concatenate([rotated, message[:ROWS]], 0)
+    target_here = jnp.where(tensor < 8, target_own, message[ROWS:].reshape(16, 4 * HEAD))
     unmixed = (mul(weights_own, panel_own, first) + mul(weights_far, panel_far, first)) / root_width
     tangent = jnp.tanh(mul(head_matrix, unmixed, first, precise) / scales)
     quantized = (scales * tangent).astype(low)
-    spread, quantized = hold((copies(quantized, ("x",)), quantized))
-    heads_own = exchange(spread, ("x",))
-    spread, heads_own = hold((copies(swap(quantized, "zh"), ("x",)), heads_own))
-    heads_far = exchange(spread, ("x",))
-    heads = in_order(zh, heads_own, heads_far, 1).reshape(8 * HEAD, COLS)
-    rotated = ((mul(rows_own, panel_own) + mul(rows_far, panel_far)) / root_width).astype(low)
+    heads = gather(quantized, ("x",)).reshape(4 * HEAD, COLS)
 
     turned = (((0,), (1,)), ((), ()))
     left_own, left_far = (
@@ -149,10 +153,8 @@
         )
         for tokens, head in ((rows_own, weights_own), (rows_far, weights_far))
     )
-    target_here = lax.dynamic_slice_in_dim(target[0], tensor * 8, 8, 0)
-
-    part = mul(rotated, heads, second).astype(low)
-    part = exchange(part.reshape(16, 8, 8 * HEAD), TENSOR)
+    part = mul(tokens, heads, second).astype(low)
+    part = exchange(part.reshape(16, 16, 4 * HEAD), TENSOR)
     part, left_own, left_far, target_here = hold((part, left_own, left_far, target_here))
     values = added(part)
     value_grad = (2.0 * (values - target_here.astype(jnp.float32)) / 1024).astype(low)
@@ -168,15 +170,17 @@
         same, jnp.stack([own_mate, far_mate]), jnp.stack([far_mate, own_mate])
     )
     value_grad, panel_core, panel_mate = hold((value_grad, panel_core, panel_mate))
-    value_grad = value_grad.reshape(ROWS, 8 * HEAD)
+    value_grad = value_grad.reshape(2 * ROWS, 4 * HEAD)
     tail = ((0, 0), (0, 0), (0, LONG - COLS), (0, 0))
     padded_core, padded_mate = jnp.pad(panel_core, tail), jnp.pad(panel_mate, tail)
     panel_core, panel_mate = panel_core.reshape(HALF, COLS), panel_mate.reshape(HALF, COLS)
 
-    quant_part = mul(value_grad, rotated, first).astype(low)
-    quant_grad = added(exchange(quant_part.reshape(8, HEAD, COLS), DP))
+    quant_grad = mul(value_grad, tokens, first).astype(low)
+    quant_grad = added(exchange(quant_grad.reshape(4, HEAD, COLS), ("x",)))
     mixed_grad = quant_grad * (1.0 - tangent * tangent)
-    rotated_grad = mul(value_grad, heads).astype(low)
+    rotated_grad = mul(value_grad, heads)
+    other = swap(rotated_grad[ROWS:].astype(low), "zh")
+    rotated_grad = (rotated_grad[:ROWS] + other.astype(jnp.float32)).astype(low)
 
     head_part = terms_of(mul(unmixed, mixed_grad, second, precise))
     head_own, head_far = split_at(head_part.reshape(2, 64, COLS), 0, zh)

time: 406 us -> 374 us (0.921)
  waiting for transfers between devices: 154 us -> 127 us
    all_to_all x13 -> x12, waiting for transfers between devices: 119 us -> 97.3 us  [exchange(): out = lax.all_to_all(flat, axes, split_axis=0, concat_axis=0, tiled=True)]
    ppermute x10 -> x11, starting transfers between devices: 63.5 us -> 74.3 us  [swap(): return lax.ppermute(block, axis, [(i, i ^ bit) for i in range(n)])]
    all_to_all x13 -> x12, starting transfers between devices: 95.2 us -> 88 us  [exchange(): out = lax.all_to_all(flat, axes, split_axis=0, concat_axis=0, tiled=True)]
    ppermute x10 -> x11, waiting for transfers between devices: 32.8 us -> 26.3 us  [swap(): return lax.ppermute(block, axis, [(i, i ^ bit) for i in range(n)])]
    broadcast_in_dim x8 -> x7, local copies, waits for them, and re-layouts: 8.24 us -> 6.71 us  [copies(): return jnp.broadcast_to(block[None], (count(axes),) + block.shape)]
  transfers between devices with their start and end apart: 24 -> 24, of which waited for: 21 -> 19; matrix products, arithmetic and copies ran while one was open for 9% -> 10% of each run, Pallas kernels for 0% -> 0%
where the time goes in v3:
time: 374 us; the launch traced here: 371 us
  starting transfers between devices  170 us (45%)
  waiting for transfers between devices  127 us (34%)
  local copies, waits for them, and re-layouts  26 us (7%)
  matrix products  21.2 us (6%)
  other arithmetic  20.9 us (6%)
  between operations  6.2 us (2%)
    all_to_all x12, waiting for transfers between devices, exchange(): out = lax.all_to_all(flat, axes, split_axis=0, concat_axis=0, tiled=True)  97.3 us
    all_to_all x12, starting transfers between devices, exchange(): out = lax.all_to_all(flat, axes, split_axis=0, concat_axis=0, tiled=True)  88 us
    ppermute x11, starting transfers between devices, swap(): return lax.ppermute(block, axis, [(i, i ^ bit) for i in range(n)])  74.3 us
    ppermute x11, waiting for transfers between devices, swap(): return lax.ppermute(block, axis, [(i, i ^ bit) for i in range(n)])  26.3 us
    dot_general x21, matrix products, mul(): lax.dot_general(a, b, dims, precision=precision, preferred_element_type=j...  19.9 us
  transfers between devices with their start and end apart: 24, of which 19 were waited for; matrix products, arithmetic and copies ran while one was open for 10% of the time, Pallas kernels for 0%

profile of v3, /device:TPU:1, one launch (start us, length us, event | category | flops | bytes accessed | tf_op | source)
XLA Modules:
  0.0 370.7 jit_solution(5080031602057751814)
XLA Ops:
  1.5 1.1 broadcast_in_dim.16
  2.7 7.7 %all-to-all-start = ((bf16[16,128,256]{2,1,0:T(8,128)(2,1)}), bf16[16,128,256]{2,1,0:T(8,128)(2,1)S(1)}, u32[]{:S(2)}, u32[]{:S(2)}) async-start(bf16[16,128,256]{2,1,0:T(8,128)(2,1)} %broadcast_in_dim.16), calls=%async_computation | async-start | bytes 2097152 | tf_op jit(solution)/shard_map/all_to_all | solution.py:37
  10.4 15.4 %collective-permute-start = (bf16[128,256]{1,0:T(8,128)(2,1)S(1)}, bf16[128,256]{1,0:T(8,128)(2,1)S(1)}, u32[]{:S(2)}, u32[]{:S(2)}) collective-permute-start(bf16[128,256]{1,0:T(8,128)(2,1)S(1)} %convert_element_type.189), channel_id=1, source_target_pairs={{0,64},{64,0},{1,65},{65,1},{2,66},{66,2},{3,67},{67,3},{4,68},{68... | collective-permute-start | bytes 196616 | tf_op jit(solution)/shard_map/ppermute | solution.py:54
  27.6 1.1 broadcast_in_dim.17
  28.7 6.8 %all-to-all-start.1 = ((bf16[16,128,256]{2,1,0:T(8,128)(2,1)}), bf16[16,128,256]{2,1,0:T(8,128)(2,1)S(1)}, u32[]{:S(2)}, u32[]{:S(2)}) async-start(bf16[16,128,256]{2,1,0:T(8,128)(2,1)} %broadcast_in_dim.17), calls=%async_computation.1 | async-start | bytes 2097152 | tf_op jit(solution)/shard_map/all_to_all | solution.py:37
  35.6 2.5 fusion.43
  38.2 2.1 broadcast_select_fusion.4
  42.9 1.3 broadcast_select_fusion.2
  44.2 3.2 all-to-all-done.1
  47.5 2.0 fusion.46
  50.7 1.0 multiply_convert_fusion
  52.4 3.7 %all-to-all-start.2 = ((bf16[4,128,256]{2,1,0:T(8,128)(2,1)}), bf16[4,128,256]{2,1,0:T(8,128)(2,1)S(1)}, u32[]{:S(2)}, u32[]{:S(2)}) async-start(bf16[4,128,256]{2,1,0:T(8,128)(2,1)} %broadcast_in_dim.18), calls=%async_computation.2 | async-start | bytes 524288 | tf_op jit(solution)/shard_map/all_to_all | solution.py:37
  56.1 1.4 fusion.6
  58.2 12.6 %collective-permute-start.1 = (bf16[160,256]{1,0:T(8,128)(2,1)}, bf16[160,256]{1,0:T(8,128)(2,1)}, u32[]{:S(2)}, u32[]{:S(2)}) collective-permute-start(bf16[160,256]{1,0:T(8,128)(2,1)} %pad_maximum_fusion.12), channel_id=1, source_target_pairs={{0,64},{64,0},{1,65},{65,1},{2,66},{66,2},{3,67},{67,3},{4,68},{68... | collective-permute-start | bytes 245768 | tf_op jit(solution)/shard_map/ppermute | solution.py:54
  72.9 1.5 slice.232
  74.4 1.8 convolution_convert_fusion.5
  76.2 18.9 %all-to-all-start.3 = ((bf16[16,16,512]{2,1,0:T(8,128)(2,1)}), bf16[16,16,512]{2,1,0:T(8,128)(2,1)}, u32[]{:S(2)}, u32[]{:S(2)}) async-start(bf16[16,16,512]{2,1,0:T(8,128)(2,1)} %bitcast.204), calls=%async_computation.3 | async-start | bytes 524288 | tf_op jit(solution)/shard_map/all_to_all | solution.py:37
  96.3 1.1 pad_maximum_fusion.2
  98.2 13.9 %all-to-all-done.3 = bf16[16,16,512]{2,1,0:T(8,128)(2,1)} async-done(((bf16[16,16,512]{2,1,0:T(8,128)(2,1)}), bf16[16,16,512]{2,1,0:T(8,128)(2,1)}, u32[]{:S(2)}, u32[]{:S(2)}) %all-to-all-start.3) | async-done | bytes 262176 | tf_op jit(solution)/shard_map/all_to_all | solution.py:37
  112.1 1.0 convert_reduce_fusion.3
  113.9 5.3 %all-to-all-start.4 = ((bf16[16,16,512]{2,1,0:T(8,128)(2,1)}), bf16[16,16,512]{2,1,0:T(8,128)(2,1)}, u32[]{:S(2)}, u32[]{:S(2)}) async-start(bf16[16,16,512]{2,1,0:T(8,128)(2,1)} %broadcast_in_dim.19), calls=%async_computation.4 | async-start | bytes 524288 | tf_op jit(solution)/shard_map/all_to_all | solution.py:37
  119.7 16.6 %all-to-all-done.4 = bf16[16,16,512]{2,1,0:T(8,128)(2,1)} async-done(((bf16[16,16,512]{2,1,0:T(8,128)(2,1)}), bf16[16,16,512]{2,1,0:T(8,128)(2,1)}, u32[]{:S(2)}, u32[]{:S(2)}) %all-to-all-start.4) | async-done | bytes 262176 | tf_op jit(solution)/shard_map/all_to_all | solution.py:37
  136.3 1.2 fusion.48
  138.8 7.5 %collective-permute-start.2 = (bf16[128,256]{1,0:T(8,128)(2,1)}, bf16[128,256]{1,0:T(8,128)(2,1)}, u32[]{:S(2)}, u32[]{:S(2)}) collective-permute-start(bf16[128,256]{1,0:T(8,128)(2,1)} %slice.371), channel_id=1, source_target_pairs={{0,64},{64,0},{1,65},{65,1},{2,66},{66,2},{3,67},{67,3},{4,68},{68... | collective-permute-start | bytes 196616 | tf_op jit(solution)/shard_map/ppermute | solution.py:54
  146.4 2.0 convolution_convert_fusion.4
  148.3 4.5 %all-to-all-start.5 = ((bf16[4,128,256]{2,1,0:T(8,128)(2,1)}), bf16[4,128,256]{2,1,0:T(8,128)(2,1)S(1)}, u32[]{:S(2)}, u32[]{:S(2)}) async-start(bf16[4,128,256]{2,1,0:T(8,128)(2,1)} %bitcast.209), calls=%async_computation.5 | async-start | bytes 524288 | tf_op jit(solution)/shard_map/all_to_all | solution.py:37
  153.9 5.1 %all-to-all-done.5 = bf16[4,128,256]{2,1,0:T(8,128)(2,1)S(1)} async-done(((bf16[4,128,256]{2,1,0:T(8,128)(2,1)}), bf16[4,128,256]{2,1,0:T(8,128)(2,1)S(1)}, u32[]{:S(2)}, u32[]{:S(2)}) %all-to-all-start.5) | async-done | bytes 262176 | tf_op jit(solution)/shard_map/all_to_all | solution.py:37
  159.0 1.2 fusion.44
  161.9 1.1 pad_maximum_fusion
  162.9 3.7 all-to-all-start.6
  166.8 1.7 convolution_convert_fusion
  168.5 1.1 pad_maximum_fusion.1
  169.6 16.1 %all-to-all-done.6 = bf16[16,132,256]{2,1,0:T(8,128)(2,1)S(1)} async-done(((bf16[16,132,256]{2,1,0:T(8,128)(2,1)}), bf16[16,132,256]{2,1,0:T(8,128)(2,1)S(1)}, u32[]{:S(2)}, u32[]{:S(2)}) %all-to-all-start.6) | async-done | bytes 1081376 | tf_op jit(solution)/shard_map/all_to_all | solution.py:37
  185.6 1.0 copy-done.2
  186.6 3.7 all-to-all-start.7
  191.2 1.4 slice_reduce_fusion
  192.6 6.4 %collective-permute-start.3 = (bf16[144,256]{1,0:T(8,128)(2,1)S(1)}, bf16[144,256]{1,0:T(8,128)(2,1)S(1)}, u32[]{:S(2)}, u32[]{:S(2)}) collective-permute-start(bf16[144,256]{1,0:T(8,128)(2,1)S(1)} %maximum_maximum_fusion.2), channel_id=1, source_target_pairs={{0,64},{64,0},{1,65},{65,1},{2,66},{66,2},{3,67},{67,3},{4,68},{68... | collective-permute-start | bytes 221192 | tf_op jit(solution)/shard_map/ppermute | solution.py:54
  199.1 7.5 %all-to-all-done.7 = bf16[16,132,256]{2,1,0:T(8,128)(2,1)S(1)} async-done(((bf16[16,132,256]{2,1,0:T(8,128)(2,1)}), bf16[16,132,256]{2,1,0:T(8,128)(2,1)S(1)}, u32[]{:S(2)}, u32[]{:S(2)}) %all-to-all-start.7) | async-done | bytes 1081376 | tf_op jit(solution)/shard_map/all_to_all | solution.py:37
  206.7 2.1 collective-permute-done.3
  209.3 2.9 collective-permute-start.4
  212.2 1.5 collective-permute-done.4
  214.2 3.0 collective-permute-start.5
  217.2 6.4 %collective-permute-done.5 = bf16[1024,128]{1,0:T(8,128)(2,1)S(1)} collective-permute-done((bf16[1024,128]{1,0:T(8,128)(2,1)S(1)}, bf16[1024,128]{1,0:T(8,128)(2,1)S(1)}, u32[]{:S(2)}, u32[]{:S(2)}) %collective-permute-start.5) | collective-permute-done | bytes 262176 | tf_op jit(solution)/shard_map/ppermute | solution.py:54
  224.4 4.0 %all-to-all-start.8 = ((bf16[4,256,128]{2,1,0:T(8,128)(2,1)}), bf16[4,256,128]{2,1,0:T(8,128)(2,1)S(1)}, u32[]{:S(2)}, u32[]{:S(2)}) async-start(bf16[4,256,128]{2,1,0:T(8,128)(2,1)} %bitcast.205), calls=%async_computation.8 | async-start | bytes 524288 | tf_op jit(solution)/shard_map/all_to_all | solution.py:37
  229.0 14.9 %all-to-all-done.8 = bf16[4,256,128]{2,1,0:T(8,128)(2,1)S(1)} async-done(((bf16[4,256,128]{2,1,0:T(8,128)(2,1)}), bf16[4,256,128]{2,1,0:T(8,128)(2,1)S(1)}, u32[]{:S(2)}, u32[]{:S(2)}) %all-to-all-start.8) | async-done | bytes 262176 | tf_op jit(solution)/shard_map/all_to_all | solution.py:37
  244.0 7.2 %collective-permute-start.6 = (f32[256,128]{1,0:T(8,128)S(1)}, f32[256,128]{1,0:T(8,128)S(1)}, u32[]{:S(2)}, u32[]{:S(2)}) collective-permute-start(f32[256,128]{1,0:T(8,128)S(1)} %convert_reduce_fusion.1), channel_id=1, source_target_pairs={{0,0},{1,32},{2,64},{3,96},{4,128},{5,160},{6,192},{7,224},{8,256}... | collective-permute-start | bytes 393224 | tf_op jit(solution)/shard_map/ppermute | solution.py:212
  251.3 3.3 collective-permute-done.6
  254.6 2.5 collective-permute-start.7
  257.8 1.8 collective-permute-done.7
  262.7 12.1 %all-to-all-start.9 = ((bf16[4,296,128]{2,1,0:T(8,128)(2,1)}), bf16[4,296,128]{2,1,0:T(8,128)(2,1)S(1)}, u32[]{:S(2)}, u32[]{:S(2)}) async-start(bf16[4,296,128]{2,1,0:T(8,128)(2,1)} %broadcast_in_dim.20), calls=%async_computation.9 | async-start | bytes 606208 | tf_op jit(solution)/shard_map/all_to_all | solution.py:37
  275.9 8.3 %all-to-all-done.9 = bf16[4,296,128]{2,1,0:T(8,128)(2,1)S(1)} async-done(((bf16[4,296,128]{2,1,0:T(8,128)(2,1)}), bf16[4,296,128]{2,1,0:T(8,128)(2,1)S(1)}, u32[]{:S(2)}, u32[]{:S(2)}) %all-to-all-start.9) | async-done | bytes 303136 | tf_op jit(solution)/shard_map/all_to_all | solution.py:37
  284.2 9.2 %collective-permute-start.9 = (bf16[4,296,128]{2,1,0:T(8,128)(2,1)S(1)}, bf16[4,296,128]{2,1,0:T(8,128)(2,1)S(1)}, u32[]{:S(2)}, u32[]{:S(2)}) collective-permute-start(bf16[4,296,128]{2,1,0:T(8,128)(2,1)S(1)} %all-to-all-done.9), channel_id=1, source_target_pairs={{0,2},{2,0},{1,3},{3,1},{4,6},{6,4},{5,7},{7,5},{8,10},{10,8},{9,1... | collective-permute-start | bytes 909320 | tf_op jit(solution)/shard_map/ppermute | solution.py:54
  293.4 5.7 %collective-permute-start.8 = (bf16[4,296,128]{2,1,0:T(8,128)(2,1)S(1)}, bf16[4,296,128]{2,1,0:T(8,128)(2,1)S(1)}, u32[]{:S(2)}, u32[]{:S(2)}) collective-permute-start(bf16[4,296,128]{2,1,0:T(8,128)(2,1)S(1)} %all-to-all-done.9), channel_id=1, source_target_pairs={{0,1},{1,0},{2,3},{3,2},{4,5},{5,4},{6,7},{7,6},{8,9},{9,8},{10,11... | collective-permute-start | bytes 909320 | tf_op jit(solution)/shard_map/ppermute | solution.py:54
  299.0 1.4 fusion.49
  300.8 3.0 collective-permute-start.10
  308.2 1.1 broadcast_in_dim.21
  309.3 10.5 %all-to-all-start.10 = ((bf16[16,152,256]{2,1,0:T(8,128)(2,1)}), bf16[16,152,256]{2,1,0:T(8,128)(2,1)S(1)}, u32[]{:S(2)}, u32[]{:S(2)}) async-start(bf16[16,152,256]{2,1,0:T(8,128)(2,1)} %broadcast_in_dim.21), calls=%async_computation.10 | async-start | bytes 2490368 | tf_op jit(solution)/shard_map/all_to_all | solution.py:37
  320.6 6.0 %collective-permute-start.11 = (bf16[152,256]{1,0:T(8,128)(2,1)S(1)}, bf16[152,256]{1,0:T(8,128)(2,1)S(1)}, u32[]{:S(2)}, u32[]{:S(2)}) collective-permute-start(bf16[152,256]{1,0:T(8,128)(2,1)S(1)} %maximum_maximum_fusion), channel_id=1, source_target_pairs={{0,64},{64,0},{1,65},{65,1},{2,66},{66,2},{3,67},{67,3},{4,68},{68... | collective-permute-start | bytes 233480 | tf_op jit(solution)/shard_map/ppermute | solution.py:54
  326.6 12.1 %collective-permute-done.11 = bf16[152,256]{1,0:T(8,128)(2,1)S(1)} collective-permute-done((bf16[152,256]{1,0:T(8,128)(2,1)S(1)}, bf16[152,256]{1,0:T(8,128)(2,1)S(1)}, u32[]{:S(2)}, u32[]{:S(2)}) %collective-permute-start.11) | collective-permute-done | bytes 77856 | tf_op jit(solution)/shard_map/ppermute | solution.py:54
  338.7 1.1 broadcast_in_dim.22
  339.8 7.1 %all-to-all-start.11 = ((bf16[16,152,256]{2,1,0:T(8,128)(2,1)}), bf16[16,152,256]{2,1,0:T(8,128)(2,1)S(1)}, u32[]{:S(2)}, u32[]{:S(2)}) async-start(bf16[16,152,256]{2,1,0:T(8,128)(2,1)} %broadcast_in_dim.22), calls=%async_computation.11 | async-start | bytes 2490368 | tf_op jit(solution)/shard_map/all_to_all | solution.py:37
  348.7 1.6 reshape.340
  352.8 11.7 %all-to-all-done.11 = bf16[16,152,256]{2,1,0:T(8,128)(2,1)S(1)} async-done(((bf16[16,152,256]{2,1,0:T(8,128)(2,1)}), bf16[16,152,256]{2,1,0:T(8,128)(2,1)S(1)}, u32[]{:S(2)}, u32[]{:S(2)}) %all-to-all-start.11) | async-done | bytes 1245216 | tf_op jit(solution)/shard_map/all_to_all | solution.py:37
  369.7 1.0 subtract_add_fusion
  (148 shorter events, 35.7 us)
Async XLA Ops:
  2.7 23.2 %copy-start.10 = (bf16[1,128,4096]{2,1,0:T(8,128)(2,1)S(1)}, bf16[1,128,4096]{2,1,0:T(8,128)(2,1)}, u32[]{:S(2)}) copy-start(bf16[1,128,4096]{2,1,0:T(8,128)(2,1)} %param.6) | copy-start | bytes 3145732
  2.7 25.0 %all-to-all-start = ((bf16[16,128,256]{2,1,0:T(8,128)(2,1)}), bf16[16,128,256]{2,1,0:T(8,128)(2,1)S(1)}, u32[]{:S(2)}, u32[]{:S(2)}) async-start(bf16[16,128,256]{2,1,0:T(8,128)(2,1)} %broadcast_in_dim.16), calls=%async_computation | async-start | bytes 2097152 | tf_op jit(solution)/shard_map/all_to_all | solution.py:37
  10.4 17.2 %collective-permute-start = (bf16[128,256]{1,0:T(8,128)(2,1)S(1)}, bf16[128,256]{1,0:T(8,128)(2,1)S(1)}, u32[]{:S(2)}, u32[]{:S(2)}) collective-permute-start(bf16[128,256]{1,0:T(8,128)(2,1)S(1)} %convert_element_type.189), channel_id=1, source_target_pairs={{0,64},{64,0},{1,65},{65,1},{2,66},{66,2},{3,67},{67,3},{4,68},{68... | collective-permute-start | bytes 196616 | tf_op jit(solution)/shard_map/ppermute | solution.py:54
  28.7 18.6 %all-to-all-start.1 = ((bf16[16,128,256]{2,1,0:T(8,128)(2,1)}), bf16[16,128,256]{2,1,0:T(8,128)(2,1)S(1)}, u32[]{:S(2)}, u32[]{:S(2)}) async-start(bf16[16,128,256]{2,1,0:T(8,128)(2,1)} %broadcast_in_dim.17), calls=%async_computation.1 | async-start | bytes 2097152 | tf_op jit(solution)/shard_map/all_to_all | solution.py:37
  35.5 2.5 copy-start.17
  49.8 0.8 copy-start.3
  49.8 0.8 copy-start.19
  50.2 2.2 copy-start.12
  52.4 22.0 %all-to-all-start.2 = ((bf16[4,128,256]{2,1,0:T(8,128)(2,1)}), bf16[4,128,256]{2,1,0:T(8,128)(2,1)S(1)}, u32[]{:S(2)}, u32[]{:S(2)}) async-start(bf16[4,128,256]{2,1,0:T(8,128)(2,1)} %broadcast_in_dim.18), calls=%async_computation.2 | async-start | bytes 524288 | tf_op jit(solution)/shard_map/all_to_all | solution.py:37
  56.1 14.6 %copy-start.13 = (bf16[128,4,1,128]{0,3,2,1:T(8,128)(2,1)S(1)}, bf16[128,4,1,128]{0,3,2,1:T(8,128)(2,1)}, u32[]{:S(2)}) copy-start(bf16[128,4,1,128]{0,3,2,1:T(8,128)(2,1)} %get-tuple-element.64) | copy-start | bytes 393220
  58.2 14.7 %collective-permute-start.1 = (bf16[160,256]{1,0:T(8,128)(2,1)}, bf16[160,256]{1,0:T(8,128)(2,1)}, u32[]{:S(2)}, u32[]{:S(2)}) collective-permute-start(bf16[160,256]{1,0:T(8,128)(2,1)} %pad_maximum_fusion.12), channel_id=1, source_target_pairs={{0,64},{64,0},{1,65},{65,1},{2,66},{66,2},{3,67},{67,3},{4,68},{68... | collective-permute-start | bytes 245768 | tf_op jit(solution)/shard_map/ppermute | solution.py:54
  76.2 36.0 %all-to-all-start.3 = ((bf16[16,16,512]{2,1,0:T(8,128)(2,1)}), bf16[16,16,512]{2,1,0:T(8,128)(2,1)}, u32[]{:S(2)}, u32[]{:S(2)}) async-start(bf16[16,16,512]{2,1,0:T(8,128)(2,1)} %bitcast.204), calls=%async_computation.3 | async-start | bytes 524288 | tf_op jit(solution)/shard_map/all_to_all | solution.py:37
  95.0 1.3 copy-start
  95.0 1.3 copy-start.1
  113.9 22.4 %all-to-all-start.4 = ((bf16[16,16,512]{2,1,0:T(8,128)(2,1)}), bf16[16,16,512]{2,1,0:T(8,128)(2,1)}, u32[]{:S(2)}, u32[]{:S(2)}) async-start(bf16[16,16,512]{2,1,0:T(8,128)(2,1)} %broadcast_in_dim.19), calls=%async_computation.4 | async-start | bytes 524288 | tf_op jit(solution)/shard_map/all_to_all | solution.py:37
  119.4 27.0 %copy-start.16 = (bf16[128,256]{1,0:T(8,128)(2,1)S(1)}, bf16[128,256]{1,0:T(8,128)(2,1)}, u32[]{:S(2)}) copy-start(bf16[128,256]{1,0:T(8,128)(2,1)} %slice.232) | copy-start | bytes 196612
  137.5 0.7 copy-start.11
  138.8 14.1 %collective-permute-start.2 = (bf16[128,256]{1,0:T(8,128)(2,1)}, bf16[128,256]{1,0:T(8,128)(2,1)}, u32[]{:S(2)}, u32[]{:S(2)}) collective-permute-start(bf16[128,256]{1,0:T(8,128)(2,1)} %slice.371), channel_id=1, source_target_pairs={{0,64},{64,0},{1,65},{65,1},{2,66},{66,2},{3,67},{67,3},{4,68},{68... | collective-permute-start | bytes 196616 | tf_op jit(solution)/shard_map/ppermute | solution.py:54
  148.3 10.6 %all-to-all-start.5 = ((bf16[4,128,256]{2,1,0:T(8,128)(2,1)}), bf16[4,128,256]{2,1,0:T(8,128)(2,1)S(1)}, u32[]{:S(2)}, u32[]{:S(2)}) async-start(bf16[4,128,256]{2,1,0:T(8,128)(2,1)} %bitcast.209), calls=%async_computation.5 | async-start | bytes 524288 | tf_op jit(solution)/shard_map/all_to_all | solution.py:37
  162.9 22.7 %all-to-all-start.6 = ((bf16[16,132,256]{2,1,0:T(8,128)(2,1)}), bf16[16,132,256]{2,1,0:T(8,128)(2,1)S(1)}, u32[]{:S(2)}, u32[]{:S(2)}) async-start(bf16[16,132,256]{2,1,0:T(8,128)(2,1)} %pad_maximum_fusion), calls=%async_computation.6 | async-start | bytes 2228224 | tf_op jit(solution)/shard_map/all_to_all | solution.py:37
  185.6 1.0 copy-start.2
  186.6 19.9 %all-to-all-start.7 = ((bf16[16,132,256]{2,1,0:T(8,128)(2,1)}), bf16[16,132,256]{2,1,0:T(8,128)(2,1)S(1)}, u32[]{:S(2)}, u32[]{:S(2)}) async-start(bf16[16,132,256]{2,1,0:T(8,128)(2,1)} %pad_maximum_fusion.1), calls=%async_computation.7 | async-start | bytes 2228224 | tf_op jit(solution)/shard_map/all_to_all | solution.py:37
  192.6 16.2 %collective-permute-start.3 = (bf16[144,256]{1,0:T(8,128)(2,1)S(1)}, bf16[144,256]{1,0:T(8,128)(2,1)S(1)}, u32[]{:S(2)}, u32[]{:S(2)}) collective-permute-start(bf16[144,256]{1,0:T(8,128)(2,1)S(1)} %maximum_maximum_fusion.2), channel_id=1, source_target_pairs={{0,64},{64,0},{1,65},{65,1},{2,66},{66,2},{3,67},{67,3},{4,68},{68... | collective-permute-start | bytes 221192 | tf_op jit(solution)/shard_map/ppermute | solution.py:54
  209.3 4.5 %collective-permute-start.4 = (bf16[2048,128]{1,0:T(8,128)(2,1)S(1)}, bf16[2048,128]{1,0:T(8,128)(2,1)S(1)}, u32[]{:S(2)}, u32[]{:S(2)}) collective-permute-start(bf16[2048,128]{1,0:T(8,128)(2,1)S(1)} %fusion.1), channel_id=1, source_target_pairs={{0,1},{1,0},{2,3},{3,2},{4,5},{5,4},{6,7},{7,6},{8,9},{9,8},{10,11... | collective-permute-start | bytes 1572872 | tf_op jit(solution)/shard_map/ppermute | solution.py:54
  214.2 9.4 %collective-permute-start.5 = (bf16[1024,128]{1,0:T(8,128)(2,1)S(1)}, bf16[1024,128]{1,0:T(8,128)(2,1)S(1)}, u32[]{:S(2)}, u32[]{:S(2)}) collective-permute-start(bf16[1024,128]{1,0:T(8,128)(2,1)S(1)} %slice.370), channel_id=1, source_target_pairs={{0,2},{2,0},{1,3},{3,1},{4,6},{6,4},{5,7},{7,5},{8,10},{10,8},{9,1... | collective-permute-start | bytes 786440 | tf_op jit(solution)/shard_map/ppermute | solution.py:54
  224.4 19.6 %all-to-all-start.8 = ((bf16[4,256,128]{2,1,0:T(8,128)(2,1)}), bf16[4,256,128]{2,1,0:T(8,128)(2,1)S(1)}, u32[]{:S(2)}, u32[]{:S(2)}) async-start(bf16[4,256,128]{2,1,0:T(8,128)(2,1)} %bitcast.205), calls=%async_computation.8 | async-start | bytes 524288 | tf_op jit(solution)/shard_map/all_to_all | solution.py:37
  244.0 10.6 %collective-permute-start.6 = (f32[256,128]{1,0:T(8,128)S(1)}, f32[256,128]{1,0:T(8,128)S(1)}, u32[]{:S(2)}, u32[]{:S(2)}) collective-permute-start(f32[256,128]{1,0:T(8,128)S(1)} %convert_reduce_fusion.1), channel_id=1, source_target_pairs={{0,0},{1,32},{2,64},{3,96},{4,128},{5,160},{6,192},{7,224},{8,256}... | collective-permute-start | bytes 393224 | tf_op jit(solution)/shard_map/ppermute | solution.py:212
  254.6 5.0 %collective-permute-start.7 = (f32[128,128]{1,0:T(8,128)S(1)}, f32[128,128]{1,0:T(8,128)S(1)}, u32[]{:S(2)}, u32[]{:S(2)}) collective-permute-start(f32[128,128]{1,0:T(8,128)S(1)} %get-tuple-element.67), channel_id=1, source_target_pairs={{0,16},{16,0},{32,48},{48,32},{1,17},{17,1},{33,49},{49,33},{2,18}... | collective-permute-start | bytes 196616 | tf_op jit(solution)/shard_map/ppermute | solution.py:54
  262.7 21.5 %all-to-all-start.9 = ((bf16[4,296,128]{2,1,0:T(8,128)(2,1)}), bf16[4,296,128]{2,1,0:T(8,128)(2,1)S(1)}, u32[]{:S(2)}, u32[]{:S(2)}) async-start(bf16[4,296,128]{2,1,0:T(8,128)(2,1)} %broadcast_in_dim.20), calls=%async_computation.9 | async-start | bytes 606208 | tf_op jit(solution)/shard_map/all_to_all | solution.py:37
  284.2 16.6 %collective-permute-start.9 = (bf16[4,296,128]{2,1,0:T(8,128)(2,1)S(1)}, bf16[4,296,128]{2,1,0:T(8,128)(2,1)S(1)}, u32[]{:S(2)}, u32[]{:S(2)}) collective-permute-start(bf16[4,296,128]{2,1,0:T(8,128)(2,1)S(1)} %all-to-all-done.9), channel_id=1, source_target_pairs={{0,2},{2,0},{1,3},{3,1},{4,6},{6,4},{5,7},{7,5},{8,10},{10,8},{9,1... | collective-permute-start | bytes 909320 | tf_op jit(solution)/shard_map/ppermute | solution.py:54
  293.4 7.1 %collective-permute-start.8 = (bf16[4,296,128]{2,1,0:T(8,128)(2,1)S(1)}, bf16[4,296,128]{2,1,0:T(8,128)(2,1)S(1)}, u32[]{:S(2)}, u32[]{:S(2)}) collective-permute-start(bf16[4,296,128]{2,1,0:T(8,128)(2,1)S(1)} %all-to-all-done.9), channel_id=1, source_target_pairs={{0,1},{1,0},{2,3},{3,2},{4,5},{5,4},{6,7},{7,6},{8,9},{9,8},{10,11... | collective-permute-start | bytes 909320 | tf_op jit(solution)/shard_map/ppermute | solution.py:54
  300.4 4.6 %copy-start.5 = (bf16[4,296,128]{2,1,0:T(8,128)(2,1)}, bf16[4,296,128]{2,1,0:T(8,128)(2,1)S(1)}, u32[]{:S(2)}) copy-start(bf16[4,296,128]{2,1,0:T(8,128)(2,1)S(1)} %collective-permute-done.8) | copy-start | bytes 909316
  300.8 4.2 %collective-permute-start.10 = (bf16[4,296,128]{2,1,0:T(8,128)(2,1)S(1)}, bf16[4,296,128]{2,1,0:T(8,128)(2,1)S(1)}, u32[]{:S(2)}, u32[]{:S(2)}) collective-permute-start(bf16[4,296,128]{2,1,0:T(8,128)(2,1)S(1)} %collective-permute-done.9), channel_id=1, source_target_pairs={{0,1},{1,0},{2,3},{3,2},{4,5},{5,4},{6,7},{7,6},{8,9},{9,8},{10,11... | collective-permute-start | bytes 909320 | tf_op jit(solution)/shard_map/ppermute | solution.py:54
  305.0 4.3 %copy-start.7 = (bf16[4,296,128]{2,1,0:T(8,128)(2,1)}, bf16[4,296,128]{2,1,0:T(8,128)(2,1)S(1)}, u32[]{:S(2)}) copy-start(bf16[4,296,128]{2,1,0:T(8,128)(2,1)S(1)} %collective-permute-done.10) | copy-start | bytes 909316
  309.3 29.4 %all-to-all-start.10 = ((bf16[16,152,256]{2,1,0:T(8,128)(2,1)}), bf16[16,152,256]{2,1,0:T(8,128)(2,1)S(1)}, u32[]{:S(2)}, u32[]{:S(2)}) async-start(bf16[16,152,256]{2,1,0:T(8,128)(2,1)} %broadcast_in_dim.21), calls=%async_computation.10 | async-start | bytes 2490368 | tf_op jit(solution)/shard_map/all_to_all | solution.py:37
  320.6 18.1 %collective-permute-start.11 = (bf16[152,256]{1,0:T(8,128)(2,1)S(1)}, bf16[152,256]{1,0:T(8,128)(2,1)S(1)}, u32[]{:S(2)}, u32[]{:S(2)}) collective-permute-start(bf16[152,256]{1,0:T(8,128)(2,1)S(1)} %maximum_maximum_fusion), channel_id=1, source_target_pairs={{0,64},{64,0},{1,65},{65,1},{2,66},{66,2},{3,67},{67,3},{4,68},{68... | collective-permute-start | bytes 233480 | tf_op jit(solution)/shard_map/ppermute | solution.py:54
  339.8 7.1 %copy-start.6 = (bf16[4,296,128]{2,1,0:T(8,128)(2,1)S(1)}, bf16[4,296,128]{2,1,0:T(8,128)(2,1)}, u32[]{:S(2)}) copy-start(bf16[4,296,128]{2,1,0:T(8,128)(2,1)} %copy-done.5) | copy-start | bytes 909316
  339.8 7.1 %copy-start.8 = (bf16[4,296,128]{2,1,0:T(8,128)(2,1)S(1)}, bf16[4,296,128]{2,1,0:T(8,128)(2,1)}, u32[]{:S(2)}) copy-start(bf16[4,296,128]{2,1,0:T(8,128)(2,1)} %copy-done.7) | copy-start | bytes 909316
  339.8 24.6 %all-to-all-start.11 = ((bf16[16,152,256]{2,1,0:T(8,128)(2,1)}), bf16[16,152,256]{2,1,0:T(8,128)(2,1)S(1)}, u32[]{:S(2)}, u32[]{:S(2)}) async-start(bf16[16,152,256]{2,1,0:T(8,128)(2,1)} %broadcast_in_dim.22), calls=%async_computation.11 | async-start | bytes 2490368 | tf_op jit(solution)/shard_map/all_to_all | solution.py:37
  346.9 1.0 copy-start.9
  352.4 12.2 %copy-start.18 = (bf16[16,1,4,256]{3,0,2,1:T(8,128)(2,1)S(1)}, bf16[16,1,4,256]{3,0,2,1:T(8,128)(2,1)}, u32[]{:S(2)}) copy-start(bf16[16,1,4,256]{3,0,2,1:T(8,128)(2,1)} %copy.116) | copy-start | bytes 98308
  352.4 12.2 %copy-start.4 = (f32[1,128,128]{2,1,0:T(8,128)S(1)}, f32[1,128,128]{2,1,0:T(8,128)}, u32[]{:S(2)}) copy-start(f32[1,128,128]{2,1,0:T(8,128)} %param.10) | copy-start | bytes 196612
  365.9 3.7 copy-start.14
  366.0 3.7 copy-start.15

commit v4 on v3

--- a/solution.py
+++ b/solution.py
@@ -108,6 +108,14 @@
     root_width = math.sqrt(D)
     zh, core, stride = lax.axis_index("zh"), lax.axis_index("c"), lax.axis_index("z1")
     tensor = lax.axis_index(TENSOR)
+    flip = lax.axis_index("y") // 2 ^ core
+
+    def flipped(blocks):
+        column = lax.axis_index("x")
+        blocks = jnp.where(column // 2 == 1, jnp.concatenate([blocks[2:], blocks[:2]], 0), blocks)
+        turned = jnp.stack([blocks[1], blocks[0], blocks[3], blocks[2]])
+        return jnp.where(column % 2 == 1, turned, blocks)
+
     low = jnp.bfloat16
     rows = hidden[0]
     weights = value_weight[0]
@@ -127,20 +135,13 @@
     rows_own, rows_far = rows_own.reshape(ROWS, HALF), rows_far.reshape(ROWS, HALF)
     weights_own, weights_far = split_at(weights.reshape(4, 2, D // 8, HEAD), 1, zh)
     weights_own, weights_far = weights_own.reshape(HALF, HEAD), weights_far.reshape(HALF, HEAD)
-    target_own, target_far = split_at(target[0].reshape(ROWS, 4, 2, HEAD), 2, zh)
-    target_own, target_far = (
-        lax.dynamic_slice_in_dim(half.reshape(ROWS, 4 * HEAD), tensor % 8 * 16, 16, 0)
-        for half in (target_own, target_far)
-    )
-    panel_far, rows_own, rows_far, weights_own, weights_far, target_far = hold(
-        (panel_far, rows_own, rows_far, weights_own, weights_far, target_far)
+    panel_far, rows_own, rows_far, weights_own, weights_far = hold(
+        (panel_far, rows_own, rows_far, weights_own, weights_far)
     )
     panel_far = panel_far.reshape(HALF, COLS)
 
     rotated = ((mul(rows_own, panel_own) + mul(rows_far, panel_far)) / root_width).astype(low)
-    message = swap(jnp.concatenate([rotated, target_far.reshape(32, COLS)], 0), "zh")
-    tokens = jnp.concatenate([rotated, message[:ROWS]], 0)
-    target_here = jnp.where(tensor < 8, target_own, message[ROWS:].reshape(16, 4 * HEAD))
+    tokens = jnp.concatenate([rotated, swap(rotated, "zh")], 0)
     unmixed = (mul(weights_own, panel_own, first) + mul(weights_far, panel_far, first)) / root_width
     tangent = jnp.tanh(mul(head_matrix, unmixed, first, precise) / scales)
     quantized = (scales * tangent).astype(low)
@@ -153,6 +154,13 @@
         )
         for tokens, head in ((rows_own, weights_own), (rows_far, weights_far))
     )
+    target_own, target_far = split_at(target[0].reshape(ROWS, 4, 2, HEAD), 2, zh)
+    target_own, target_far = (
+        lax.dynamic_slice_in_dim(half.reshape(ROWS, 4 * HEAD), tensor % 8 * 16, 16, 0)
+        for half in (target_own, target_far)
+    )
+    target_here = jnp.where(tensor < 8, target_own, swap(target_far, "zh"))
+
     part = mul(tokens, heads, second).astype(low)
     part = exchange(part.reshape(16, 16, 4 * HEAD), TENSOR)
     part, left_own, left_far, target_here = hold((part, left_own, left_far, target_here))
@@ -160,9 +168,9 @@
     value_grad = (2.0 * (values - target_here.astype(jnp.float32)) / 1024).astype(low)
     value_grad = gather(value_grad, TENSOR)
 
-    own_core, own_mate = split_at(panel_own.reshape(4, 2, COLS, COLS), 1, core)
-    far_core, far_mate = split_at(panel_far.reshape(4, 2, COLS, COLS), 1, core)
-    same = stride == zh
+    own_core, own_mate = split_at(flipped(panel_own.reshape(4, 2, COLS, COLS)), 1, flip)
+    far_core, far_mate = split_at(flipped(panel_far.reshape(4, 2, COLS, COLS)), 1, flip)
+    same = stride == 0
     panel_core = jnp.where(
         same, jnp.stack([own_core, far_core]), jnp.stack([far_core, own_core])
     )
@@ -206,14 +214,15 @@
     near = (near + swap(next_to.astype(low), "z1").astype(jnp.float32)).astype(low)
     product = added(exchange(near.reshape(4, COLS, ROWS), ("zq",)))
     odd = lax.axis_index("y") % 2
-    pairs = [
-        (p * 16 + k, (2 * k + p % 2) * 16 + p // 2) for p in range(32) for k in range(16)
-    ]
-    mirror = lax.ppermute(product, ALL, pairs)
+    pairs = []
+    for here in range(512):
+        i, h, j, q, o, e = here >> 7, here >> 6 & 1, here >> 4 & 3, here >> 2 & 3, here >> 1 & 1, here & 1
+        pairs.append((here, (i ^ q) << 7 | (h ^ o) << 6 | (j ^ 2 * e) << 4 | (here & 15)))
+    mirror = lax.ppermute(product.astype(low), ALL, pairs)
     mine, other = split_at(mirror.reshape(2, ROWS, ROWS), 0, odd)
     other = swap(other, "y")
     mirror = in_order(odd, mine.T, other.T, 0).reshape(COLS, ROWS)
-    skew = product - mirror
+    skew = product - mirror.astype(jnp.float32)
     square = jnp.broadcast_to(three_terms(jnp.sum(skew * skew))[:, None], (3, ROWS))
 
     message = jnp.concatenate(
@@ -240,8 +249,8 @@
     all_own = gather(message, PLANE)
     all_far = gather(message_far, PLANE)
 
-    near = in_order(core, near[:, :COLS], near_mate[:, :COLS], 1)
-    far = in_order(core, far[:, :COLS], far_mate[:, :COLS], 1)
+    near = flipped(in_order(flip, near[:, :COLS], near_mate[:, :COLS], 1))
+    far = flipped(in_order(flip, far[:, :COLS], far_mate[:, :COLS], 1))
     skew_own, skew_far = jnp.where(same, near, far), jnp.where(same, far, near)
     twice = mul(
         skew_own.reshape(HALF, ROWS), all_own[:, :ROWS].reshape(HALF, COLS), first

time: 374 us -> 376 us (level)
  waiting for transfers between devices: 127 us -> 139 us
  starting transfers between devices: 170 us -> 160 us
    all_to_all x12, starting transfers between devices: 88 us -> 66.7 us  [exchange(): out = lax.all_to_all(flat, axes, split_axis=0, concat_axis=0, tiled=True)]
    ppermute x11 -> x12, starting transfers between devices: 74.3 us -> 86.1 us  [swap(): return lax.ppermute(block, axis, [(i, i ^ bit) for i in range(n)])]
    ppermute x11 -> x12, waiting for transfers between devices: 26.3 us -> 35.8 us  [swap(): return lax.ppermute(block, axis, [(i, i ^ bit) for i in range(n)])]
    all_to_all x12, waiting for transfers between devices: 97.3 us -> 102 us  [exchange(): out = lax.all_to_all(flat, axes, split_axis=0, concat_axis=0, tiled=True)]
    unnamed x44 -> x59, local copies, waits for them, and re-layouts: 5.92 us -> 9 us
  transfers between devices with their start and end apart: 24 -> 25, of which waited for: 19 -> 20; matrix products, arithmetic and copies ran while one was open for 10% -> 9% of each run, Pallas kernels for 0% -> 0%
where the time goes in v4:
time: 376 us; the launch traced here: 371 us
  starting transfers between devices  160 us (43%)
  waiting for transfers between devices  139 us (37%)
  local copies, waits for them, and re-layouts  23.7 us (6%)
  other arithmetic  22.3 us (6%)
  matrix products  19.3 us (5%)
  between operations  6.39 us (2%)
    all_to_all x12, waiting for transfers between devices, exchange(): out = lax.all_to_all(flat, axes, split_axis=0, concat_axis=0, tiled=True)  102 us
    ppermute x12, starting transfers between devices, swap(): return lax.ppermute(block, axis, [(i, i ^ bit) for i in range(n)])  86.1 us
    all_to_all x12, starting transfers between devices, exchange(): out = lax.all_to_all(flat, axes, split_axis=0, concat_axis=0, tiled=True)  66.7 us
    ppermute x12, waiting for transfers between devices, swap(): return lax.ppermute(block, axis, [(i, i ^ bit) for i in range(n)])  35.8 us
    dot_general x21, matrix products, mul(): lax.dot_general(a, b, dims, precision=precision, preferred_element_type=j...  18 us
    unnamed x59, local copies, waits for them, and re-layouts  9 us
  transfers between devices with their start and end apart: 25, of which 20 were waited for; matrix products, arithmetic and copies ran while one was open for 9% of the time, Pallas kernels for 0%

profile of v4, /device:TPU:1, one launch (start us, length us, event | category | flops | bytes accessed | tf_op | source)
XLA Modules:
  0.0 370.6 jit_solution(11309981267258415804)
XLA Ops:
  0.7 1.1 copy.85
  2.0 16.3 %collective-permute-start.2 = (bf16[16,512]{1,0:T(8,128)(2,1)S(1)}, bf16[16,512]{1,0:T(8,128)(2,1)}, u32[]{:S(2)}, u32[]{:S(2)}) collective-permute-start(bf16[16,512]{1,0:T(8,128)(2,1)S(1)} %copy.112), channel_id=1, source_target_pairs={{0,64},{64,0},{1,65},{65,1},{2,66},{66,2},{3,67},{67,3},{4,68},{68... | collective-permute-start | bytes 49160 | tf_op jit(solution)/shard_map/ppermute | solution.py:54
  18.4 1.1 broadcast_in_dim.16
  19.5 6.9 %all-to-all-start = ((bf16[16,128,256]{2,1,0:T(8,128)(2,1)}), bf16[16,128,256]{2,1,0:T(8,128)(2,1)S(1)}, u32[]{:S(2)}, u32[]{:S(2)}) async-start(bf16[16,128,256]{2,1,0:T(8,128)(2,1)} %broadcast_in_dim.16), calls=%async_computation | async-start | bytes 2097152 | tf_op jit(solution)/shard_map/all_to_all | solution.py:37
  26.3 1.9 collective-permute-start
  29.1 1.3 broadcast_select_fusion.2
  30.4 1.5 fusion.48
  34.5 6.4 %collective-permute-done = bf16[128,256]{1,0:T(8,128)(2,1)S(1)} collective-permute-done((bf16[128,256]{1,0:T(8,128)(2,1)S(1)}, bf16[128,256]{1,0:T(8,128)(2,1)S(1)}, u32[]{:S(2)}, u32[]{:S(2)}) %collective-permute-start) | collective-permute-done | bytes 65568 | tf_op jit(solution)/shard_map/ppermute | solution.py:54
  41.6 1.1 broadcast_in_dim.17
  42.7 6.2 %all-to-all-start.1 = ((bf16[16,128,256]{2,1,0:T(8,128)(2,1)}), bf16[16,128,256]{2,1,0:T(8,128)(2,1)S(1)}, u32[]{:S(2)}, u32[]{:S(2)}) async-start(bf16[16,128,256]{2,1,0:T(8,128)(2,1)} %broadcast_in_dim.17), calls=%async_computation.1 | async-start | bytes 2097152 | tf_op jit(solution)/shard_map/all_to_all | solution.py:37
  51.1 9.5 %all-to-all-done.1 = bf16[16,128,256]{2,1,0:T(8,128)(2,1)S(1)} async-done(((bf16[16,128,256]{2,1,0:T(8,128)(2,1)}), bf16[16,128,256]{2,1,0:T(8,128)(2,1)S(1)}, u32[]{:S(2)}, u32[]{:S(2)}) %all-to-all-start.1) | async-done | bytes 1048608 | tf_op jit(solution)/shard_map/all_to_all | solution.py:37
  60.7 1.3 fusion.55
  63.4 8.7 %collective-permute-start.1 = (bf16[128,256]{1,0:T(8,128)(2,1)S(1)}, bf16[128,256]{1,0:T(8,128)(2,1)S(1)}, u32[]{:S(2)}, u32[]{:S(2)}) collective-permute-start(bf16[128,256]{1,0:T(8,128)(2,1)S(1)} %fusion.6), channel_id=1, source_target_pairs={{0,64},{64,0},{1,65},{65,1},{2,66},{66,2},{3,67},{67,3},{4,68},{68... | collective-permute-start | bytes 196616 | tf_op jit(solution)/shard_map/ppermute | solution.py:54
  74.2 3.4 all-to-all-start.2
  77.6 1.4 convolution_convert_fusion.2
  79.0 4.4 %all-to-all-done.2 = bf16[4,128,256]{2,1,0:T(8,128)(2,1)S(1)} async-done(((bf16[4,128,256]{2,1,0:T(8,128)(2,1)}), bf16[4,128,256]{2,1,0:T(8,128)(2,1)S(1)}, u32[]{:S(2)}, u32[]{:S(2)}) %all-to-all-start.2) | async-done | bytes 262176 | tf_op jit(solution)/shard_map/all_to_all | solution.py:37
  84.3 12.3 %all-to-all-start.3 = ((bf16[16,16,512]{2,1,0:T(8,128)(2,1)}), bf16[16,16,512]{2,1,0:T(8,128)(2,1)}, u32[]{:S(2)}, u32[]{:S(2)}) async-start(bf16[16,16,512]{2,1,0:T(8,128)(2,1)} %bitcast.8), calls=%async_computation.3 | async-start | bytes 524288 | tf_op jit(solution)/shard_map/all_to_all | solution.py:37
  98.6 1.5 pad_maximum_fusion.2
  100.4 13.4 %all-to-all-done.3 = bf16[16,16,512]{2,1,0:T(8,128)(2,1)} async-done(((bf16[16,16,512]{2,1,0:T(8,128)(2,1)}), bf16[16,16,512]{2,1,0:T(8,128)(2,1)}, u32[]{:S(2)}, u32[]{:S(2)}) %all-to-all-start.3) | async-done | bytes 262176 | tf_op jit(solution)/shard_map/all_to_all | solution.py:37
  113.8 1.0 convert_reduce_fusion.3
  115.5 5.3 %all-to-all-start.4 = ((bf16[16,16,512]{2,1,0:T(8,128)(2,1)}), bf16[16,16,512]{2,1,0:T(8,128)(2,1)}, u32[]{:S(2)}, u32[]{:S(2)}) async-start(bf16[16,16,512]{2,1,0:T(8,128)(2,1)} %broadcast_in_dim.19), calls=%async_computation.4 | async-start | bytes 524288 | tf_op jit(solution)/shard_map/all_to_all | solution.py:37
  122.6 15.3 %all-to-all-done.4 = bf16[16,16,512]{2,1,0:T(8,128)(2,1)} async-done(((bf16[16,16,512]{2,1,0:T(8,128)(2,1)}), bf16[16,16,512]{2,1,0:T(8,128)(2,1)}, u32[]{:S(2)}, u32[]{:S(2)}) %all-to-all-start.4) | async-done | bytes 262176 | tf_op jit(solution)/shard_map/all_to_all | solution.py:37
  137.9 1.2 fusion.57
  139.8 6.3 %collective-permute-start.3 = (bf16[128,256]{1,0:T(8,128)(2,1)}, bf16[128,256]{1,0:T(8,128)(2,1)}, u32[]{:S(2)}, u32[]{:S(2)}) collective-permute-start(bf16[128,256]{1,0:T(8,128)(2,1)} %slice.487), channel_id=1, source_target_pairs={{0,64},{64,0},{1,65},{65,1},{2,66},{66,2},{3,67},{67,3},{4,68},{68... | collective-permute-start | bytes 196616 | tf_op jit(solution)/shard_map/ppermute | solution.py:54
  146.1 1.9 convolution_convert_fusion.4
  148.0 3.5 all-to-all-start.5
  151.5 4.6 %collective-permute-done.3 = bf16[128,256]{1,0:T(8,128)(2,1)} collective-permute-done((bf16[128,256]{1,0:T(8,128)(2,1)}, bf16[128,256]{1,0:T(8,128)(2,1)}, u32[]{:S(2)}, u32[]{:S(2)}) %collective-permute-start.3) | collective-permute-done | bytes 65568 | tf_op jit(solution)/shard_map/ppermute | solution.py:54
  157.4 1.2 fusion.53
  160.3 1.1 pad_maximum_fusion
  161.4 3.7 all-to-all-start.6
  165.2 1.7 convolution_convert_fusion
  166.9 1.1 pad_maximum_fusion.1
  168.0 16.0 %all-to-all-done.6 = bf16[16,132,256]{2,1,0:T(8,128)(2,1)S(1)} async-done(((bf16[16,132,256]{2,1,0:T(8,128)(2,1)}), bf16[16,132,256]{2,1,0:T(8,128)(2,1)S(1)}, u32[]{:S(2)}, u32[]{:S(2)}) %all-to-all-start.6) | async-done | bytes 1081376 | tf_op jit(solution)/shard_map/all_to_all | solution.py:37
  184.1 1.0 copy-done.3
  185.1 3.8 %all-to-all-start.7 = ((bf16[16,132,256]{2,1,0:T(8,128)(2,1)}), bf16[16,132,256]{2,1,0:T(8,128)(2,1)S(1)}, u32[]{:S(2)}, u32[]{:S(2)}) async-start(bf16[16,132,256]{2,1,0:T(8,128)(2,1)} %pad_maximum_fusion.1), calls=%async_computation.7 | async-start | bytes 2228224 | tf_op jit(solution)/shard_map/all_to_all | solution.py:37
  189.7 1.4 slice_reduce_fusion
  191.1 7.9 %collective-permute-start.4 = (bf16[144,256]{1,0:T(8,128)(2,1)S(1)}, bf16[144,256]{1,0:T(8,128)(2,1)S(1)}, u32[]{:S(2)}, u32[]{:S(2)}) collective-permute-start(bf16[144,256]{1,0:T(8,128)(2,1)S(1)} %maximum_maximum_fusion.2), channel_id=1, source_target_pairs={{0,64},{64,0},{1,65},{65,1},{2,66},{66,2},{3,67},{67,3},{4,68},{68... | collective-permute-start | bytes 221192 | tf_op jit(solution)/shard_map/ppermute | solution.py:54
  199.1 6.1 %all-to-all-done.7 = bf16[16,132,256]{2,1,0:T(8,128)(2,1)S(1)} async-done(((bf16[16,132,256]{2,1,0:T(8,128)(2,1)}), bf16[16,132,256]{2,1,0:T(8,128)(2,1)S(1)}, u32[]{:S(2)}, u32[]{:S(2)}) %all-to-all-start.7) | async-done | bytes 1081376 | tf_op jit(solution)/shard_map/all_to_all | solution.py:37
  205.7 5.2 %collective-permute-start.5 = (bf16[2048,128]{1,0:T(8,128)(2,1)S(1)}, bf16[2048,128]{1,0:T(8,128)(2,1)S(1)}, u32[]{:S(2)}, u32[]{:S(2)}) collective-permute-start(bf16[2048,128]{1,0:T(8,128)(2,1)S(1)} %fusion.1), channel_id=1, source_target_pairs={{0,1},{1,0},{2,3},{3,2},{4,5},{5,4},{6,7},{7,6},{8,9},{9,8},{10,11... | collective-permute-start | bytes 1572872 | tf_op jit(solution)/shard_map/ppermute | solution.py:54
  210.9 1.5 collective-permute-done.5
  212.9 4.1 %collective-permute-start.6 = (bf16[1024,128]{1,0:T(8,128)(2,1)S(1)}, bf16[1024,128]{1,0:T(8,128)(2,1)S(1)}, u32[]{:S(2)}, u32[]{:S(2)}) collective-permute-start(bf16[1024,128]{1,0:T(8,128)(2,1)S(1)} %slice.486), channel_id=1, source_target_pairs={{0,2},{2,0},{1,3},{3,1},{4,6},{6,4},{5,7},{7,5},{8,10},{10,8},{9,1... | collective-permute-start | bytes 786440 | tf_op jit(solution)/shard_map/ppermute | solution.py:54
  216.9 6.4 %collective-permute-done.6 = bf16[1024,128]{1,0:T(8,128)(2,1)S(1)} collective-permute-done((bf16[1024,128]{1,0:T(8,128)(2,1)S(1)}, bf16[1024,128]{1,0:T(8,128)(2,1)S(1)}, u32[]{:S(2)}, u32[]{:S(2)}) %collective-permute-start.6) | collective-permute-done | bytes 262176 | tf_op jit(solution)/shard_map/ppermute | solution.py:54
  224.1 3.5 all-to-all-start.8
  228.1 15.2 %all-to-all-done.8 = bf16[4,256,128]{2,1,0:T(8,128)(2,1)S(1)} async-done(((bf16[4,256,128]{2,1,0:T(8,128)(2,1)}), bf16[4,256,128]{2,1,0:T(8,128)(2,1)S(1)}, u32[]{:S(2)}, u32[]{:S(2)}) %all-to-all-start.8) | async-done | bytes 262176 | tf_op jit(solution)/shard_map/all_to_all | solution.py:37
  243.4 6.8 %collective-permute-start.7 = (bf16[256,128]{1,0:T(8,128)(2,1)S(1)}, bf16[256,128]{1,0:T(8,128)(2,1)S(1)}, u32[]{:S(2)}, u32[]{:S(2)}) collective-permute-start(bf16[256,128]{1,0:T(8,128)(2,1)S(1)} %convert_element_type.233), channel_id=1, source_target_pairs={{0,0},{1,33},{2,66},{3,99},{4,132},{5,165},{6,198},{7,231},{8,264}... | collective-permute-start | bytes 196616 | tf_op jit(solution)/shard_map/ppermute | solution.py:221
  250.2 1.6 collective-permute-done.7
  251.8 3.3 collective-permute-start.8
  259.6 6.3 %all-to-all-start.9 = ((bf16[4,296,128]{2,1,0:T(8,128)(2,1)}), bf16[4,296,128]{2,1,0:T(8,128)(2,1)S(1)}, u32[]{:S(2)}, u32[]{:S(2)}) async-start(bf16[4,296,128]{2,1,0:T(8,128)(2,1)} %broadcast_in_dim.20), calls=%async_computation.9 | async-start | bytes 606208 | tf_op jit(solution)/shard_map/all_to_all | solution.py:37
  267.7 7.4 %all-to-all-done.9 = bf16[4,296,128]{2,1,0:T(8,128)(2,1)S(1)} async-done(((bf16[4,296,128]{2,1,0:T(8,128)(2,1)}), bf16[4,296,128]{2,1,0:T(8,128)(2,1)S(1)}, u32[]{:S(2)}, u32[]{:S(2)}) %all-to-all-start.9) | async-done | bytes 303136 | tf_op jit(solution)/shard_map/all_to_all | solution.py:37
  275.1 5.8 %collective-permute-start.9 = (bf16[4,296,128]{2,1,0:T(8,128)(2,1)S(1)}, bf16[4,296,128]{2,1,0:T(8,128)(2,1)S(1)}, u32[]{:S(2)}, u32[]{:S(2)}) collective-permute-start(bf16[4,296,128]{2,1,0:T(8,128)(2,1)S(1)} %all-to-all-done.9), channel_id=1, source_target_pairs={{0,1},{1,0},{2,3},{3,2},{4,5},{5,4},{6,7},{7,6},{8,9},{9,8},{10,11... | collective-permute-start | bytes 909320 | tf_op jit(solution)/shard_map/ppermute | solution.py:54
  280.9 17.8 %collective-permute-start.10 = (bf16[4,296,128]{2,1,0:T(8,128)(2,1)S(1)}, bf16[4,296,128]{2,1,0:T(8,128)(2,1)S(1)}, u32[]{:S(2)}, u32[]{:S(2)}) collective-permute-start(bf16[4,296,128]{2,1,0:T(8,128)(2,1)S(1)} %all-to-all-done.9), channel_id=1, source_target_pairs={{0,2},{2,0},{1,3},{3,1},{4,6},{6,4},{5,7},{7,5},{8,10},{10,8},{9,1... | collective-permute-start | bytes 909320 | tf_op jit(solution)/shard_map/ppermute | solution.py:54
  298.7 1.4 fusion.58
  301.4 4.8 %collective-permute-done.10 = bf16[4,296,128]{2,1,0:T(8,128)(2,1)S(1)} collective-permute-done((bf16[4,296,128]{2,1,0:T(8,128)(2,1)S(1)}, bf16[4,296,128]{2,1,0:T(8,128)(2,1)S(1)}, u32[]{:S(2)}, u32[]{:S(2)}) %collective-permute-start.10) | collective-permute-done | bytes 303136 | tf_op jit(solution)/shard_map/ppermute | solution.py:54
  306.2 2.5 collective-permute-start.11
  313.1 1.1 broadcast_in_dim.21
  314.3 5.2 %all-to-all-start.10 = ((bf16[16,152,256]{2,1,0:T(8,128)(2,1)}), bf16[16,152,256]{2,1,0:T(8,128)(2,1)S(1)}, u32[]{:S(2)}, u32[]{:S(2)}) async-start(bf16[16,152,256]{2,1,0:T(8,128)(2,1)} %broadcast_in_dim.21), calls=%async_computation.10 | async-start | bytes 2490368 | tf_op jit(solution)/shard_map/all_to_all | solution.py:37
  321.3 6.5 %collective-permute-start.12 = (bf16[152,256]{1,0:T(8,128)(2,1)S(1)}, bf16[152,256]{1,0:T(8,128)(2,1)S(1)}, u32[]{:S(2)}, u32[]{:S(2)}) collective-permute-start(bf16[152,256]{1,0:T(8,128)(2,1)S(1)} %maximum_maximum_fusion), channel_id=1, source_target_pairs={{0,64},{64,0},{1,65},{65,1},{2,66},{66,2},{3,67},{67,3},{4,68},{68... | collective-permute-start | bytes 233480 | tf_op jit(solution)/shard_map/ppermute | solution.py:54
  328.7 10.6 %collective-permute-done.12 = bf16[152,256]{1,0:T(8,128)(2,1)S(1)} collective-permute-done((bf16[152,256]{1,0:T(8,128)(2,1)S(1)}, bf16[152,256]{1,0:T(8,128)(2,1)S(1)}, u32[]{:S(2)}, u32[]{:S(2)}) %collective-permute-start.12) | collective-permute-done | bytes 77856 | tf_op jit(solution)/shard_map/ppermute | solution.py:54
  339.3 1.1 broadcast_in_dim.22
  340.5 6.6 %all-to-all-start.11 = ((bf16[16,152,256]{2,1,0:T(8,128)(2,1)}), bf16[16,152,256]{2,1,0:T(8,128)(2,1)S(1)}, u32[]{:S(2)}, u32[]{:S(2)}) async-start(bf16[16,152,256]{2,1,0:T(8,128)(2,1)} %broadcast_in_dim.22), calls=%async_computation.11 | async-start | bytes 2490368 | tf_op jit(solution)/shard_map/all_to_all | solution.py:37
  347.2 1.2 maximum_select_fusion.9
  348.5 1.2 broadcast_select_fusion
  350.9 13.7 %all-to-all-done.11 = bf16[16,152,256]{2,1,0:T(8,128)(2,1)S(1)} async-done(((bf16[16,152,256]{2,1,0:T(8,128)(2,1)}), bf16[16,152,256]{2,1,0:T(8,128)(2,1)S(1)}, u32[]{:S(2)}, u32[]{:S(2)}) %all-to-all-start.11) | async-done | bytes 1245216 | tf_op jit(solution)/shard_map/all_to_all | solution.py:37
  369.6 1.0 subtract_add_fusion
  (175 shorter events, 38.7 us)
Async XLA Ops:
  0.6 17.7 %copy-start.24 = (f32[128,256]{1,0:T(8,128)S(1)}, f32[128,256]{1,0:T(8,128)}, u32[]{:S(2)}) copy-start(f32[128,256]{1,0:T(8,128)} %param.11) | copy-start | bytes 393220
  2.0 32.4 %collective-permute-start.2 = (bf16[16,512]{1,0:T(8,128)(2,1)S(1)}, bf16[16,512]{1,0:T(8,128)(2,1)}, u32[]{:S(2)}, u32[]{:S(2)}) collective-permute-start(bf16[16,512]{1,0:T(8,128)(2,1)S(1)} %copy.112), channel_id=1, source_target_pairs={{0,64},{64,0},{1,65},{65,1},{2,66},{66,2},{3,67},{67,3},{4,68},{68... | collective-permute-start | bytes 49160 | tf_op jit(solution)/shard_map/ppermute | solution.py:54
  19.5 8.8 %copy-start.16 = (bf16[1,128,4096]{2,1,0:T(8,128)(2,1)S(1)}, bf16[1,128,4096]{2,1,0:T(8,128)(2,1)}, u32[]{:S(2)}) copy-start(bf16[1,128,4096]{2,1,0:T(8,128)(2,1)} %param.6) | copy-start | bytes 3145732
  19.5 22.2 %all-to-all-start = ((bf16[16,128,256]{2,1,0:T(8,128)(2,1)}), bf16[16,128,256]{2,1,0:T(8,128)(2,1)S(1)}, u32[]{:S(2)}, u32[]{:S(2)}) async-start(bf16[16,128,256]{2,1,0:T(8,128)(2,1)} %broadcast_in_dim.16), calls=%async_computation | async-start | bytes 2097152 | tf_op jit(solution)/shard_map/all_to_all | solution.py:37
  26.3 14.6 %collective-permute-start = (bf16[128,256]{1,0:T(8,128)(2,1)S(1)}, bf16[128,256]{1,0:T(8,128)(2,1)S(1)}, u32[]{:S(2)}, u32[]{:S(2)}) collective-permute-start(bf16[128,256]{1,0:T(8,128)(2,1)S(1)} %convert_element_type.202), channel_id=1, source_target_pairs={{0,64},{64,0},{1,65},{65,1},{2,66},{66,2},{3,67},{67,3},{4,68},{68... | collective-permute-start | bytes 196616 | tf_op jit(solution)/shard_map/ppermute | solution.py:54
  42.7 18.0 %all-to-all-start.1 = ((bf16[16,128,256]{2,1,0:T(8,128)(2,1)}), bf16[16,128,256]{2,1,0:T(8,128)(2,1)S(1)}, u32[]{:S(2)}, u32[]{:S(2)}) async-start(bf16[16,128,256]{2,1,0:T(8,128)(2,1)} %broadcast_in_dim.17), calls=%async_computation.1 | async-start | bytes 2097152 | tf_op jit(solution)/shard_map/all_to_all | solution.py:37
  62.0 1.0 copy-start
  63.4 9.1 %copy-start.10 = (f32[1,128,128]{2,1,0:T(8,128)S(1)}, f32[1,128,128]{2,1,0:T(8,128)}, u32[]{:S(2)}) copy-start(f32[1,128,128]{2,1,0:T(8,128)} %param.10) | copy-start | bytes 196612
  63.4 9.1 %copy-start.26 = (f32[1,128]{1,0:T(1,128)S(1)}, f32[1,128]{1,0:T(1,128)}, u32[]{:S(2)}) copy-start(f32[1,128]{1,0:T(1,128)} %param.9) | copy-start | bytes 1540
  63.4 15.6 %collective-permute-start.1 = (bf16[128,256]{1,0:T(8,128)(2,1)S(1)}, bf16[128,256]{1,0:T(8,128)(2,1)S(1)}, u32[]{:S(2)}, u32[]{:S(2)}) collective-permute-start(bf16[128,256]{1,0:T(8,128)(2,1)S(1)} %fusion.6), channel_id=1, source_target_pairs={{0,64},{64,0},{1,65},{65,1},{2,66},{66,2},{3,67},{67,3},{4,68},{68... | collective-permute-start | bytes 196616 | tf_op jit(solution)/shard_map/ppermute | solution.py:54
  72.4 6.5 %copy-start.18 = (f32[128,256]{1,0:T(8,128)}, f32[128,256]{1,0:T(8,128)S(1)}, u32[]{:S(2)}) copy-start(f32[128,256]{1,0:T(8,128)S(1)} %fusion.4) | copy-start | bytes 393220
  74.2 9.2 %all-to-all-start.2 = ((bf16[4,128,256]{2,1,0:T(8,128)(2,1)}), bf16[4,128,256]{2,1,0:T(8,128)(2,1)S(1)}, u32[]{:S(2)}, u32[]{:S(2)}) async-start(bf16[4,128,256]{2,1,0:T(8,128)(2,1)} %broadcast_in_dim.18), calls=%async_computation.2 | async-start | bytes 524288 | tf_op jit(solution)/shard_map/all_to_all | solution.py:37
  84.3 29.4 %all-to-all-start.3 = ((bf16[16,16,512]{2,1,0:T(8,128)(2,1)}), bf16[16,16,512]{2,1,0:T(8,128)(2,1)}, u32[]{:S(2)}, u32[]{:S(2)}) async-start(bf16[16,16,512]{2,1,0:T(8,128)(2,1)} %bitcast.8), calls=%async_computation.3 | async-start | bytes 524288 | tf_op jit(solution)/shard_map/all_to_all | solution.py:37
  97.3 1.0 copy-start.1
  97.3 1.2 copy-start.2
  97.3 1.3 copy-start.9
  115.5 22.4 %all-to-all-start.4 = ((bf16[16,16,512]{2,1,0:T(8,128)(2,1)}), bf16[16,16,512]{2,1,0:T(8,128)(2,1)}, u32[]{:S(2)}, u32[]{:S(2)}) async-start(bf16[16,16,512]{2,1,0:T(8,128)(2,1)} %broadcast_in_dim.19), calls=%async_computation.4 | async-start | bytes 524288 | tf_op jit(solution)/shard_map/all_to_all | solution.py:37
  121.0 1.0 copy-start.6
  121.0 1.2 copy-start.7
  139.1 7.0 %copy-start.17 = (f32[256,256]{1,0:T(8,128)}, f32[256,256]{1,0:T(8,128)S(1)}, u32[]{:S(2)}) copy-start(f32[256,256]{1,0:T(8,128)S(1)} %fusion.57) | copy-start | bytes 786436
  139.8 16.4 %collective-permute-start.3 = (bf16[128,256]{1,0:T(8,128)(2,1)}, bf16[128,256]{1,0:T(8,128)(2,1)}, u32[]{:S(2)}, u32[]{:S(2)}) collective-permute-start(bf16[128,256]{1,0:T(8,128)(2,1)} %slice.487), channel_id=1, source_target_pairs={{0,64},{64,0},{1,65},{65,1},{2,66},{66,2},{3,67},{67,3},{4,68},{68... | collective-permute-start | bytes 196616 | tf_op jit(solution)/shard_map/ppermute | solution.py:54
  148.0 11.8 %copy-start.4 = (bf16[256,2048]{1,0:T(8,128)(2,1)S(1)}, bf16[256,2048]{1,0:T(8,128)(2,1)}, u32[]{:S(2)}) copy-start(bf16[256,2048]{1,0:T(8,128)(2,1)} %get-tuple-element.32) | copy-start | bytes 3145732
  148.0 9.4 %all-to-all-start.5 = ((bf16[4,128,256]{2,1,0:T(8,128)(2,1)}), bf16[4,128,256]{2,1,0:T(8,128)(2,1)S(1)}, u32[]{:S(2)}, u32[]{:S(2)}) async-start(bf16[4,128,256]{2,1,0:T(8,128)(2,1)} %bitcast.203), calls=%async_computation.5 | async-start | bytes 524288 | tf_op jit(solution)/shard_map/all_to_all | solution.py:37
  161.4 22.7 %all-to-all-start.6 = ((bf16[16,132,256]{2,1,0:T(8,128)(2,1)}), bf16[16,132,256]{2,1,0:T(8,128)(2,1)S(1)}, u32[]{:S(2)}, u32[]{:S(2)}) async-start(bf16[16,132,256]{2,1,0:T(8,128)(2,1)} %pad_maximum_fusion), calls=%async_computation.6 | async-start | bytes 2228224 | tf_op jit(solution)/shard_map/all_to_all | solution.py:37
  184.0 1.0 copy-start.3
  185.1 20.0 %all-to-all-start.7 = ((bf16[16,132,256]{2,1,0:T(8,128)(2,1)}), bf16[16,132,256]{2,1,0:T(8,128)(2,1)S(1)}, u32[]{:S(2)}, u32[]{:S(2)}) async-start(bf16[16,132,256]{2,1,0:T(8,128)(2,1)} %pad_maximum_fusion.1), calls=%async_computation.7 | async-start | bytes 2228224 | tf_op jit(solution)/shard_map/all_to_all | solution.py:37
  191.1 14.1 %collective-permute-start.4 = (bf16[144,256]{1,0:T(8,128)(2,1)S(1)}, bf16[144,256]{1,0:T(8,128)(2,1)S(1)}, u32[]{:S(2)}, u32[]{:S(2)}) collective-permute-start(bf16[144,256]{1,0:T(8,128)(2,1)S(1)} %maximum_maximum_fusion.2), channel_id=1, source_target_pairs={{0,64},{64,0},{1,65},{65,1},{2,66},{66,2},{3,67},{67,3},{4,68},{68... | collective-permute-start | bytes 221192 | tf_op jit(solution)/shard_map/ppermute | solution.py:54
  205.7 6.7 %collective-permute-start.5 = (bf16[2048,128]{1,0:T(8,128)(2,1)S(1)}, bf16[2048,128]{1,0:T(8,128)(2,1)S(1)}, u32[]{:S(2)}, u32[]{:S(2)}) collective-permute-start(bf16[2048,128]{1,0:T(8,128)(2,1)S(1)} %fusion.1), channel_id=1, source_target_pairs={{0,1},{1,0},{2,3},{3,2},{4,5},{5,4},{6,7},{7,6},{8,9},{9,8},{10,11... | collective-permute-start | bytes 1572872 | tf_op jit(solution)/shard_map/ppermute | solution.py:54
  212.9 10.4 %collective-permute-start.6 = (bf16[1024,128]{1,0:T(8,128)(2,1)S(1)}, bf16[1024,128]{1,0:T(8,128)(2,1)S(1)}, u32[]{:S(2)}, u32[]{:S(2)}) collective-permute-start(bf16[1024,128]{1,0:T(8,128)(2,1)S(1)} %slice.486), channel_id=1, source_target_pairs={{0,2},{2,0},{1,3},{3,1},{4,6},{6,4},{5,7},{7,5},{8,10},{10,8},{9,1... | collective-permute-start | bytes 786440 | tf_op jit(solution)/shard_map/ppermute | solution.py:54
  224.1 19.2 %all-to-all-start.8 = ((bf16[4,256,128]{2,1,0:T(8,128)(2,1)}), bf16[4,256,128]{2,1,0:T(8,128)(2,1)S(1)}, u32[]{:S(2)}, u32[]{:S(2)}) async-start(bf16[4,256,128]{2,1,0:T(8,128)(2,1)} %bitcast.199), calls=%async_computation.8 | async-start | bytes 524288 | tf_op jit(solution)/shard_map/all_to_all | solution.py:37
  243.4 8.5 %collective-permute-start.7 = (bf16[256,128]{1,0:T(8,128)(2,1)S(1)}, bf16[256,128]{1,0:T(8,128)(2,1)S(1)}, u32[]{:S(2)}, u32[]{:S(2)}) collective-permute-start(bf16[256,128]{1,0:T(8,128)(2,1)S(1)} %convert_element_type.233), channel_id=1, source_target_pairs={{0,0},{1,33},{2,66},{3,99},{4,132},{5,165},{6,198},{7,231},{8,264}... | collective-permute-start | bytes 196616 | tf_op jit(solution)/shard_map/ppermute | solution.py:221
  251.8 4.7 %collective-permute-start.8 = (bf16[128,128]{1,0:T(8,128)(2,1)S(1)}, bf16[128,128]{1,0:T(8,128)(2,1)S(1)}, u32[]{:S(2)}, u32[]{:S(2)}) collective-permute-start(bf16[128,128]{1,0:T(8,128)(2,1)S(1)} %get-tuple-element.87), channel_id=1, source_target_pairs={{0,16},{16,0},{32,48},{48,32},{1,17},{17,1},{33,49},{49,33},{2,18}... | collective-permute-start | bytes 98312 | tf_op jit(solution)/shard_map/ppermute | solution.py:54
  259.6 15.4 %all-to-all-start.9 = ((bf16[4,296,128]{2,1,0:T(8,128)(2,1)}), bf16[4,296,128]{2,1,0:T(8,128)(2,1)S(1)}, u32[]{:S(2)}, u32[]{:S(2)}) async-start(bf16[4,296,128]{2,1,0:T(8,128)(2,1)} %broadcast_in_dim.20), calls=%async_computation.9 | async-start | bytes 606208 | tf_op jit(solution)/shard_map/all_to_all | solution.py:37
  275.1 25.0 %collective-permute-start.9 = (bf16[4,296,128]{2,1,0:T(8,128)(2,1)S(1)}, bf16[4,296,128]{2,1,0:T(8,128)(2,1)S(1)}, u32[]{:S(2)}, u32[]{:S(2)}) collective-permute-start(bf16[4,296,128]{2,1,0:T(8,128)(2,1)S(1)} %all-to-all-done.9), channel_id=1, source_target_pairs={{0,1},{1,0},{2,3},{3,2},{4,5},{5,4},{6,7},{7,6},{8,9},{9,8},{10,11... | collective-permute-start | bytes 909320 | tf_op jit(solution)/shard_map/ppermute | solution.py:54
  280.9 25.3 %collective-permute-start.10 = (bf16[4,296,128]{2,1,0:T(8,128)(2,1)S(1)}, bf16[4,296,128]{2,1,0:T(8,128)(2,1)S(1)}, u32[]{:S(2)}, u32[]{:S(2)}) collective-permute-start(bf16[4,296,128]{2,1,0:T(8,128)(2,1)S(1)} %all-to-all-done.9), channel_id=1, source_target_pairs={{0,2},{2,0},{1,3},{3,1},{4,6},{6,4},{5,7},{7,5},{8,10},{10,8},{9,1... | collective-permute-start | bytes 909320 | tf_op jit(solution)/shard_map/ppermute | solution.py:54
  300.1 1.1 copy-start.5
  306.2 6.8 %copy-start.12 = (bf16[4,296,128]{2,1,0:T(8,128)(2,1)}, bf16[4,296,128]{2,1,0:T(8,128)(2,1)S(1)}, u32[]{:S(2)}) copy-start(bf16[4,296,128]{2,1,0:T(8,128)(2,1)S(1)} %collective-permute-done.10) | copy-start | bytes 909316
  306.2 3.7 %collective-permute-start.11 = (bf16[4,296,128]{2,1,0:T(8,128)(2,1)S(1)}, bf16[4,296,128]{2,1,0:T(8,128)(2,1)S(1)}, u32[]{:S(2)}, u32[]{:S(2)}) collective-permute-start(bf16[4,296,128]{2,1,0:T(8,128)(2,1)S(1)} %collective-permute-done.10), channel_id=1, source_target_pairs={{0,1},{1,0},{2,3},{3,2},{4,5},{5,4},{6,7},{7,6},{8,9},{9,8},{10,11... | collective-permute-start | bytes 909320 | tf_op jit(solution)/shard_map/ppermute | solution.py:54
  310.0 4.3 %copy-start.14 = (bf16[4,296,128]{2,1,0:T(8,128)(2,1)}, bf16[4,296,128]{2,1,0:T(8,128)(2,1)S(1)}, u32[]{:S(2)}) copy-start(bf16[4,296,128]{2,1,0:T(8,128)(2,1)S(1)} %collective-permute-done.11) | copy-start | bytes 909316
  314.3 25.1 %all-to-all-start.10 = ((bf16[16,152,256]{2,1,0:T(8,128)(2,1)}), bf16[16,152,256]{2,1,0:T(8,128)(2,1)S(1)}, u32[]{:S(2)}, u32[]{:S(2)}) async-start(bf16[16,152,256]{2,1,0:T(8,128)(2,1)} %broadcast_in_dim.21), calls=%async_computation.10 | async-start | bytes 2490368 | tf_op jit(solution)/shard_map/all_to_all | solution.py:37
  319.5 1.0 copy-start.13
  319.5 8.2 %copy-start.15 = (bf16[4,296,128]{2,1,0:T(8,128)(2,1)S(1)}, bf16[4,296,128]{2,1,0:T(8,128)(2,1)}, u32[]{:S(2)}) copy-start(bf16[4,296,128]{2,1,0:T(8,128)(2,1)} %copy-done.14) | copy-start | bytes 909316
  321.3 18.0 %collective-permute-start.12 = (bf16[152,256]{1,0:T(8,128)(2,1)S(1)}, bf16[152,256]{1,0:T(8,128)(2,1)S(1)}, u32[]{:S(2)}, u32[]{:S(2)}) collective-permute-start(bf16[152,256]{1,0:T(8,128)(2,1)S(1)} %maximum_maximum_fusion), channel_id=1, source_target_pairs={{0,64},{64,0},{1,65},{65,1},{2,66},{66,2},{3,67},{67,3},{4,68},{68... | collective-permute-start | bytes 233480 | tf_op jit(solution)/shard_map/ppermute | solution.py:54
  340.5 24.1 %all-to-all-start.11 = ((bf16[16,152,256]{2,1,0:T(8,128)(2,1)}), bf16[16,152,256]{2,1,0:T(8,128)(2,1)S(1)}, u32[]{:S(2)}, u32[]{:S(2)}) async-start(bf16[16,152,256]{2,1,0:T(8,128)(2,1)} %broadcast_in_dim.22), calls=%async_computation.11 | async-start | bytes 2490368 | tf_op jit(solution)/shard_map/all_to_all | solution.py:37
  347.1 1.3 copy-start.19
  347.2 1.3 copy-start.20
  347.2 1.3 copy-start.21
  347.2 1.3 copy-start.22
  350.5 14.2 %copy-start.11 = (f32[1,128,128]{2,1,0:T(8,128)S(1)}, f32[1,128,128]{2,1,0:T(8,128)}, u32[]{:S(2)}) copy-start(f32[1,128,128]{2,1,0:T(8,128)} %param.10) | copy-start | bytes 196612
  366.0 3.6 copy-start.8
  366.0 3.6 copy-start.23
  366.0 3.6 copy-start.25

commit v5 on v4

--- a/solution.py
+++ b/solution.py
@@ -135,13 +135,22 @@
     rows_own, rows_far = rows_own.reshape(ROWS, HALF), rows_far.reshape(ROWS, HALF)
     weights_own, weights_far = split_at(weights.reshape(4, 2, D // 8, HEAD), 1, zh)
     weights_own, weights_far = weights_own.reshape(HALF, HEAD), weights_far.reshape(HALF, HEAD)
-    panel_far, rows_own, rows_far, weights_own, weights_far = hold(
-        (panel_far, rows_own, rows_far, weights_own, weights_far)
+    target_own, target_far = split_at(target[0].reshape(ROWS, 4, 2, HEAD), 2, zh)
+    target_own, target_far = (
+        lax.dynamic_slice_in_dim(half.reshape(ROWS, 4 * HEAD), tensor % 8 * 16, 16, 0)
+        for half in (target_own, target_far)
+    )
+    panel_far, rows_own, rows_far, weights_own, weights_far, target_far = hold(
+        (panel_far, rows_own, rows_far, weights_own, weights_far, target_far)
     )
     panel_far = panel_far.reshape(HALF, COLS)
 
     rotated = ((mul(rows_own, panel_own) + mul(rows_far, panel_far)) / root_width).astype(low)
-    tokens = jnp.concatenate([rotated, swap(rotated, "zh")], 0)
+    message = jnp.concatenate([rotated, target_far.reshape(32, COLS)], 0)
+    message, weights_own, weights_far = hold((message, weights_own, weights_far))
+    message = swap(message, "zh")
+    tokens = jnp.concatenate([rotated, message[:ROWS]], 0)
+    target_here = jnp.where(tensor < 8, target_own, message[ROWS:].reshape(16, 4 * HEAD))
     unmixed = (mul(weights_own, panel_own, first) + mul(weights_far, panel_far, first)) / root_width
     tangent = jnp.tanh(mul(head_matrix, unmixed, first, precise) / scales)
     quantized = (scales * tangent).astype(low)
@@ -154,13 +163,6 @@
         )
         for tokens, head in ((rows_own, weights_own), (rows_far, weights_far))
     )
-    target_own, target_far = split_at(target[0].reshape(ROWS, 4, 2, HEAD), 2, zh)
-    target_own, target_far = (
-        lax.dynamic_slice_in_dim(half.reshape(ROWS, 4 * HEAD), tensor % 8 * 16, 16, 0)
-        for half in (target_own, target_far)
-    )
-    target_here = jnp.where(tensor < 8, target_own, swap(target_far, "zh"))
-
     part = mul(tokens, heads, second).astype(low)
     part = exchange(part.reshape(16, 16, 4 * HEAD), TENSOR)
     part, left_own, left_far, target_here = hold((part, left_own, left_far, target_here))

time: 376 us -> 368 us (0.979)
  starting transfers between devices: 160 us -> 156 us
    ppermute x12 -> x11, starting transfers between devices: 86.1 us -> 77.3 us  [swap(): return lax.ppermute(block, axis, [(i, i ^ bit) for i in range(n)])]
    all_to_all x12, starting transfers between devices: 66.7 us -> 73.6 us  [exchange(): out = lax.all_to_all(flat, axes, split_axis=0, concat_axis=0, tiled=True)]
    ppermute x12 -> x11, waiting for transfers between devices: 35.8 us -> 33.7 us  [swap(): return lax.ppermute(block, axis, [(i, i ^ bit) for i in range(n)])]
    unnamed x59 -> x70, local copies, waits for them, and re-layouts: 9 us -> 7.35 us
  transfers between devices with their start and end apart: 25 -> 24, of which waited for: 20 -> 18; matrix products, arithmetic and copies ran while one was open for 9% -> 9% of each run, Pallas kernels for 0% -> 0%
where the time goes in v5:
time: 368 us; the launch traced here: 364 us
  starting transfers between devices  156 us (42%)
  waiting for transfers between devices  136 us (37%)
  local copies, waits for them, and re-layouts  24.8 us (7%)
  other arithmetic  22.5 us (6%)
  matrix products  18.4 us (5%)
  between operations  6.36 us (2%)
    all_to_all x12, waiting for transfers between devices, exchange(): out = lax.all_to_all(flat, axes, split_axis=0, concat_axis=0, tiled=True)  100 us
    ppermute x11, starting transfers between devices, swap(): return lax.ppermute(block, axis, [(i, i ^ bit) for i in range(n)])  77.3 us
    all_to_all x12, starting transfers between devices, exchange(): out = lax.all_to_all(flat, axes, split_axis=0, concat_axis=0, tiled=True)  73.6 us
    ppermute x11, waiting for transfers between devices, swap(): return lax.ppermute(block, axis, [(i, i ^ bit) for i in range(n)])  33.7 us
    dot_general x21, matrix products, mul(): lax.dot_general(a, b, dims, precision=precision, preferred_element_type=j...  17 us
  transfers between devices with their start and end apart: 24, of which 18 were waited for; matrix products, arithmetic and copies ran while one was open for 9% of the time, Pallas kernels for 0%

profile of v5, /device:TPU:1, one launch (start us, length us, event | category | flops | bytes accessed | tf_op | source)
XLA Modules:
  0.0 363.6 jit_solution(10358576473744124401)
XLA Ops:
  1.5 1.1 broadcast_in_dim.16
  2.7 7.7 %all-to-all-start = ((bf16[16,128,256]{2,1,0:T(8,128)(2,1)}), bf16[16,128,256]{2,1,0:T(8,128)(2,1)S(1)}, u32[]{:S(2)}, u32[]{:S(2)}) async-start(bf16[16,128,256]{2,1,0:T(8,128)(2,1)} %broadcast_in_dim.16), calls=%async_computation | async-start | bytes 2097152 | tf_op jit(solution)/shard_map/all_to_all | solution.py:37
  10.4 15.6 %collective-permute-start = (bf16[128,256]{1,0:T(8,128)(2,1)S(1)}, bf16[128,256]{1,0:T(8,128)(2,1)S(1)}, u32[]{:S(2)}, u32[]{:S(2)}) collective-permute-start(bf16[128,256]{1,0:T(8,128)(2,1)S(1)} %convert_element_type.202), channel_id=1, source_target_pairs={{0,64},{64,0},{1,65},{65,1},{2,66},{66,2},{3,67},{67,3},{4,68},{68... | collective-permute-start | bytes 196616 | tf_op jit(solution)/shard_map/ppermute | solution.py:54
  27.3 1.5 fusion.48
  31.4 1.1 broadcast_in_dim.17
  32.5 6.7 %all-to-all-start.1 = ((bf16[16,128,256]{2,1,0:T(8,128)(2,1)}), bf16[16,128,256]{2,1,0:T(8,128)(2,1)S(1)}, u32[]{:S(2)}, u32[]{:S(2)}) async-start(bf16[16,128,256]{2,1,0:T(8,128)(2,1)} %broadcast_in_dim.17), calls=%async_computation.1 | async-start | bytes 2097152 | tf_op jit(solution)/shard_map/all_to_all | solution.py:37
  41.4 12.8 %all-to-all-done.1 = bf16[16,128,256]{2,1,0:T(8,128)(2,1)S(1)} async-done(((bf16[16,128,256]{2,1,0:T(8,128)(2,1)}), bf16[16,128,256]{2,1,0:T(8,128)(2,1)S(1)}, u32[]{:S(2)}, u32[]{:S(2)}) %all-to-all-start.1) | async-done | bytes 1048608 | tf_op jit(solution)/shard_map/all_to_all | solution.py:37
  54.3 1.0 fusion.47
  57.7 6.3 %collective-permute-start.1 = (bf16[160,256]{1,0:T(8,128)(2,1)}, bf16[160,256]{1,0:T(8,128)(2,1)}, u32[]{:S(2)}, u32[]{:S(2)}) collective-permute-start(bf16[160,256]{1,0:T(8,128)(2,1)} %pad_maximum_fusion.12), channel_id=1, source_target_pairs={{0,64},{64,0},{1,65},{65,1},{2,66},{66,2},{3,67},{67,3},{4,68},{68... | collective-permute-start | bytes 245768 | tf_op jit(solution)/shard_map/ppermute | solution.py:54
  64.5 1.0 multiply_convert_fusion
  66.2 3.4 all-to-all-start.2
  69.7 1.4 convolution_convert_fusion.2
  71.1 3.7 %collective-permute-done.1 = bf16[160,256]{1,0:T(8,128)(2,1)} collective-permute-done((bf16[160,256]{1,0:T(8,128)(2,1)}, bf16[160,256]{1,0:T(8,128)(2,1)}, u32[]{:S(2)}, u32[]{:S(2)}) %collective-permute-start.1) | collective-permute-done | bytes 81952 | tf_op jit(solution)/shard_map/ppermute | solution.py:54
  75.7 1.0 convolution_convert_fusion.5
  76.7 14.1 %all-to-all-start.3 = ((bf16[16,16,512]{2,1,0:T(8,128)(2,1)}), bf16[16,16,512]{2,1,0:T(8,128)(2,1)}, u32[]{:S(2)}, u32[]{:S(2)}) async-start(bf16[16,16,512]{2,1,0:T(8,128)(2,1)} %bitcast.10), calls=%async_computation.3 | async-start | bytes 524288 | tf_op jit(solution)/shard_map/all_to_all | solution.py:37
  91.8 1.5 pad_maximum_fusion.2
  94.4 13.4 %all-to-all-done.3 = bf16[16,16,512]{2,1,0:T(8,128)(2,1)} async-done(((bf16[16,16,512]{2,1,0:T(8,128)(2,1)}), bf16[16,16,512]{2,1,0:T(8,128)(2,1)}, u32[]{:S(2)}, u32[]{:S(2)}) %all-to-all-start.3) | async-done | bytes 262176 | tf_op jit(solution)/shard_map/all_to_all | solution.py:37
  107.9 1.0 convert_reduce_fusion.3
  109.6 5.3 %all-to-all-start.4 = ((bf16[16,16,512]{2,1,0:T(8,128)(2,1)}), bf16[16,16,512]{2,1,0:T(8,128)(2,1)}, u32[]{:S(2)}, u32[]{:S(2)}) async-start(bf16[16,16,512]{2,1,0:T(8,128)(2,1)} %broadcast_in_dim.19), calls=%async_computation.4 | async-start | bytes 524288 | tf_op jit(solution)/shard_map/all_to_all | solution.py:37
  115.2 0.9 copy-done.7
  116.7 15.3 %all-to-all-done.4 = bf16[16,16,512]{2,1,0:T(8,128)(2,1)} async-done(((bf16[16,16,512]{2,1,0:T(8,128)(2,1)}), bf16[16,16,512]{2,1,0:T(8,128)(2,1)}, u32[]{:S(2)}, u32[]{:S(2)}) %all-to-all-start.4) | async-done | bytes 262176 | tf_op jit(solution)/shard_map/all_to_all | solution.py:37
  132.0 1.2 fusion.57
  133.9 6.4 %collective-permute-start.2 = (bf16[128,256]{1,0:T(8,128)(2,1)}, bf16[128,256]{1,0:T(8,128)(2,1)}, u32[]{:S(2)}, u32[]{:S(2)}) collective-permute-start(bf16[128,256]{1,0:T(8,128)(2,1)} %slice.497), channel_id=1, source_target_pairs={{0,64},{64,0},{1,65},{65,1},{2,66},{66,2},{3,67},{67,3},{4,68},{68... | collective-permute-start | bytes 196616 | tf_op jit(solution)/shard_map/ppermute | solution.py:54
  140.3 1.9 convolution_convert_fusion.4
  142.3 3.5 all-to-all-start.5
  145.8 4.6 %collective-permute-done.2 = bf16[128,256]{1,0:T(8,128)(2,1)} collective-permute-done((bf16[128,256]{1,0:T(8,128)(2,1)}, bf16[128,256]{1,0:T(8,128)(2,1)}, u32[]{:S(2)}, u32[]{:S(2)}) %collective-permute-start.2) | collective-permute-done | bytes 65568 | tf_op jit(solution)/shard_map/ppermute | solution.py:54
  151.7 1.2 fusion.53
  154.6 1.1 pad_maximum_fusion
  155.7 3.7 %all-to-all-start.6 = ((bf16[16,132,256]{2,1,0:T(8,128)(2,1)}), bf16[16,132,256]{2,1,0:T(8,128)(2,1)S(1)}, u32[]{:S(2)}, u32[]{:S(2)}) async-start(bf16[16,132,256]{2,1,0:T(8,128)(2,1)} %pad_maximum_fusion), calls=%async_computation.6 | async-start | bytes 2228224 | tf_op jit(solution)/shard_map/all_to_all | solution.py:37
  159.5 1.7 convolution_convert_fusion
  161.2 1.1 pad_maximum_fusion.1
  162.3 16.0 %all-to-all-done.6 = bf16[16,132,256]{2,1,0:T(8,128)(2,1)S(1)} async-done(((bf16[16,132,256]{2,1,0:T(8,128)(2,1)}), bf16[16,132,256]{2,1,0:T(8,128)(2,1)S(1)}, u32[]{:S(2)}, u32[]{:S(2)}) %all-to-all-start.6) | async-done | bytes 1081376 | tf_op jit(solution)/shard_map/all_to_all | solution.py:37
  178.3 1.0 copy-done.4
  179.3 3.8 %all-to-all-start.7 = ((bf16[16,132,256]{2,1,0:T(8,128)(2,1)}), bf16[16,132,256]{2,1,0:T(8,128)(2,1)S(1)}, u32[]{:S(2)}, u32[]{:S(2)}) async-start(bf16[16,132,256]{2,1,0:T(8,128)(2,1)} %pad_maximum_fusion.1), calls=%async_computation.7 | async-start | bytes 2228224 | tf_op jit(solution)/shard_map/all_to_all | solution.py:37
  184.0 1.4 slice_reduce_fusion
  185.4 7.7 %collective-permute-start.3 = (bf16[144,256]{1,0:T(8,128)(2,1)S(1)}, bf16[144,256]{1,0:T(8,128)(2,1)S(1)}, u32[]{:S(2)}, u32[]{:S(2)}) collective-permute-start(bf16[144,256]{1,0:T(8,128)(2,1)S(1)} %maximum_maximum_fusion.2), channel_id=1, source_target_pairs={{0,64},{64,0},{1,65},{65,1},{2,66},{66,2},{3,67},{67,3},{4,68},{68... | collective-permute-start | bytes 221192 | tf_op jit(solution)/shard_map/ppermute | solution.py:54
  193.1 6.3 %all-to-all-done.7 = bf16[16,132,256]{2,1,0:T(8,128)(2,1)S(1)} async-done(((bf16[16,132,256]{2,1,0:T(8,128)(2,1)}), bf16[16,132,256]{2,1,0:T(8,128)(2,1)S(1)}, u32[]{:S(2)}, u32[]{:S(2)}) %all-to-all-start.7) | async-done | bytes 1081376 | tf_op jit(solution)/shard_map/all_to_all | solution.py:37
  200.0 5.2 %collective-permute-start.4 = (bf16[2048,128]{1,0:T(8,128)(2,1)S(1)}, bf16[2048,128]{1,0:T(8,128)(2,1)S(1)}, u32[]{:S(2)}, u32[]{:S(2)}) collective-permute-start(bf16[2048,128]{1,0:T(8,128)(2,1)S(1)} %fusion.1), channel_id=1, source_target_pairs={{0,1},{1,0},{2,3},{3,2},{4,5},{5,4},{6,7},{7,6},{8,9},{9,8},{10,11... | collective-permute-start | bytes 1572872 | tf_op jit(solution)/shard_map/ppermute | solution.py:54
  205.2 1.5 collective-permute-done.4
  207.2 3.9 %collective-permute-start.5 = (bf16[1024,128]{1,0:T(8,128)(2,1)S(1)}, bf16[1024,128]{1,0:T(8,128)(2,1)S(1)}, u32[]{:S(2)}, u32[]{:S(2)}) collective-permute-start(bf16[1024,128]{1,0:T(8,128)(2,1)S(1)} %slice.496), channel_id=1, source_target_pairs={{0,2},{2,0},{1,3},{3,1},{4,6},{6,4},{5,7},{7,5},{8,10},{10,8},{9,1... | collective-permute-start | bytes 786440 | tf_op jit(solution)/shard_map/ppermute | solution.py:54
  211.1 6.4 %collective-permute-done.5 = bf16[1024,128]{1,0:T(8,128)(2,1)S(1)} collective-permute-done((bf16[1024,128]{1,0:T(8,128)(2,1)S(1)}, bf16[1024,128]{1,0:T(8,128)(2,1)S(1)}, u32[]{:S(2)}, u32[]{:S(2)}) %collective-permute-start.5) | collective-permute-done | bytes 262176 | tf_op jit(solution)/shard_map/ppermute | solution.py:54
  218.3 3.4 all-to-all-start.8
  222.3 14.9 %all-to-all-done.8 = bf16[4,256,128]{2,1,0:T(8,128)(2,1)S(1)} async-done(((bf16[4,256,128]{2,1,0:T(8,128)(2,1)}), bf16[4,256,128]{2,1,0:T(8,128)(2,1)S(1)}, u32[]{:S(2)}, u32[]{:S(2)}) %all-to-all-start.8) | async-done | bytes 262176 | tf_op jit(solution)/shard_map/all_to_all | solution.py:37
  237.3 4.9 %collective-permute-start.6 = (bf16[256,128]{1,0:T(8,128)(2,1)S(1)}, bf16[256,128]{1,0:T(8,128)(2,1)S(1)}, u32[]{:S(2)}, u32[]{:S(2)}) collective-permute-start(bf16[256,128]{1,0:T(8,128)(2,1)S(1)} %convert_element_type.233), channel_id=1, source_target_pairs={{0,0},{1,33},{2,66},{3,99},{4,132},{5,165},{6,198},{7,231},{8,264}... | collective-permute-start | bytes 196616 | tf_op jit(solution)/shard_map/ppermute | solution.py:223
  242.2 1.6 collective-permute-done.6
  243.8 3.4 collective-permute-start.7
  251.7 7.9 %all-to-all-start.9 = ((bf16[4,296,128]{2,1,0:T(8,128)(2,1)}), bf16[4,296,128]{2,1,0:T(8,128)(2,1)S(1)}, u32[]{:S(2)}, u32[]{:S(2)}) async-start(bf16[4,296,128]{2,1,0:T(8,128)(2,1)} %broadcast_in_dim.20), calls=%async_computation.9 | async-start | bytes 606208 | tf_op jit(solution)/shard_map/all_to_all | solution.py:37
  261.4 7.6 %all-to-all-done.9 = bf16[4,296,128]{2,1,0:T(8,128)(2,1)S(1)} async-done(((bf16[4,296,128]{2,1,0:T(8,128)(2,1)}), bf16[4,296,128]{2,1,0:T(8,128)(2,1)S(1)}, u32[]{:S(2)}, u32[]{:S(2)}) %all-to-all-start.9) | async-done | bytes 303136 | tf_op jit(solution)/shard_map/all_to_all | solution.py:37
  269.1 5.4 %collective-permute-start.8 = (bf16[4,296,128]{2,1,0:T(8,128)(2,1)S(1)}, bf16[4,296,128]{2,1,0:T(8,128)(2,1)S(1)}, u32[]{:S(2)}, u32[]{:S(2)}) collective-permute-start(bf16[4,296,128]{2,1,0:T(8,128)(2,1)S(1)} %all-to-all-done.9), channel_id=1, source_target_pairs={{0,1},{1,0},{2,3},{3,2},{4,5},{5,4},{6,7},{7,6},{8,9},{9,8},{10,11... | collective-permute-start | bytes 909320 | tf_op jit(solution)/shard_map/ppermute | solution.py:54
  274.5 13.9 %collective-permute-start.9 = (bf16[4,296,128]{2,1,0:T(8,128)(2,1)S(1)}, bf16[4,296,128]{2,1,0:T(8,128)(2,1)S(1)}, u32[]{:S(2)}, u32[]{:S(2)}) collective-permute-start(bf16[4,296,128]{2,1,0:T(8,128)(2,1)S(1)} %all-to-all-done.9), channel_id=1, source_target_pairs={{0,2},{2,0},{1,3},{3,1},{4,6},{6,4},{5,7},{7,5},{8,10},{10,8},{9,1... | collective-permute-start | bytes 909320 | tf_op jit(solution)/shard_map/ppermute | solution.py:54
  288.3 1.4 fusion.58
  291.1 4.8 %collective-permute-done.9 = bf16[4,296,128]{2,1,0:T(8,128)(2,1)S(1)} collective-permute-done((bf16[4,296,128]{2,1,0:T(8,128)(2,1)S(1)}, bf16[4,296,128]{2,1,0:T(8,128)(2,1)S(1)}, u32[]{:S(2)}, u32[]{:S(2)}) %collective-permute-start.9) | collective-permute-done | bytes 303136 | tf_op jit(solution)/shard_map/ppermute | solution.py:54
  295.9 2.5 collective-permute-start.10
  301.7 1.0 fusion.54
  302.8 1.2 broadcast_in_dim.21
  303.9 7.6 %all-to-all-start.10 = ((bf16[16,152,256]{2,1,0:T(8,128)(2,1)}), bf16[16,152,256]{2,1,0:T(8,128)(2,1)S(1)}, u32[]{:S(2)}, u32[]{:S(2)}) async-start(bf16[16,152,256]{2,1,0:T(8,128)(2,1)} %broadcast_in_dim.21), calls=%async_computation.10 | async-start | bytes 2490368 | tf_op jit(solution)/shard_map/all_to_all | solution.py:37
  313.3 6.9 %collective-permute-start.11 = (bf16[152,256]{1,0:T(8,128)(2,1)S(1)}, bf16[152,256]{1,0:T(8,128)(2,1)S(1)}, u32[]{:S(2)}, u32[]{:S(2)}) collective-permute-start(bf16[152,256]{1,0:T(8,128)(2,1)S(1)} %maximum_maximum_fusion), channel_id=1, source_target_pairs={{0,64},{64,0},{1,65},{65,1},{2,66},{66,2},{3,67},{67,3},{4,68},{68... | collective-permute-start | bytes 233480 | tf_op jit(solution)/shard_map/ppermute | solution.py:54
  321.1 11.3 %collective-permute-done.11 = bf16[152,256]{1,0:T(8,128)(2,1)S(1)} collective-permute-done((bf16[152,256]{1,0:T(8,128)(2,1)S(1)}, bf16[152,256]{1,0:T(8,128)(2,1)S(1)}, u32[]{:S(2)}, u32[]{:S(2)}) %collective-permute-start.11) | collective-permute-done | bytes 77856 | tf_op jit(solution)/shard_map/ppermute | solution.py:54
  332.4 1.2 broadcast_in_dim.22
  333.5 6.6 %all-to-all-start.11 = ((bf16[16,152,256]{2,1,0:T(8,128)(2,1)}), bf16[16,152,256]{2,1,0:T(8,128)(2,1)S(1)}, u32[]{:S(2)}, u32[]{:S(2)}) async-start(bf16[16,152,256]{2,1,0:T(8,128)(2,1)} %broadcast_in_dim.22), calls=%async_computation.11 | async-start | bytes 2490368 | tf_op jit(solution)/shard_map/all_to_all | solution.py:37
  340.2 1.2 maximum_select_fusion.9
  341.5 1.2 broadcast_select_fusion
  343.9 13.8 %all-to-all-done.11 = bf16[16,152,256]{2,1,0:T(8,128)(2,1)S(1)} async-done(((bf16[16,152,256]{2,1,0:T(8,128)(2,1)}), bf16[16,152,256]{2,1,0:T(8,128)(2,1)S(1)}, u32[]{:S(2)}, u32[]{:S(2)}) %all-to-all-start.11) | async-done | bytes 1245216 | tf_op jit(solution)/shard_map/all_to_all | solution.py:37
  362.6 1.0 subtract_add_fusion
  (190 shorter events, 37.2 us)
Async XLA Ops:
  2.6 23.4 %copy-start.31 = (bf16[1,128,1024]{2,1,0:T(8,128)(2,1)S(1)}, bf16[1,128,1024]{2,1,0:T(8,128)(2,1)}, u32[]{:S(2)}) copy-start(bf16[1,128,1024]{2,1,0:T(8,128)(2,1)} %param.7) | copy-start | bytes 786436
  2.7 28.7 %all-to-all-start = ((bf16[16,128,256]{2,1,0:T(8,128)(2,1)}), bf16[16,128,256]{2,1,0:T(8,128)(2,1)S(1)}, u32[]{:S(2)}, u32[]{:S(2)}) async-start(bf16[16,128,256]{2,1,0:T(8,128)(2,1)} %broadcast_in_dim.16), calls=%async_computation | async-start | bytes 2097152 | tf_op jit(solution)/shard_map/all_to_all | solution.py:37
  10.4 16.1 %copy-start.20 = (bf16[1,128,4096]{2,1,0:T(8,128)(2,1)S(1)}, bf16[1,128,4096]{2,1,0:T(8,128)(2,1)}, u32[]{:S(2)}) copy-start(bf16[1,128,4096]{2,1,0:T(8,128)(2,1)} %param.6) | copy-start | bytes 3145732
  10.4 21.0 %collective-permute-start = (bf16[128,256]{1,0:T(8,128)(2,1)S(1)}, bf16[128,256]{1,0:T(8,128)(2,1)S(1)}, u32[]{:S(2)}, u32[]{:S(2)}) collective-permute-start(bf16[128,256]{1,0:T(8,128)(2,1)S(1)} %convert_element_type.202), channel_id=1, source_target_pairs={{0,64},{64,0},{1,65},{65,1},{2,66},{66,2},{3,67},{67,3},{4,68},{68... | collective-permute-start | bytes 196616 | tf_op jit(solution)/shard_map/ppermute | solution.py:54
  29.3 1.9 copy-start.19
  32.5 21.7 %all-to-all-start.1 = ((bf16[16,128,256]{2,1,0:T(8,128)(2,1)}), bf16[16,128,256]{2,1,0:T(8,128)(2,1)S(1)}, u32[]{:S(2)}, u32[]{:S(2)}) async-start(bf16[16,128,256]{2,1,0:T(8,128)(2,1)} %broadcast_in_dim.17), calls=%async_computation.1 | async-start | bytes 2097152 | tf_op jit(solution)/shard_map/all_to_all | solution.py:37
  54.3 1.2 copy-start.2
  55.3 1.1 copy-start
  57.7 6.7 %copy-start.13 = (f32[1,128,128]{2,1,0:T(8,128)S(1)}, f32[1,128,128]{2,1,0:T(8,128)}, u32[]{:S(2)}) copy-start(f32[1,128,128]{2,1,0:T(8,128)} %param.10) | copy-start | bytes 196612
  57.7 6.7 %copy-start.32 = (f32[1,128]{1,0:T(1,128)S(1)}, f32[1,128]{1,0:T(1,128)}, u32[]{:S(2)}) copy-start(f32[1,128]{1,0:T(1,128)} %param.9) | copy-start | bytes 1540
  57.7 17.1 %collective-permute-start.1 = (bf16[160,256]{1,0:T(8,128)(2,1)}, bf16[160,256]{1,0:T(8,128)(2,1)}, u32[]{:S(2)}, u32[]{:S(2)}) collective-permute-start(bf16[160,256]{1,0:T(8,128)(2,1)} %pad_maximum_fusion.12), channel_id=1, source_target_pairs={{0,64},{64,0},{1,65},{65,1},{2,66},{66,2},{3,67},{67,3},{4,68},{68... | collective-permute-start | bytes 245768 | tf_op jit(solution)/shard_map/ppermute | solution.py:54
  64.5 1.8 copy-start.22
  66.2 9.4 %all-to-all-start.2 = ((bf16[4,128,256]{2,1,0:T(8,128)(2,1)}), bf16[4,128,256]{2,1,0:T(8,128)(2,1)S(1)}, u32[]{:S(2)}, u32[]{:S(2)}) async-start(bf16[4,128,256]{2,1,0:T(8,128)(2,1)} %broadcast_in_dim.18), calls=%async_computation.2 | async-start | bytes 524288 | tf_op jit(solution)/shard_map/all_to_all | solution.py:37
  71.1 20.3 %copy-start.1 = (bf16[16,8,4,512]{3,1,2,0:T(8,128)(2,1)S(1)}, bf16[16,8,4,512]{3,1,2,0:T(8,128)(2,1)}, u32[]{:S(2)}) copy-start(bf16[16,8,4,512]{3,1,2,0:T(8,128)(2,1)} %copy.120) | copy-start | bytes 1572868
  71.1 20.3 %copy-start.3 = (bf16[16,8,4,512]{3,1,2,0:T(8,128)(2,1)S(1)}, bf16[16,8,4,512]{3,1,2,0:T(8,128)(2,1)}, u32[]{:S(2)}) copy-start(bf16[16,8,4,512]{3,1,2,0:T(8,128)(2,1)} %copy.119) | copy-start | bytes 1572868
  75.7 15.1 %copy-start.29 = (bf16[128,256]{1,0:T(8,128)(2,1)}, bf16[128,256]{1,0:T(8,128)(2,1)S(1)}, u32[]{:S(2)}) copy-start(bf16[128,256]{1,0:T(8,128)(2,1)S(1)} %slice.344) | copy-start | bytes 196612
  76.7 31.2 %all-to-all-start.3 = ((bf16[16,16,512]{2,1,0:T(8,128)(2,1)}), bf16[16,16,512]{2,1,0:T(8,128)(2,1)}, u32[]{:S(2)}, u32[]{:S(2)}) async-start(bf16[16,16,512]{2,1,0:T(8,128)(2,1)} %bitcast.10), calls=%async_computation.3 | async-start | bytes 524288 | tf_op jit(solution)/shard_map/all_to_all | solution.py:37
  90.8 1.0 copy-start.12
  91.8 1.5 copy-start.10
  91.8 1.6 copy-start.11
  109.6 22.4 %all-to-all-start.4 = ((bf16[16,16,512]{2,1,0:T(8,128)(2,1)}), bf16[16,16,512]{2,1,0:T(8,128)(2,1)}, u32[]{:S(2)}, u32[]{:S(2)}) async-start(bf16[16,16,512]{2,1,0:T(8,128)(2,1)} %broadcast_in_dim.19), calls=%async_computation.4 | async-start | bytes 524288 | tf_op jit(solution)/shard_map/all_to_all | solution.py:37
  115.1 1.0 copy-start.7
  115.1 1.2 copy-start.8
  116.3 24.0 %copy-start.30 = (bf16[128,256]{1,0:T(8,128)(2,1)S(1)}, bf16[128,256]{1,0:T(8,128)(2,1)}, u32[]{:S(2)}) copy-start(bf16[128,256]{1,0:T(8,128)(2,1)} %copy-done.29) | copy-start | bytes 196612
  133.2 7.1 %copy-start.21 = (f32[256,256]{1,0:T(8,128)}, f32[256,256]{1,0:T(8,128)S(1)}, u32[]{:S(2)}) copy-start(f32[256,256]{1,0:T(8,128)S(1)} %fusion.57) | copy-start | bytes 786436
  133.9 16.6 %collective-permute-start.2 = (bf16[128,256]{1,0:T(8,128)(2,1)}, bf16[128,256]{1,0:T(8,128)(2,1)}, u32[]{:S(2)}, u32[]{:S(2)}) collective-permute-start(bf16[128,256]{1,0:T(8,128)(2,1)} %slice.497), channel_id=1, source_target_pairs={{0,64},{64,0},{1,65},{65,1},{2,66},{66,2},{3,67},{67,3},{4,68},{68... | collective-permute-start | bytes 196616 | tf_op jit(solution)/shard_map/ppermute | solution.py:54
  142.3 11.8 %copy-start.5 = (bf16[256,2048]{1,0:T(8,128)(2,1)S(1)}, bf16[256,2048]{1,0:T(8,128)(2,1)}, u32[]{:S(2)}) copy-start(bf16[256,2048]{1,0:T(8,128)(2,1)} %get-tuple-element.40) | copy-start | bytes 3145732
  142.3 9.4 %all-to-all-start.5 = ((bf16[4,128,256]{2,1,0:T(8,128)(2,1)}), bf16[4,128,256]{2,1,0:T(8,128)(2,1)S(1)}, u32[]{:S(2)}, u32[]{:S(2)}) async-start(bf16[4,128,256]{2,1,0:T(8,128)(2,1)} %bitcast.203), calls=%async_computation.5 | async-start | bytes 524288 | tf_op jit(solution)/shard_map/all_to_all | solution.py:37
  155.7 22.7 %all-to-all-start.6 = ((bf16[16,132,256]{2,1,0:T(8,128)(2,1)}), bf16[16,132,256]{2,1,0:T(8,128)(2,1)S(1)}, u32[]{:S(2)}, u32[]{:S(2)}) async-start(bf16[16,132,256]{2,1,0:T(8,128)(2,1)} %pad_maximum_fusion), calls=%async_computation.6 | async-start | bytes 2228224 | tf_op jit(solution)/shard_map/all_to_all | solution.py:37
  178.3 1.0 copy-start.4
  179.3 20.0 %all-to-all-start.7 = ((bf16[16,132,256]{2,1,0:T(8,128)(2,1)}), bf16[16,132,256]{2,1,0:T(8,128)(2,1)S(1)}, u32[]{:S(2)}, u32[]{:S(2)}) async-start(bf16[16,132,256]{2,1,0:T(8,128)(2,1)} %pad_maximum_fusion.1), calls=%async_computation.7 | async-start | bytes 2228224 | tf_op jit(solution)/shard_map/all_to_all | solution.py:37
  185.4 14.1 %collective-permute-start.3 = (bf16[144,256]{1,0:T(8,128)(2,1)S(1)}, bf16[144,256]{1,0:T(8,128)(2,1)S(1)}, u32[]{:S(2)}, u32[]{:S(2)}) collective-permute-start(bf16[144,256]{1,0:T(8,128)(2,1)S(1)} %maximum_maximum_fusion.2), channel_id=1, source_target_pairs={{0,64},{64,0},{1,65},{65,1},{2,66},{66,2},{3,67},{67,3},{4,68},{68... | collective-permute-start | bytes 221192 | tf_op jit(solution)/shard_map/ppermute | solution.py:54
  200.0 6.8 %collective-permute-start.4 = (bf16[2048,128]{1,0:T(8,128)(2,1)S(1)}, bf16[2048,128]{1,0:T(8,128)(2,1)S(1)}, u32[]{:S(2)}, u32[]{:S(2)}) collective-permute-start(bf16[2048,128]{1,0:T(8,128)(2,1)S(1)} %fusion.1), channel_id=1, source_target_pairs={{0,1},{1,0},{2,3},{3,2},{4,5},{5,4},{6,7},{7,6},{8,9},{9,8},{10,11... | collective-permute-start | bytes 1572872 | tf_op jit(solution)/shard_map/ppermute | solution.py:54
  207.2 10.3 %collective-permute-start.5 = (bf16[1024,128]{1,0:T(8,128)(2,1)S(1)}, bf16[1024,128]{1,0:T(8,128)(2,1)S(1)}, u32[]{:S(2)}, u32[]{:S(2)}) collective-permute-start(bf16[1024,128]{1,0:T(8,128)(2,1)S(1)} %slice.496), channel_id=1, source_target_pairs={{0,2},{2,0},{1,3},{3,1},{4,6},{6,4},{5,7},{7,5},{8,10},{10,8},{9,1... | collective-permute-start | bytes 786440 | tf_op jit(solution)/shard_map/ppermute | solution.py:54
  218.3 18.9 %all-to-all-start.8 = ((bf16[4,256,128]{2,1,0:T(8,128)(2,1)}), bf16[4,256,128]{2,1,0:T(8,128)(2,1)S(1)}, u32[]{:S(2)}, u32[]{:S(2)}) async-start(bf16[4,256,128]{2,1,0:T(8,128)(2,1)} %bitcast.199), calls=%async_computation.8 | async-start | bytes 524288 | tf_op jit(solution)/shard_map/all_to_all | solution.py:37
  237.3 6.5 %collective-permute-start.6 = (bf16[256,128]{1,0:T(8,128)(2,1)S(1)}, bf16[256,128]{1,0:T(8,128)(2,1)S(1)}, u32[]{:S(2)}, u32[]{:S(2)}) collective-permute-start(bf16[256,128]{1,0:T(8,128)(2,1)S(1)} %convert_element_type.233), channel_id=1, source_target_pairs={{0,0},{1,33},{2,66},{3,99},{4,132},{5,165},{6,198},{7,231},{8,264}... | collective-permute-start | bytes 196616 | tf_op jit(solution)/shard_map/ppermute | solution.py:223
  243.8 4.7 %collective-permute-start.7 = (bf16[128,128]{1,0:T(8,128)(2,1)S(1)}, bf16[128,128]{1,0:T(8,128)(2,1)S(1)}, u32[]{:S(2)}, u32[]{:S(2)}) collective-permute-start(bf16[128,128]{1,0:T(8,128)(2,1)S(1)} %get-tuple-element.95), channel_id=1, source_target_pairs={{0,16},{16,0},{32,48},{48,32},{1,17},{17,1},{33,49},{49,33},{2,18}... | collective-permute-start | bytes 98312 | tf_op jit(solution)/shard_map/ppermute | solution.py:54
  251.7 17.4 %all-to-all-start.9 = ((bf16[4,296,128]{2,1,0:T(8,128)(2,1)}), bf16[4,296,128]{2,1,0:T(8,128)(2,1)S(1)}, u32[]{:S(2)}, u32[]{:S(2)}) async-start(bf16[4,296,128]{2,1,0:T(8,128)(2,1)} %broadcast_in_dim.20), calls=%async_computation.9 | async-start | bytes 606208 | tf_op jit(solution)/shard_map/all_to_all | solution.py:37
  269.1 20.7 %collective-permute-start.8 = (bf16[4,296,128]{2,1,0:T(8,128)(2,1)S(1)}, bf16[4,296,128]{2,1,0:T(8,128)(2,1)S(1)}, u32[]{:S(2)}, u32[]{:S(2)}) collective-permute-start(bf16[4,296,128]{2,1,0:T(8,128)(2,1)S(1)} %all-to-all-done.9), channel_id=1, source_target_pairs={{0,1},{1,0},{2,3},{3,2},{4,5},{5,4},{6,7},{7,6},{8,9},{9,8},{10,11... | collective-permute-start | bytes 909320 | tf_op jit(solution)/shard_map/ppermute | solution.py:54
  274.5 21.4 %collective-permute-start.9 = (bf16[4,296,128]{2,1,0:T(8,128)(2,1)S(1)}, bf16[4,296,128]{2,1,0:T(8,128)(2,1)S(1)}, u32[]{:S(2)}, u32[]{:S(2)}) collective-permute-start(bf16[4,296,128]{2,1,0:T(8,128)(2,1)S(1)} %all-to-all-done.9), channel_id=1, source_target_pairs={{0,2},{2,0},{1,3},{3,1},{4,6},{6,4},{5,7},{7,5},{8,10},{10,8},{9,1... | collective-permute-start | bytes 909320 | tf_op jit(solution)/shard_map/ppermute | solution.py:54
  289.7 1.1 copy-start.6
  295.9 6.8 %copy-start.15 = (bf16[4,296,128]{2,1,0:T(8,128)(2,1)}, bf16[4,296,128]{2,1,0:T(8,128)(2,1)S(1)}, u32[]{:S(2)}) copy-start(bf16[4,296,128]{2,1,0:T(8,128)(2,1)S(1)} %collective-permute-done.9) | copy-start | bytes 909316
  295.9 3.7 %collective-permute-start.10 = (bf16[4,296,128]{2,1,0:T(8,128)(2,1)S(1)}, bf16[4,296,128]{2,1,0:T(8,128)(2,1)S(1)}, u32[]{:S(2)}, u32[]{:S(2)}) collective-permute-start(bf16[4,296,128]{2,1,0:T(8,128)(2,1)S(1)} %collective-permute-done.9), channel_id=1, source_target_pairs={{0,1},{1,0},{2,3},{3,2},{4,5},{5,4},{6,7},{7,6},{8,9},{9,8},{10,11... | collective-permute-start | bytes 909320 | tf_op jit(solution)/shard_map/ppermute | solution.py:54
  299.6 4.3 %copy-start.17 = (bf16[4,296,128]{2,1,0:T(8,128)(2,1)}, bf16[4,296,128]{2,1,0:T(8,128)(2,1)S(1)}, u32[]{:S(2)}) copy-start(bf16[4,296,128]{2,1,0:T(8,128)(2,1)S(1)} %collective-permute-done.10) | copy-start | bytes 909316
  303.9 28.5 %all-to-all-start.10 = ((bf16[16,152,256]{2,1,0:T(8,128)(2,1)}), bf16[16,152,256]{2,1,0:T(8,128)(2,1)S(1)}, u32[]{:S(2)}, u32[]{:S(2)}) async-start(bf16[16,152,256]{2,1,0:T(8,128)(2,1)} %broadcast_in_dim.21), calls=%async_computation.10 | async-start | bytes 2490368 | tf_op jit(solution)/shard_map/all_to_all | solution.py:37
  311.5 1.0 copy-start.16
  311.5 8.7 %copy-start.18 = (bf16[4,296,128]{2,1,0:T(8,128)(2,1)S(1)}, bf16[4,296,128]{2,1,0:T(8,128)(2,1)}, u32[]{:S(2)}) copy-start(bf16[4,296,128]{2,1,0:T(8,128)(2,1)} %copy-done.17) | copy-start | bytes 909316
  313.3 19.1 %collective-permute-start.11 = (bf16[152,256]{1,0:T(8,128)(2,1)S(1)}, bf16[152,256]{1,0:T(8,128)(2,1)S(1)}, u32[]{:S(2)}, u32[]{:S(2)}) collective-permute-start(bf16[152,256]{1,0:T(8,128)(2,1)S(1)} %maximum_maximum_fusion), channel_id=1, source_target_pairs={{0,64},{64,0},{1,65},{65,1},{2,66},{66,2},{3,67},{67,3},{4,68},{68... | collective-permute-start | bytes 233480 | tf_op jit(solution)/shard_map/ppermute | solution.py:54
  333.5 24.1 %all-to-all-start.11 = ((bf16[16,152,256]{2,1,0:T(8,128)(2,1)}), bf16[16,152,256]{2,1,0:T(8,128)(2,1)S(1)}, u32[]{:S(2)}, u32[]{:S(2)}) async-start(bf16[16,152,256]{2,1,0:T(8,128)(2,1)} %broadcast_in_dim.22), calls=%async_computation.11 | async-start | bytes 2490368 | tf_op jit(solution)/shard_map/all_to_all | solution.py:37
  340.2 1.3 copy-start.23
  340.2 1.3 copy-start.24
  340.2 1.3 copy-start.25
  340.2 1.3 copy-start.26
  343.5 14.3 %copy-start.14 = (f32[1,128,128]{2,1,0:T(8,128)S(1)}, f32[1,128,128]{2,1,0:T(8,128)}, u32[]{:S(2)}) copy-start(f32[1,128,128]{2,1,0:T(8,128)} %param.10) | copy-start | bytes 196612
  359.0 3.5 copy-start.9
  359.0 3.5 copy-start.27
  359.0 3.5 copy-start.28

commit v6 on v5

--- a/solution.py
+++ b/solution.py
@@ -163,7 +163,8 @@
         )
         for tokens, head in ((rows_own, weights_own), (rows_far, weights_far))
     )
-    part = mul(tokens, heads, second).astype(low)
+    part_far = mul(message, heads, second)[:ROWS]
+    part = jnp.concatenate([mul(rotated, heads, second).astype(low), part_far.astype(low)], 0)
     part = exchange(part.reshape(16, 16, 4 * HEAD), TENSOR)
     part, left_own, left_far, target_here = hold((part, left_own, left_far, target_here))
     values = added(part)

time: 368 us -> 369 us (level)
  waiting for transfers between devices: 136 us -> 141 us
    all_to_all x12, waiting for transfers between devices: 100 us -> 106 us  [exchange(): out = lax.all_to_all(flat, axes, split_axis=0, concat_axis=0, tiled=True)]
    dot_general x21 -> x22, matrix products: 17 us -> 15.7 us  [mul(): lax.dot_general(a, b, dims, precision=precision, preferred_element_type=j...]
    unnamed x70 -> x66, local copies, waits for them, and re-layouts: 7.35 us -> 7.48 us
where the time goes in v6:
time: 369 us; the launch traced here: 365 us
  starting transfers between devices  153 us (41%)
  waiting for transfers between devices  141 us (38%)
  local copies, waits for them, and re-layouts  23.8 us (6%)
  other arithmetic  23.4 us (6%)
  matrix products  17 us (5%)
  between operations  6.47 us (2%)
    all_to_all x12, waiting for transfers between devices, exchange(): out = lax.all_to_all(flat, axes, split_axis=0, concat_axis=0, tiled=True)  106 us
    ppermute x11, starting transfers between devices, swap(): return lax.ppermute(block, axis, [(i, i ^ bit) for i in range(n)])  78.3 us
    all_to_all x12, starting transfers between devices, exchange(): out = lax.all_to_all(flat, axes, split_axis=0, concat_axis=0, tiled=True)  71.8 us
    ppermute x11, waiting for transfers between devices, swap(): return lax.ppermute(block, axis, [(i, i ^ bit) for i in range(n)])  31.7 us
    dot_general x22, matrix products, mul(): lax.dot_general(a, b, dims, precision=precision, preferred_element_type=j...  15.7 us
    unnamed x66, local copies, waits for them, and re-layouts  7.48 us
  transfers between devices with their start and end apart: 24, of which 18 were waited for; matrix products, arithmetic and copies ran while one was open for 9% of the time, Pallas kernels for 0%

profile of v6, /device:TPU:1, one launch (start us, length us, event | category | flops | bytes accessed | tf_op | source)
XLA Modules:
  0.0 365.0 jit_solution(5450691192520798058)
XLA Ops:
  1.5 1.1 broadcast_in_dim.16
  2.6 7.7 %all-to-all-start = ((bf16[16,128,256]{2,1,0:T(8,128)(2,1)}), bf16[16,128,256]{2,1,0:T(8,128)(2,1)S(1)}, u32[]{:S(2)}, u32[]{:S(2)}) async-start(bf16[16,128,256]{2,1,0:T(8,128)(2,1)} %broadcast_in_dim.16), calls=%async_computation | async-start | bytes 2097152 | tf_op jit(solution)/shard_map/all_to_all | solution.py:37
  10.4 15.6 %collective-permute-start = (bf16[128,256]{1,0:T(8,128)(2,1)S(1)}, bf16[128,256]{1,0:T(8,128)(2,1)S(1)}, u32[]{:S(2)}, u32[]{:S(2)}) collective-permute-start(bf16[128,256]{1,0:T(8,128)(2,1)S(1)} %convert_element_type.203), channel_id=1, source_target_pairs={{0,64},{64,0},{1,65},{65,1},{2,66},{66,2},{3,67},{67,3},{4,68},{68... | collective-permute-start | bytes 196616 | tf_op jit(solution)/shard_map/ppermute | solution.py:54
  27.2 1.5 fusion.50
  31.4 1.1 broadcast_in_dim.17
  32.4 6.7 %all-to-all-start.1 = ((bf16[16,128,256]{2,1,0:T(8,128)(2,1)}), bf16[16,128,256]{2,1,0:T(8,128)(2,1)S(1)}, u32[]{:S(2)}, u32[]{:S(2)}) async-start(bf16[16,128,256]{2,1,0:T(8,128)(2,1)} %broadcast_in_dim.17), calls=%async_computation.1 | async-start | bytes 2097152 | tf_op jit(solution)/shard_map/all_to_all | solution.py:37
  41.3 12.8 %all-to-all-done.1 = bf16[16,128,256]{2,1,0:T(8,128)(2,1)S(1)} async-done(((bf16[16,128,256]{2,1,0:T(8,128)(2,1)}), bf16[16,128,256]{2,1,0:T(8,128)(2,1)S(1)}, u32[]{:S(2)}, u32[]{:S(2)}) %all-to-all-start.1) | async-done | bytes 1048608 | tf_op jit(solution)/shard_map/all_to_all | solution.py:37
  54.3 1.1 fusion.49
  57.7 6.4 %collective-permute-start.1 = (bf16[160,256]{1,0:T(8,128)(2,1)}, bf16[160,256]{1,0:T(8,128)(2,1)S(1)}, u32[]{:S(2)}, u32[]{:S(2)}) collective-permute-start(bf16[160,256]{1,0:T(8,128)(2,1)} %pad_maximum_fusion.10), channel_id=1, source_target_pairs={{0,64},{64,0},{1,65},{65,1},{2,66},{66,2},{3,67},{67,3},{4,68},{68... | collective-permute-start | bytes 245768 | tf_op jit(solution)/shard_map/ppermute | solution.py:54
  64.5 1.0 multiply_convert_fusion
  66.2 3.4 all-to-all-start.2
  70.2 5.2 %all-to-all-done.2 = bf16[4,128,256]{2,1,0:T(8,128)(2,1)S(1)} async-done(((bf16[4,128,256]{2,1,0:T(8,128)(2,1)}), bf16[4,128,256]{2,1,0:T(8,128)(2,1)S(1)}, u32[]{:S(2)}, u32[]{:S(2)}) %all-to-all-start.2) | async-done | bytes 262176 | tf_op jit(solution)/shard_map/all_to_all | solution.py:37
  77.3 14.3 %all-to-all-start.3 = ((bf16[16,16,512]{2,1,0:T(8,128)(2,1)}), bf16[16,16,512]{2,1,0:T(8,128)(2,1)}, u32[]{:S(2)}, u32[]{:S(2)}) async-start(bf16[16,16,512]{2,1,0:T(8,128)(2,1)} %bitcast.203), calls=%async_computation.3 | async-start | bytes 524288 | tf_op jit(solution)/shard_map/all_to_all | solution.py:37
  92.3 1.5 pad_maximum_fusion.2
  94.5 14.2 %all-to-all-done.3 = bf16[16,16,512]{2,1,0:T(8,128)(2,1)} async-done(((bf16[16,16,512]{2,1,0:T(8,128)(2,1)}), bf16[16,16,512]{2,1,0:T(8,128)(2,1)}, u32[]{:S(2)}, u32[]{:S(2)}) %all-to-all-start.3) | async-done | bytes 262176 | tf_op jit(solution)/shard_map/all_to_all | solution.py:37
  108.7 1.0 convert_reduce_fusion.3
  110.4 5.3 %all-to-all-start.4 = ((bf16[16,16,512]{2,1,0:T(8,128)(2,1)}), bf16[16,16,512]{2,1,0:T(8,128)(2,1)}, u32[]{:S(2)}, u32[]{:S(2)}) async-start(bf16[16,16,512]{2,1,0:T(8,128)(2,1)} %broadcast_in_dim.19), calls=%async_computation.4 | async-start | bytes 524288 | tf_op jit(solution)/shard_map/all_to_all | solution.py:37
  116.1 0.9 copy-done.7
  117.6 15.3 %all-to-all-done.4 = bf16[16,16,512]{2,1,0:T(8,128)(2,1)} async-done(((bf16[16,16,512]{2,1,0:T(8,128)(2,1)}), bf16[16,16,512]{2,1,0:T(8,128)(2,1)}, u32[]{:S(2)}, u32[]{:S(2)}) %all-to-all-start.4) | async-done | bytes 262176 | tf_op jit(solution)/shard_map/all_to_all | solution.py:37
  132.8 1.2 fusion.60
  134.7 6.4 %collective-permute-start.2 = (bf16[128,256]{1,0:T(8,128)(2,1)}, bf16[128,256]{1,0:T(8,128)(2,1)}, u32[]{:S(2)}, u32[]{:S(2)}) collective-permute-start(bf16[128,256]{1,0:T(8,128)(2,1)} %slice.505), channel_id=1, source_target_pairs={{0,64},{64,0},{1,65},{65,1},{2,66},{66,2},{3,67},{67,3},{4,68},{68... | collective-permute-start | bytes 196616 | tf_op jit(solution)/shard_map/ppermute | solution.py:54
  141.2 1.9 convolution_convert_fusion.4
  143.1 3.5 all-to-all-start.5
  146.6 4.6 %collective-permute-done.2 = bf16[128,256]{1,0:T(8,128)(2,1)} collective-permute-done((bf16[128,256]{1,0:T(8,128)(2,1)}, bf16[128,256]{1,0:T(8,128)(2,1)}, u32[]{:S(2)}, u32[]{:S(2)}) %collective-permute-start.2) | collective-permute-done | bytes 65568 | tf_op jit(solution)/shard_map/ppermute | solution.py:54
  152.5 1.2 fusion.55
  153.8 0.9 fusion.27
  155.4 1.1 pad_maximum_fusion
  156.5 3.7 %all-to-all-start.6 = ((bf16[16,132,256]{2,1,0:T(8,128)(2,1)}), bf16[16,132,256]{2,1,0:T(8,128)(2,1)S(1)}, u32[]{:S(2)}, u32[]{:S(2)}) async-start(bf16[16,132,256]{2,1,0:T(8,128)(2,1)} %pad_maximum_fusion), calls=%async_computation.6 | async-start | bytes 2228224 | tf_op jit(solution)/shard_map/all_to_all | solution.py:37
  160.3 1.7 convolution_convert_fusion
  162.0 1.1 pad_maximum_fusion.1
  163.1 16.0 %all-to-all-done.6 = bf16[16,132,256]{2,1,0:T(8,128)(2,1)S(1)} async-done(((bf16[16,132,256]{2,1,0:T(8,128)(2,1)}), bf16[16,132,256]{2,1,0:T(8,128)(2,1)S(1)}, u32[]{:S(2)}, u32[]{:S(2)}) %all-to-all-start.6) | async-done | bytes 1081376 | tf_op jit(solution)/shard_map/all_to_all | solution.py:37
  179.1 1.0 copy-done.4
  180.1 3.8 %all-to-all-start.7 = ((bf16[16,132,256]{2,1,0:T(8,128)(2,1)}), bf16[16,132,256]{2,1,0:T(8,128)(2,1)S(1)}, u32[]{:S(2)}, u32[]{:S(2)}) async-start(bf16[16,132,256]{2,1,0:T(8,128)(2,1)} %pad_maximum_fusion.1), calls=%async_computation.7 | async-start | bytes 2228224 | tf_op jit(solution)/shard_map/all_to_all | solution.py:37
  184.8 1.4 slice_reduce_fusion
  186.2 7.7 %collective-permute-start.3 = (bf16[144,256]{1,0:T(8,128)(2,1)S(1)}, bf16[144,256]{1,0:T(8,128)(2,1)S(1)}, u32[]{:S(2)}, u32[]{:S(2)}) collective-permute-start(bf16[144,256]{1,0:T(8,128)(2,1)S(1)} %maximum_maximum_fusion.2), channel_id=1, source_target_pairs={{0,64},{64,0},{1,65},{65,1},{2,66},{66,2},{3,67},{67,3},{4,68},{68... | collective-permute-start | bytes 221192 | tf_op jit(solution)/shard_map/ppermute | solution.py:54
  193.9 6.2 %all-to-all-done.7 = bf16[16,132,256]{2,1,0:T(8,128)(2,1)S(1)} async-done(((bf16[16,132,256]{2,1,0:T(8,128)(2,1)}), bf16[16,132,256]{2,1,0:T(8,128)(2,1)S(1)}, u32[]{:S(2)}, u32[]{:S(2)}) %all-to-all-start.7) | async-done | bytes 1081376 | tf_op jit(solution)/shard_map/all_to_all | solution.py:37
  200.8 5.2 %collective-permute-start.4 = (bf16[2048,128]{1,0:T(8,128)(2,1)S(1)}, bf16[2048,128]{1,0:T(8,128)(2,1)S(1)}, u32[]{:S(2)}, u32[]{:S(2)}) collective-permute-start(bf16[2048,128]{1,0:T(8,128)(2,1)S(1)} %fusion.1), channel_id=1, source_target_pairs={{0,1},{1,0},{2,3},{3,2},{4,5},{5,4},{6,7},{7,6},{8,9},{9,8},{10,11... | collective-permute-start | bytes 1572872 | tf_op jit(solution)/shard_map/ppermute | solution.py:54
  206.0 1.5 collective-permute-done.4
  208.0 4.0 %collective-permute-start.5 = (bf16[1024,128]{1,0:T(8,128)(2,1)S(1)}, bf16[1024,128]{1,0:T(8,128)(2,1)S(1)}, u32[]{:S(2)}, u32[]{:S(2)}) collective-permute-start(bf16[1024,128]{1,0:T(8,128)(2,1)S(1)} %slice.503), channel_id=1, source_target_pairs={{0,2},{2,0},{1,3},{3,1},{4,6},{6,4},{5,7},{7,5},{8,10},{10,8},{9,1... | collective-permute-start | bytes 786440 | tf_op jit(solution)/shard_map/ppermute | solution.py:54
  212.0 6.4 %collective-permute-done.5 = bf16[1024,128]{1,0:T(8,128)(2,1)S(1)} collective-permute-done((bf16[1024,128]{1,0:T(8,128)(2,1)S(1)}, bf16[1024,128]{1,0:T(8,128)(2,1)S(1)}, u32[]{:S(2)}, u32[]{:S(2)}) %collective-permute-start.5) | collective-permute-done | bytes 262176 | tf_op jit(solution)/shard_map/ppermute | solution.py:54
  219.1 5.2 %all-to-all-start.8 = ((bf16[4,256,128]{2,1,0:T(8,128)(2,1)}), bf16[4,256,128]{2,1,0:T(8,128)(2,1)S(1)}, u32[]{:S(2)}, u32[]{:S(2)}) async-start(bf16[4,256,128]{2,1,0:T(8,128)(2,1)} %bitcast.204), calls=%async_computation.8 | async-start | bytes 524288 | tf_op jit(solution)/shard_map/all_to_all | solution.py:37
  224.9 14.9 %all-to-all-done.8 = bf16[4,256,128]{2,1,0:T(8,128)(2,1)S(1)} async-done(((bf16[4,256,128]{2,1,0:T(8,128)(2,1)}), bf16[4,256,128]{2,1,0:T(8,128)(2,1)S(1)}, u32[]{:S(2)}, u32[]{:S(2)}) %all-to-all-start.8) | async-done | bytes 262176 | tf_op jit(solution)/shard_map/all_to_all | solution.py:37
  240.0 3.0 collective-permute-start.6
  243.0 3.5 collective-permute-done.6
  246.5 1.9 collective-permute-start.7
  249.1 2.0 collective-permute-done.7
  254.3 5.8 %all-to-all-start.9 = ((bf16[4,296,128]{2,1,0:T(8,128)(2,1)}), bf16[4,296,128]{2,1,0:T(8,128)(2,1)S(1)}, u32[]{:S(2)}, u32[]{:S(2)}) async-start(bf16[4,296,128]{2,1,0:T(8,128)(2,1)} %broadcast_in_dim.20), calls=%async_computation.9 | async-start | bytes 606208 | tf_op jit(solution)/shard_map/all_to_all | solution.py:37
  261.9 7.4 %all-to-all-done.9 = bf16[4,296,128]{2,1,0:T(8,128)(2,1)S(1)} async-done(((bf16[4,296,128]{2,1,0:T(8,128)(2,1)}), bf16[4,296,128]{2,1,0:T(8,128)(2,1)S(1)}, u32[]{:S(2)}, u32[]{:S(2)}) %all-to-all-start.9) | async-done | bytes 303136 | tf_op jit(solution)/shard_map/all_to_all | solution.py:37
  269.3 5.7 %collective-permute-start.8 = (bf16[4,296,128]{2,1,0:T(8,128)(2,1)S(1)}, bf16[4,296,128]{2,1,0:T(8,128)(2,1)S(1)}, u32[]{:S(2)}, u32[]{:S(2)}) collective-permute-start(bf16[4,296,128]{2,1,0:T(8,128)(2,1)S(1)} %all-to-all-done.9), channel_id=1, source_target_pairs={{0,1},{1,0},{2,3},{3,2},{4,5},{5,4},{6,7},{7,6},{8,9},{9,8},{10,11... | collective-permute-start | bytes 909320 | tf_op jit(solution)/shard_map/ppermute | solution.py:54
  275.1 16.9 %collective-permute-start.9 = (bf16[4,296,128]{2,1,0:T(8,128)(2,1)S(1)}, bf16[4,296,128]{2,1,0:T(8,128)(2,1)S(1)}, u32[]{:S(2)}, u32[]{:S(2)}) collective-permute-start(bf16[4,296,128]{2,1,0:T(8,128)(2,1)S(1)} %all-to-all-done.9), channel_id=1, source_target_pairs={{0,2},{2,0},{1,3},{3,1},{4,6},{6,4},{5,7},{7,5},{8,10},{10,8},{9,1... | collective-permute-start | bytes 909320 | tf_op jit(solution)/shard_map/ppermute | solution.py:54
  292.0 1.4 fusion.61
  294.8 4.8 %collective-permute-done.9 = bf16[4,296,128]{2,1,0:T(8,128)(2,1)S(1)} collective-permute-done((bf16[4,296,128]{2,1,0:T(8,128)(2,1)S(1)}, bf16[4,296,128]{2,1,0:T(8,128)(2,1)S(1)}, u32[]{:S(2)}, u32[]{:S(2)}) %collective-permute-start.9) | collective-permute-done | bytes 303136 | tf_op jit(solution)/shard_map/ppermute | solution.py:54
  299.6 2.5 collective-permute-start.10
  305.4 1.0 fusion.56
  306.4 1.2 broadcast_in_dim.21
  307.6 5.6 %all-to-all-start.10 = ((bf16[16,152,256]{2,1,0:T(8,128)(2,1)}), bf16[16,152,256]{2,1,0:T(8,128)(2,1)S(1)}, u32[]{:S(2)}, u32[]{:S(2)}) async-start(bf16[16,152,256]{2,1,0:T(8,128)(2,1)} %broadcast_in_dim.21), calls=%async_computation.10 | async-start | bytes 2490368 | tf_op jit(solution)/shard_map/all_to_all | solution.py:37
  315.1 5.9 %collective-permute-start.11 = (bf16[152,256]{1,0:T(8,128)(2,1)S(1)}, bf16[152,256]{1,0:T(8,128)(2,1)S(1)}, u32[]{:S(2)}, u32[]{:S(2)}) collective-permute-start(bf16[152,256]{1,0:T(8,128)(2,1)S(1)} %maximum_maximum_fusion), channel_id=1, source_target_pairs={{0,64},{64,0},{1,65},{65,1},{2,66},{66,2},{3,67},{67,3},{4,68},{68... | collective-permute-start | bytes 233480 | tf_op jit(solution)/shard_map/ppermute | solution.py:54
  322.0 11.5 %collective-permute-done.11 = bf16[152,256]{1,0:T(8,128)(2,1)S(1)} collective-permute-done((bf16[152,256]{1,0:T(8,128)(2,1)S(1)}, bf16[152,256]{1,0:T(8,128)(2,1)S(1)}, u32[]{:S(2)}, u32[]{:S(2)}) %collective-permute-start.11) | collective-permute-done | bytes 77856 | tf_op jit(solution)/shard_map/ppermute | solution.py:54
  333.5 1.2 broadcast_in_dim.22
  334.6 6.8 %all-to-all-start.11 = ((bf16[16,152,256]{2,1,0:T(8,128)(2,1)}), bf16[16,152,256]{2,1,0:T(8,128)(2,1)S(1)}, u32[]{:S(2)}, u32[]{:S(2)}) async-start(bf16[16,152,256]{2,1,0:T(8,128)(2,1)} %broadcast_in_dim.22), calls=%async_computation.11 | async-start | bytes 2490368 | tf_op jit(solution)/shard_map/all_to_all | solution.py:37
  341.5 1.2 maximum_select_fusion.9
  342.8 1.2 broadcast_select_fusion
  345.1 13.8 %all-to-all-done.11 = bf16[16,152,256]{2,1,0:T(8,128)(2,1)S(1)} async-done(((bf16[16,152,256]{2,1,0:T(8,128)(2,1)}), bf16[16,152,256]{2,1,0:T(8,128)(2,1)S(1)}, u32[]{:S(2)}, u32[]{:S(2)}) %all-to-all-start.11) | async-done | bytes 1245216 | tf_op jit(solution)/shard_map/all_to_all | solution.py:37
  364.0 1.0 subtract_add_fusion
  (191 shorter events, 36.6 us)
Async XLA Ops:
  2.6 23.4 %copy-start.29 = (bf16[1,128,1024]{2,1,0:T(8,128)(2,1)S(1)}, bf16[1,128,1024]{2,1,0:T(8,128)(2,1)}, u32[]{:S(2)}) copy-start(bf16[1,128,1024]{2,1,0:T(8,128)(2,1)} %param.7) | copy-start | bytes 786436
  2.6 28.7 %all-to-all-start = ((bf16[16,128,256]{2,1,0:T(8,128)(2,1)}), bf16[16,128,256]{2,1,0:T(8,128)(2,1)S(1)}, u32[]{:S(2)}, u32[]{:S(2)}) async-start(bf16[16,128,256]{2,1,0:T(8,128)(2,1)} %broadcast_in_dim.16), calls=%async_computation | async-start | bytes 2097152 | tf_op jit(solution)/shard_map/all_to_all | solution.py:37
  10.4 16.1 %copy-start.19 = (bf16[1,128,4096]{2,1,0:T(8,128)(2,1)S(1)}, bf16[1,128,4096]{2,1,0:T(8,128)(2,1)}, u32[]{:S(2)}) copy-start(bf16[1,128,4096]{2,1,0:T(8,128)(2,1)} %param.6) | copy-start | bytes 3145732
  10.4 21.0 %collective-permute-start = (bf16[128,256]{1,0:T(8,128)(2,1)S(1)}, bf16[128,256]{1,0:T(8,128)(2,1)S(1)}, u32[]{:S(2)}, u32[]{:S(2)}) collective-permute-start(bf16[128,256]{1,0:T(8,128)(2,1)S(1)} %convert_element_type.203), channel_id=1, source_target_pairs={{0,64},{64,0},{1,65},{65,1},{2,66},{66,2},{3,67},{67,3},{4,68},{68... | collective-permute-start | bytes 196616 | tf_op jit(solution)/shard_map/ppermute | solution.py:54
  29.3 1.8 copy-start.18
  32.4 21.7 %all-to-all-start.1 = ((bf16[16,128,256]{2,1,0:T(8,128)(2,1)}), bf16[16,128,256]{2,1,0:T(8,128)(2,1)S(1)}, u32[]{:S(2)}, u32[]{:S(2)}) async-start(bf16[16,128,256]{2,1,0:T(8,128)(2,1)} %broadcast_in_dim.17), calls=%async_computation.1 | async-start | bytes 2097152 | tf_op jit(solution)/shard_map/all_to_all | solution.py:37
  54.2 1.2 copy-start.2
  55.3 1.1 copy-start
  57.7 6.8 %copy-start.12 = (f32[1,128,128]{2,1,0:T(8,128)S(1)}, f32[1,128,128]{2,1,0:T(8,128)}, u32[]{:S(2)}) copy-start(f32[1,128,128]{2,1,0:T(8,128)} %param.10) | copy-start | bytes 196612
  57.7 6.8 %copy-start.30 = (f32[1,128]{1,0:T(1,128)S(1)}, f32[1,128]{1,0:T(1,128)}, u32[]{:S(2)}) copy-start(f32[1,128]{1,0:T(1,128)} %param.9) | copy-start | bytes 1540
  57.7 17.9 %collective-permute-start.1 = (bf16[160,256]{1,0:T(8,128)(2,1)}, bf16[160,256]{1,0:T(8,128)(2,1)S(1)}, u32[]{:S(2)}, u32[]{:S(2)}) collective-permute-start(bf16[160,256]{1,0:T(8,128)(2,1)} %pad_maximum_fusion.10), channel_id=1, source_target_pairs={{0,64},{64,0},{1,65},{65,1},{2,66},{66,2},{3,67},{67,3},{4,68},{68... | collective-permute-start | bytes 245768 | tf_op jit(solution)/shard_map/ppermute | solution.py:54
  64.4 1.7 copy-start.21
  66.2 9.2 %all-to-all-start.2 = ((bf16[4,128,256]{2,1,0:T(8,128)(2,1)}), bf16[4,128,256]{2,1,0:T(8,128)(2,1)S(1)}, u32[]{:S(2)}, u32[]{:S(2)}) async-start(bf16[4,128,256]{2,1,0:T(8,128)(2,1)} %broadcast_in_dim.18), calls=%async_computation.2 | async-start | bytes 524288 | tf_op jit(solution)/shard_map/all_to_all | solution.py:37
  75.6 0.6 copy-start.28
  76.5 15.7 %copy-start.1 = (bf16[16,8,4,512]{3,1,2,0:T(8,128)(2,1)S(1)}, bf16[16,8,4,512]{3,1,2,0:T(8,128)(2,1)}, u32[]{:S(2)}) copy-start(bf16[16,8,4,512]{3,1,2,0:T(8,128)(2,1)} %copy.120) | copy-start | bytes 1572868
  76.5 15.7 %copy-start.3 = (bf16[16,8,4,512]{3,1,2,0:T(8,128)(2,1)S(1)}, bf16[16,8,4,512]{3,1,2,0:T(8,128)(2,1)}, u32[]{:S(2)}) copy-start(bf16[16,8,4,512]{3,1,2,0:T(8,128)(2,1)} %copy.119) | copy-start | bytes 1572868
  77.3 31.4 %all-to-all-start.3 = ((bf16[16,16,512]{2,1,0:T(8,128)(2,1)}), bf16[16,16,512]{2,1,0:T(8,128)(2,1)}, u32[]{:S(2)}, u32[]{:S(2)}) async-start(bf16[16,16,512]{2,1,0:T(8,128)(2,1)} %bitcast.203), calls=%async_computation.3 | async-start | bytes 524288 | tf_op jit(solution)/shard_map/all_to_all | solution.py:37
  92.2 1.5 copy-start.10
  92.2 1.5 copy-start.11
  93.8 0.7 slice-start
  110.4 22.4 %all-to-all-start.4 = ((bf16[16,16,512]{2,1,0:T(8,128)(2,1)}), bf16[16,16,512]{2,1,0:T(8,128)(2,1)}, u32[]{:S(2)}, u32[]{:S(2)}) async-start(bf16[16,16,512]{2,1,0:T(8,128)(2,1)} %broadcast_in_dim.19), calls=%async_computation.4 | async-start | bytes 524288 | tf_op jit(solution)/shard_map/all_to_all | solution.py:37
  116.0 1.0 copy-start.7
  116.0 1.2 copy-start.8
  117.2 24.0 %slice-start.1 = ((bf16[160,256]{1,0:T(8,128)(2,1)}), bf16[128,256]{1,0:T(8,128)(2,1)S(1)}, s32[]{:S(2)}) async-start(bf16[160,256]{1,0:T(8,128)(2,1)} %copy-done.28), calls=%async_computation.13 | async-start | bytes 131072 | tf_op jit(solution)/shard_map/slice | solution.py:152
  134.0 7.2 %copy-start.20 = (f32[256,256]{1,0:T(8,128)}, f32[256,256]{1,0:T(8,128)S(1)}, u32[]{:S(2)}) copy-start(f32[256,256]{1,0:T(8,128)S(1)} %fusion.60) | copy-start | bytes 786436
  134.7 16.6 %collective-permute-start.2 = (bf16[128,256]{1,0:T(8,128)(2,1)}, bf16[128,256]{1,0:T(8,128)(2,1)}, u32[]{:S(2)}, u32[]{:S(2)}) collective-permute-start(bf16[128,256]{1,0:T(8,128)(2,1)} %slice.505), channel_id=1, source_target_pairs={{0,64},{64,0},{1,65},{65,1},{2,66},{66,2},{3,67},{67,3},{4,68},{68... | collective-permute-start | bytes 196616 | tf_op jit(solution)/shard_map/ppermute | solution.py:54
  143.1 11.8 %copy-start.5 = (bf16[256,2048]{1,0:T(8,128)(2,1)S(1)}, bf16[256,2048]{1,0:T(8,128)(2,1)}, u32[]{:S(2)}) copy-start(bf16[256,2048]{1,0:T(8,128)(2,1)} %get-tuple-element.40) | copy-start | bytes 3145732
  143.1 9.4 %all-to-all-start.5 = ((bf16[4,128,256]{2,1,0:T(8,128)(2,1)}), bf16[4,128,256]{2,1,0:T(8,128)(2,1)S(1)}, u32[]{:S(2)}, u32[]{:S(2)}) async-start(bf16[4,128,256]{2,1,0:T(8,128)(2,1)} %bitcast.208), calls=%async_computation.5 | async-start | bytes 524288 | tf_op jit(solution)/shard_map/all_to_all | solution.py:37
  156.5 22.6 %all-to-all-start.6 = ((bf16[16,132,256]{2,1,0:T(8,128)(2,1)}), bf16[16,132,256]{2,1,0:T(8,128)(2,1)S(1)}, u32[]{:S(2)}, u32[]{:S(2)}) async-start(bf16[16,132,256]{2,1,0:T(8,128)(2,1)} %pad_maximum_fusion), calls=%async_computation.6 | async-start | bytes 2228224 | tf_op jit(solution)/shard_map/all_to_all | solution.py:37
  179.1 1.0 copy-start.4
  180.1 20.1 %all-to-all-start.7 = ((bf16[16,132,256]{2,1,0:T(8,128)(2,1)}), bf16[16,132,256]{2,1,0:T(8,128)(2,1)S(1)}, u32[]{:S(2)}, u32[]{:S(2)}) async-start(bf16[16,132,256]{2,1,0:T(8,128)(2,1)} %pad_maximum_fusion.1), calls=%async_computation.7 | async-start | bytes 2228224 | tf_op jit(solution)/shard_map/all_to_all | solution.py:37
  186.2 14.1 %collective-permute-start.3 = (bf16[144,256]{1,0:T(8,128)(2,1)S(1)}, bf16[144,256]{1,0:T(8,128)(2,1)S(1)}, u32[]{:S(2)}, u32[]{:S(2)}) collective-permute-start(bf16[144,256]{1,0:T(8,128)(2,1)S(1)} %maximum_maximum_fusion.2), channel_id=1, source_target_pairs={{0,64},{64,0},{1,65},{65,1},{2,66},{66,2},{3,67},{67,3},{4,68},{68... | collective-permute-start | bytes 221192 | tf_op jit(solution)/shard_map/ppermute | solution.py:54
  200.8 6.7 %collective-permute-start.4 = (bf16[2048,128]{1,0:T(8,128)(2,1)S(1)}, bf16[2048,128]{1,0:T(8,128)(2,1)S(1)}, u32[]{:S(2)}, u32[]{:S(2)}) collective-permute-start(bf16[2048,128]{1,0:T(8,128)(2,1)S(1)} %fusion.1), channel_id=1, source_target_pairs={{0,1},{1,0},{2,3},{3,2},{4,5},{5,4},{6,7},{7,6},{8,9},{9,8},{10,11... | collective-permute-start | bytes 1572872 | tf_op jit(solution)/shard_map/ppermute | solution.py:54
  208.0 10.3 %collective-permute-start.5 = (bf16[1024,128]{1,0:T(8,128)(2,1)S(1)}, bf16[1024,128]{1,0:T(8,128)(2,1)S(1)}, u32[]{:S(2)}, u32[]{:S(2)}) collective-permute-start(bf16[1024,128]{1,0:T(8,128)(2,1)S(1)} %slice.503), channel_id=1, source_target_pairs={{0,2},{2,0},{1,3},{3,1},{4,6},{6,4},{5,7},{7,5},{8,10},{10,8},{9,1... | collective-permute-start | bytes 786440 | tf_op jit(solution)/shard_map/ppermute | solution.py:54
  219.1 20.8 %all-to-all-start.8 = ((bf16[4,256,128]{2,1,0:T(8,128)(2,1)}), bf16[4,256,128]{2,1,0:T(8,128)(2,1)S(1)}, u32[]{:S(2)}, u32[]{:S(2)}) async-start(bf16[4,256,128]{2,1,0:T(8,128)(2,1)} %bitcast.204), calls=%async_computation.8 | async-start | bytes 524288 | tf_op jit(solution)/shard_map/all_to_all | solution.py:37
  240.0 6.5 %collective-permute-start.6 = (bf16[256,128]{1,0:T(8,128)(2,1)S(1)}, bf16[256,128]{1,0:T(8,128)(2,1)S(1)}, u32[]{:S(2)}, u32[]{:S(2)}) collective-permute-start(bf16[256,128]{1,0:T(8,128)(2,1)S(1)} %convert_element_type.234), channel_id=1, source_target_pairs={{0,0},{1,33},{2,66},{3,99},{4,132},{5,165},{6,198},{7,231},{8,264}... | collective-permute-start | bytes 196616 | tf_op jit(solution)/shard_map/ppermute | solution.py:224
  246.5 4.7 %collective-permute-start.7 = (bf16[128,128]{1,0:T(8,128)(2,1)S(1)}, bf16[128,128]{1,0:T(8,128)(2,1)S(1)}, u32[]{:S(2)}, u32[]{:S(2)}) collective-permute-start(bf16[128,128]{1,0:T(8,128)(2,1)S(1)} %get-tuple-element.95), channel_id=1, source_target_pairs={{0,16},{16,0},{32,48},{48,32},{1,17},{17,1},{33,49},{49,33},{2,18}... | collective-permute-start | bytes 98312 | tf_op jit(solution)/shard_map/ppermute | solution.py:54
  254.3 15.0 %all-to-all-start.9 = ((bf16[4,296,128]{2,1,0:T(8,128)(2,1)}), bf16[4,296,128]{2,1,0:T(8,128)(2,1)S(1)}, u32[]{:S(2)}, u32[]{:S(2)}) async-start(bf16[4,296,128]{2,1,0:T(8,128)(2,1)} %broadcast_in_dim.20), calls=%async_computation.9 | async-start | bytes 606208 | tf_op jit(solution)/shard_map/all_to_all | solution.py:37
  269.3 24.1 %collective-permute-start.8 = (bf16[4,296,128]{2,1,0:T(8,128)(2,1)S(1)}, bf16[4,296,128]{2,1,0:T(8,128)(2,1)S(1)}, u32[]{:S(2)}, u32[]{:S(2)}) collective-permute-start(bf16[4,296,128]{2,1,0:T(8,128)(2,1)S(1)} %all-to-all-done.9), channel_id=1, source_target_pairs={{0,1},{1,0},{2,3},{3,2},{4,5},{5,4},{6,7},{7,6},{8,9},{9,8},{10,11... | collective-permute-start | bytes 909320 | tf_op jit(solution)/shard_map/ppermute | solution.py:54
  275.1 24.5 %collective-permute-start.9 = (bf16[4,296,128]{2,1,0:T(8,128)(2,1)S(1)}, bf16[4,296,128]{2,1,0:T(8,128)(2,1)S(1)}, u32[]{:S(2)}, u32[]{:S(2)}) collective-permute-start(bf16[4,296,128]{2,1,0:T(8,128)(2,1)S(1)} %all-to-all-done.9), channel_id=1, source_target_pairs={{0,2},{2,0},{1,3},{3,1},{4,6},{6,4},{5,7},{7,5},{8,10},{10,8},{9,1... | collective-permute-start | bytes 909320 | tf_op jit(solution)/shard_map/ppermute | solution.py:54
  293.4 1.1 copy-start.6
  299.6 6.8 %copy-start.14 = (bf16[4,296,128]{2,1,0:T(8,128)(2,1)}, bf16[4,296,128]{2,1,0:T(8,128)(2,1)S(1)}, u32[]{:S(2)}) copy-start(bf16[4,296,128]{2,1,0:T(8,128)(2,1)S(1)} %collective-permute-done.9) | copy-start | bytes 909316
  299.6 3.7 %collective-permute-start.10 = (bf16[4,296,128]{2,1,0:T(8,128)(2,1)S(1)}, bf16[4,296,128]{2,1,0:T(8,128)(2,1)S(1)}, u32[]{:S(2)}, u32[]{:S(2)}) collective-permute-start(bf16[4,296,128]{2,1,0:T(8,128)(2,1)S(1)} %collective-permute-done.9), channel_id=1, source_target_pairs={{0,1},{1,0},{2,3},{3,2},{4,5},{5,4},{6,7},{7,6},{8,9},{9,8},{10,11... | collective-permute-start | bytes 909320 | tf_op jit(solution)/shard_map/ppermute | solution.py:54
  303.3 4.3 %copy-start.16 = (bf16[4,296,128]{2,1,0:T(8,128)(2,1)}, bf16[4,296,128]{2,1,0:T(8,128)(2,1)S(1)}, u32[]{:S(2)}) copy-start(bf16[4,296,128]{2,1,0:T(8,128)(2,1)S(1)} %collective-permute-done.10) | copy-start | bytes 909316
  307.6 25.8 %all-to-all-start.10 = ((bf16[16,152,256]{2,1,0:T(8,128)(2,1)}), bf16[16,152,256]{2,1,0:T(8,128)(2,1)S(1)}, u32[]{:S(2)}, u32[]{:S(2)}) async-start(bf16[16,152,256]{2,1,0:T(8,128)(2,1)} %broadcast_in_dim.21), calls=%async_computation.10 | async-start | bytes 2490368 | tf_op jit(solution)/shard_map/all_to_all | solution.py:37
  313.3 1.0 copy-start.15
  313.3 7.8 %copy-start.17 = (bf16[4,296,128]{2,1,0:T(8,128)(2,1)S(1)}, bf16[4,296,128]{2,1,0:T(8,128)(2,1)}, u32[]{:S(2)}) copy-start(bf16[4,296,128]{2,1,0:T(8,128)(2,1)} %copy-done.16) | copy-start | bytes 909316
  315.1 18.4 %collective-permute-start.11 = (bf16[152,256]{1,0:T(8,128)(2,1)S(1)}, bf16[152,256]{1,0:T(8,128)(2,1)S(1)}, u32[]{:S(2)}, u32[]{:S(2)}) collective-permute-start(bf16[152,256]{1,0:T(8,128)(2,1)S(1)} %maximum_maximum_fusion), channel_id=1, source_target_pairs={{0,64},{64,0},{1,65},{65,1},{2,66},{66,2},{3,67},{67,3},{4,68},{68... | collective-permute-start | bytes 233480 | tf_op jit(solution)/shard_map/ppermute | solution.py:54
  334.6 24.3 %all-to-all-start.11 = ((bf16[16,152,256]{2,1,0:T(8,128)(2,1)}), bf16[16,152,256]{2,1,0:T(8,128)(2,1)S(1)}, u32[]{:S(2)}, u32[]{:S(2)}) async-start(bf16[16,152,256]{2,1,0:T(8,128)(2,1)} %broadcast_in_dim.22), calls=%async_computation.11 | async-start | bytes 2490368 | tf_op jit(solution)/shard_map/all_to_all | solution.py:37
  341.4 1.3 copy-start.22
  341.4 1.3 copy-start.23
  341.4 1.3 copy-start.24
  341.4 1.3 copy-start.25
  344.8 14.3 %copy-start.13 = (f32[1,128,128]{2,1,0:T(8,128)S(1)}, f32[1,128,128]{2,1,0:T(8,128)}, u32[]{:S(2)}) copy-start(f32[1,128,128]{2,1,0:T(8,128)} %param.10) | copy-start | bytes 196612
  360.4 3.6 copy-start.9
  360.4 3.6 copy-start.26
  360.4 3.6 copy-start.27

commit v7 on v5

--- a/solution.py
+++ b/solution.py
@@ -186,6 +186,7 @@
     panel_core, panel_mate = panel_core.reshape(HALF, COLS), panel_mate.reshape(HALF, COLS)
 
     quant_grad = mul(value_grad, tokens, first).astype(low)
+    quant_grad, value_grad = hold((quant_grad, value_grad))
     quant_grad = added(exchange(quant_grad.reshape(4, HEAD, COLS), ("x",)))
     mixed_grad = quant_grad * (1.0 - tangent * tangent)
     rotated_grad = mul(value_grad, heads)

time: 368 us -> 370 us (level)
  transfers between devices with their start and end apart: 24 -> 24, of which waited for: 18 -> 17; matrix products, arithmetic and copies ran while one was open for 9% -> 9% of each run, Pallas kernels for 0% -> 0%
where the time goes in v7:
time: 370 us; the launch traced here: 366 us
  starting transfers between devices  156 us (42%)
  waiting for transfers between devices  138 us (37%)
  local copies, waits for them, and re-layouts  24.8 us (7%)
  other arithmetic  22.5 us (6%)
  matrix products  18.4 us (5%)
  between operations  6.34 us (2%)
    all_to_all x12, waiting for transfers between devices, exchange(): out = lax.all_to_all(flat, axes, split_axis=0, concat_axis=0, tiled=True)  99.9 us
    ppermute x11, starting transfers between devices, swap(): return lax.ppermute(block, axis, [(i, i ^ bit) for i in range(n)])  76.7 us
    all_to_all x12, starting transfers between devices, exchange(): out = lax.all_to_all(flat, axes, split_axis=0, concat_axis=0, tiled=True)  74.6 us
    ppermute x11, waiting for transfers between devices, swap(): return lax.ppermute(block, axis, [(i, i ^ bit) for i in range(n)])  36 us
    dot_general x21, matrix products, mul(): lax.dot_general(a, b, dims, precision=precision, preferred_element_type=j...  17.1 us
    unnamed x70, local copies, waits for them, and re-layouts  8.06 us
  transfers between devices with their start and end apart: 24, of which 17 were waited for; matrix products, arithmetic and copies ran while one was open for 9% of the time, Pallas kernels for 0%

profile of v7, /device:TPU:1, one launch (start us, length us, event | category | flops | bytes accessed | tf_op | source)
XLA Modules:
  0.0 365.8 jit_solution(17958531460224630381)
XLA Ops:
  1.5 1.1 broadcast_in_dim.16
  2.7 7.7 %all-to-all-start = ((bf16[16,128,256]{2,1,0:T(8,128)(2,1)}), bf16[16,128,256]{2,1,0:T(8,128)(2,1)S(1)}, u32[]{:S(2)}, u32[]{:S(2)}) async-start(bf16[16,128,256]{2,1,0:T(8,128)(2,1)} %broadcast_in_dim.16), calls=%async_computation | async-start | bytes 2097152 | tf_op jit(solution)/shard_map/all_to_all | solution.py:37
  10.4 15.6 %collective-permute-start = (bf16[128,256]{1,0:T(8,128)(2,1)S(1)}, bf16[128,256]{1,0:T(8,128)(2,1)S(1)}, u32[]{:S(2)}, u32[]{:S(2)}) collective-permute-start(bf16[128,256]{1,0:T(8,128)(2,1)S(1)} %convert_element_type.202), channel_id=1, source_target_pairs={{0,64},{64,0},{1,65},{65,1},{2,66},{66,2},{3,67},{67,3},{4,68},{68... | collective-permute-start | bytes 196616 | tf_op jit(solution)/shard_map/ppermute | solution.py:54
  27.3 1.5 fusion.48
  31.4 1.1 broadcast_in_dim.17
  32.5 6.7 %all-to-all-start.1 = ((bf16[16,128,256]{2,1,0:T(8,128)(2,1)}), bf16[16,128,256]{2,1,0:T(8,128)(2,1)S(1)}, u32[]{:S(2)}, u32[]{:S(2)}) async-start(bf16[16,128,256]{2,1,0:T(8,128)(2,1)} %broadcast_in_dim.17), calls=%async_computation.1 | async-start | bytes 2097152 | tf_op jit(solution)/shard_map/all_to_all | solution.py:37
  41.4 12.8 %all-to-all-done.1 = bf16[16,128,256]{2,1,0:T(8,128)(2,1)S(1)} async-done(((bf16[16,128,256]{2,1,0:T(8,128)(2,1)}), bf16[16,128,256]{2,1,0:T(8,128)(2,1)S(1)}, u32[]{:S(2)}, u32[]{:S(2)}) %all-to-all-start.1) | async-done | bytes 1048608 | tf_op jit(solution)/shard_map/all_to_all | solution.py:37
  54.3 1.0 fusion.47
  57.7 6.3 %collective-permute-start.1 = (bf16[160,256]{1,0:T(8,128)(2,1)}, bf16[160,256]{1,0:T(8,128)(2,1)}, u32[]{:S(2)}, u32[]{:S(2)}) collective-permute-start(bf16[160,256]{1,0:T(8,128)(2,1)} %pad_maximum_fusion.12), channel_id=1, source_target_pairs={{0,64},{64,0},{1,65},{65,1},{2,66},{66,2},{3,67},{67,3},{4,68},{68... | collective-permute-start | bytes 245768 | tf_op jit(solution)/shard_map/ppermute | solution.py:54
  64.5 1.0 multiply_convert_fusion
  66.2 3.4 all-to-all-start.2
  69.7 1.4 convolution_convert_fusion.2
  71.1 3.7 %collective-permute-done.1 = bf16[160,256]{1,0:T(8,128)(2,1)} collective-permute-done((bf16[160,256]{1,0:T(8,128)(2,1)}, bf16[160,256]{1,0:T(8,128)(2,1)}, u32[]{:S(2)}, u32[]{:S(2)}) %collective-permute-start.1) | collective-permute-done | bytes 81952 | tf_op jit(solution)/shard_map/ppermute | solution.py:54
  75.7 1.0 convolution_convert_fusion.5
  76.7 14.1 %all-to-all-start.3 = ((bf16[16,16,512]{2,1,0:T(8,128)(2,1)}), bf16[16,16,512]{2,1,0:T(8,128)(2,1)}, u32[]{:S(2)}, u32[]{:S(2)}) async-start(bf16[16,16,512]{2,1,0:T(8,128)(2,1)} %bitcast.10), calls=%async_computation.3 | async-start | bytes 524288 | tf_op jit(solution)/shard_map/all_to_all | solution.py:37
  91.8 1.5 pad_maximum_fusion.2
  94.4 13.4 %all-to-all-done.3 = bf16[16,16,512]{2,1,0:T(8,128)(2,1)} async-done(((bf16[16,16,512]{2,1,0:T(8,128)(2,1)}), bf16[16,16,512]{2,1,0:T(8,128)(2,1)}, u32[]{:S(2)}, u32[]{:S(2)}) %all-to-all-start.3) | async-done | bytes 262176 | tf_op jit(solution)/shard_map/all_to_all | solution.py:37
  107.9 1.0 convert_reduce_fusion.3
  109.6 5.3 %all-to-all-start.4 = ((bf16[16,16,512]{2,1,0:T(8,128)(2,1)}), bf16[16,16,512]{2,1,0:T(8,128)(2,1)}, u32[]{:S(2)}, u32[]{:S(2)}) async-start(bf16[16,16,512]{2,1,0:T(8,128)(2,1)} %broadcast_in_dim.19), calls=%async_computation.4 | async-start | bytes 524288 | tf_op jit(solution)/shard_map/all_to_all | solution.py:37
  115.2 0.9 copy-done.7
  116.7 15.3 %all-to-all-done.4 = bf16[16,16,512]{2,1,0:T(8,128)(2,1)} async-done(((bf16[16,16,512]{2,1,0:T(8,128)(2,1)}), bf16[16,16,512]{2,1,0:T(8,128)(2,1)}, u32[]{:S(2)}, u32[]{:S(2)}) %all-to-all-start.4) | async-done | bytes 262176 | tf_op jit(solution)/shard_map/all_to_all | solution.py:37
  132.0 1.9 convolution_convert_fusion.4
  133.9 1.2 fusion.57
  135.9 6.6 %collective-permute-start.2 = (bf16[128,256]{1,0:T(8,128)(2,1)S(1)}, bf16[128,256]{1,0:T(8,128)(2,1)S(1)}, u32[]{:S(2)}, u32[]{:S(2)}) collective-permute-start(bf16[128,256]{1,0:T(8,128)(2,1)S(1)} %slice.497), channel_id=1, source_target_pairs={{0,64},{64,0},{1,65},{65,1},{2,66},{66,2},{3,67},{67,3},{4,68},{68... | collective-permute-start | bytes 196616 | tf_op jit(solution)/shard_map/ppermute | solution.py:54
  142.4 3.4 all-to-all-start.5
  145.9 6.4 %collective-permute-done.2 = bf16[128,256]{1,0:T(8,128)(2,1)S(1)} collective-permute-done((bf16[128,256]{1,0:T(8,128)(2,1)S(1)}, bf16[128,256]{1,0:T(8,128)(2,1)S(1)}, u32[]{:S(2)}, u32[]{:S(2)}) %collective-permute-start.2) | collective-permute-done | bytes 65568 | tf_op jit(solution)/shard_map/ppermute | solution.py:54
  153.2 1.2 fusion.53
  156.1 1.1 pad_maximum_fusion
  157.2 3.7 %all-to-all-start.6 = ((bf16[16,132,256]{2,1,0:T(8,128)(2,1)}), bf16[16,132,256]{2,1,0:T(8,128)(2,1)S(1)}, u32[]{:S(2)}, u32[]{:S(2)}) async-start(bf16[16,132,256]{2,1,0:T(8,128)(2,1)} %pad_maximum_fusion), calls=%async_computation.6 | async-start | bytes 2228224 | tf_op jit(solution)/shard_map/all_to_all | solution.py:37
  161.0 1.7 convolution_convert_fusion
  162.8 1.1 pad_maximum_fusion.1
  163.9 14.4 %all-to-all-done.6 = bf16[16,132,256]{2,1,0:T(8,128)(2,1)S(1)} async-done(((bf16[16,132,256]{2,1,0:T(8,128)(2,1)}), bf16[16,132,256]{2,1,0:T(8,128)(2,1)S(1)}, u32[]{:S(2)}, u32[]{:S(2)}) %all-to-all-start.6) | async-done | bytes 1081376 | tf_op jit(solution)/shard_map/all_to_all | solution.py:37
  178.2 1.0 copy-done.4
  179.2 3.7 %all-to-all-start.7 = ((bf16[16,132,256]{2,1,0:T(8,128)(2,1)}), bf16[16,132,256]{2,1,0:T(8,128)(2,1)S(1)}, u32[]{:S(2)}, u32[]{:S(2)}) async-start(bf16[16,132,256]{2,1,0:T(8,128)(2,1)} %pad_maximum_fusion.1), calls=%async_computation.7 | async-start | bytes 2228224 | tf_op jit(solution)/shard_map/all_to_all | solution.py:37
  183.8 1.4 slice_reduce_fusion
  185.2 8.0 %collective-permute-start.3 = (bf16[144,256]{1,0:T(8,128)(2,1)S(1)}, bf16[144,256]{1,0:T(8,128)(2,1)S(1)}, u32[]{:S(2)}, u32[]{:S(2)}) collective-permute-start(bf16[144,256]{1,0:T(8,128)(2,1)S(1)} %maximum_maximum_fusion.2), channel_id=1, source_target_pairs={{0,64},{64,0},{1,65},{65,1},{2,66},{66,2},{3,67},{67,3},{4,68},{68... | collective-permute-start | bytes 221192 | tf_op jit(solution)/shard_map/ppermute | solution.py:54
  193.2 7.9 %all-to-all-done.7 = bf16[16,132,256]{2,1,0:T(8,128)(2,1)S(1)} async-done(((bf16[16,132,256]{2,1,0:T(8,128)(2,1)}), bf16[16,132,256]{2,1,0:T(8,128)(2,1)S(1)}, u32[]{:S(2)}, u32[]{:S(2)}) %all-to-all-start.7) | async-done | bytes 1081376 | tf_op jit(solution)/shard_map/all_to_all | solution.py:37
  201.7 1.9 collective-permute-start.4
  203.6 1.9 collective-permute-done.4
  206.0 3.7 %collective-permute-start.5 = (bf16[1024,128]{1,0:T(8,128)(2,1)S(1)}, bf16[1024,128]{1,0:T(8,128)(2,1)S(1)}, u32[]{:S(2)}, u32[]{:S(2)}) collective-permute-start(bf16[1024,128]{1,0:T(8,128)(2,1)S(1)} %slice.496), channel_id=1, source_target_pairs={{0,2},{2,0},{1,3},{3,1},{4,6},{6,4},{5,7},{7,5},{8,10},{10,8},{9,1... | collective-permute-start | bytes 786440 | tf_op jit(solution)/shard_map/ppermute | solution.py:54
  209.7 6.4 %collective-permute-done.5 = bf16[1024,128]{1,0:T(8,128)(2,1)S(1)} collective-permute-done((bf16[1024,128]{1,0:T(8,128)(2,1)S(1)}, bf16[1024,128]{1,0:T(8,128)(2,1)S(1)}, u32[]{:S(2)}, u32[]{:S(2)}) %collective-permute-start.5) | collective-permute-done | bytes 262176 | tf_op jit(solution)/shard_map/ppermute | solution.py:54
  216.8 9.2 %all-to-all-start.8 = ((bf16[4,256,128]{2,1,0:T(8,128)(2,1)}), bf16[4,256,128]{2,1,0:T(8,128)(2,1)S(1)}, u32[]{:S(2)}, u32[]{:S(2)}) async-start(bf16[4,256,128]{2,1,0:T(8,128)(2,1)} %bitcast.199), calls=%async_computation.8 | async-start | bytes 524288 | tf_op jit(solution)/shard_map/all_to_all | solution.py:37
  226.6 14.9 %all-to-all-done.8 = bf16[4,256,128]{2,1,0:T(8,128)(2,1)S(1)} async-done(((bf16[4,256,128]{2,1,0:T(8,128)(2,1)}), bf16[4,256,128]{2,1,0:T(8,128)(2,1)S(1)}, u32[]{:S(2)}, u32[]{:S(2)}) %all-to-all-start.8) | async-done | bytes 262176 | tf_op jit(solution)/shard_map/all_to_all | solution.py:37
  241.6 4.8 %collective-permute-start.6 = (bf16[256,128]{1,0:T(8,128)(2,1)S(1)}, bf16[256,128]{1,0:T(8,128)(2,1)S(1)}, u32[]{:S(2)}, u32[]{:S(2)}) collective-permute-start(bf16[256,128]{1,0:T(8,128)(2,1)S(1)} %convert_element_type.233), channel_id=1, source_target_pairs={{0,0},{1,33},{2,66},{3,99},{4,132},{5,165},{6,198},{7,231},{8,264}... | collective-permute-start | bytes 196616 | tf_op jit(solution)/shard_map/ppermute | solution.py:224
  246.5 1.7 collective-permute-done.6
  248.2 3.3 collective-permute-start.7
  255.9 5.5 %all-to-all-start.9 = ((bf16[4,296,128]{2,1,0:T(8,128)(2,1)}), bf16[4,296,128]{2,1,0:T(8,128)(2,1)S(1)}, u32[]{:S(2)}, u32[]{:S(2)}) async-start(bf16[4,296,128]{2,1,0:T(8,128)(2,1)} %broadcast_in_dim.20), calls=%async_computation.9 | async-start | bytes 606208 | tf_op jit(solution)/shard_map/all_to_all | solution.py:37
  263.2 7.4 %all-to-all-done.9 = bf16[4,296,128]{2,1,0:T(8,128)(2,1)S(1)} async-done(((bf16[4,296,128]{2,1,0:T(8,128)(2,1)}), bf16[4,296,128]{2,1,0:T(8,128)(2,1)S(1)}, u32[]{:S(2)}, u32[]{:S(2)}) %all-to-all-start.9) | async-done | bytes 303136 | tf_op jit(solution)/shard_map/all_to_all | solution.py:37
  270.6 5.8 %collective-permute-start.8 = (bf16[4,296,128]{2,1,0:T(8,128)(2,1)S(1)}, bf16[4,296,128]{2,1,0:T(8,128)(2,1)S(1)}, u32[]{:S(2)}, u32[]{:S(2)}) collective-permute-start(bf16[4,296,128]{2,1,0:T(8,128)(2,1)S(1)} %all-to-all-done.9), channel_id=1, source_target_pairs={{0,1},{1,0},{2,3},{3,2},{4,5},{5,4},{6,7},{7,6},{8,9},{9,8},{10,11... | collective-permute-start | bytes 909320 | tf_op jit(solution)/shard_map/ppermute | solution.py:54
  276.4 16.5 %collective-permute-start.9 = (bf16[4,296,128]{2,1,0:T(8,128)(2,1)S(1)}, bf16[4,296,128]{2,1,0:T(8,128)(2,1)S(1)}, u32[]{:S(2)}, u32[]{:S(2)}) collective-permute-start(bf16[4,296,128]{2,1,0:T(8,128)(2,1)S(1)} %all-to-all-done.9), channel_id=1, source_target_pairs={{0,2},{2,0},{1,3},{3,1},{4,6},{6,4},{5,7},{7,5},{8,10},{10,8},{9,1... | collective-permute-start | bytes 909320 | tf_op jit(solution)/shard_map/ppermute | solution.py:54
  293.0 1.4 fusion.58
  295.7 4.8 %collective-permute-done.9 = bf16[4,296,128]{2,1,0:T(8,128)(2,1)S(1)} collective-permute-done((bf16[4,296,128]{2,1,0:T(8,128)(2,1)S(1)}, bf16[4,296,128]{2,1,0:T(8,128)(2,1)S(1)}, u32[]{:S(2)}, u32[]{:S(2)}) %collective-permute-start.9) | collective-permute-done | bytes 303136 | tf_op jit(solution)/shard_map/ppermute | solution.py:54
  300.5 2.5 collective-permute-start.10
  306.3 1.0 fusion.54
  307.4 1.2 broadcast_in_dim.21
  308.6 5.4 %all-to-all-start.10 = ((bf16[16,152,256]{2,1,0:T(8,128)(2,1)}), bf16[16,152,256]{2,1,0:T(8,128)(2,1)S(1)}, u32[]{:S(2)}, u32[]{:S(2)}) async-start(bf16[16,152,256]{2,1,0:T(8,128)(2,1)} %broadcast_in_dim.21), calls=%async_computation.10 | async-start | bytes 2490368 | tf_op jit(solution)/shard_map/all_to_all | solution.py:37
  315.7 6.5 %collective-permute-start.11 = (bf16[152,256]{1,0:T(8,128)(2,1)S(1)}, bf16[152,256]{1,0:T(8,128)(2,1)S(1)}, u32[]{:S(2)}, u32[]{:S(2)}) collective-permute-start(bf16[152,256]{1,0:T(8,128)(2,1)S(1)} %maximum_maximum_fusion), channel_id=1, source_target_pairs={{0,64},{64,0},{1,65},{65,1},{2,66},{66,2},{3,67},{67,3},{4,68},{68... | collective-permute-start | bytes 233480 | tf_op jit(solution)/shard_map/ppermute | solution.py:54
  323.2 11.3 %collective-permute-done.11 = bf16[152,256]{1,0:T(8,128)(2,1)S(1)} collective-permute-done((bf16[152,256]{1,0:T(8,128)(2,1)S(1)}, bf16[152,256]{1,0:T(8,128)(2,1)S(1)}, u32[]{:S(2)}, u32[]{:S(2)}) %collective-permute-start.11) | collective-permute-done | bytes 77856 | tf_op jit(solution)/shard_map/ppermute | solution.py:54
  334.5 1.2 broadcast_in_dim.22
  335.7 6.7 %all-to-all-start.11 = ((bf16[16,152,256]{2,1,0:T(8,128)(2,1)}), bf16[16,152,256]{2,1,0:T(8,128)(2,1)S(1)}, u32[]{:S(2)}, u32[]{:S(2)}) async-start(bf16[16,152,256]{2,1,0:T(8,128)(2,1)} %broadcast_in_dim.22), calls=%async_computation.11 | async-start | bytes 2490368 | tf_op jit(solution)/shard_map/all_to_all | solution.py:37
  342.4 1.2 maximum_select_fusion.9
  343.7 1.2 broadcast_select_fusion
  346.0 13.8 %all-to-all-done.11 = bf16[16,152,256]{2,1,0:T(8,128)(2,1)S(1)} async-done(((bf16[16,152,256]{2,1,0:T(8,128)(2,1)}), bf16[16,152,256]{2,1,0:T(8,128)(2,1)S(1)}, u32[]{:S(2)}, u32[]{:S(2)}) %all-to-all-start.11) | async-done | bytes 1245216 | tf_op jit(solution)/shard_map/all_to_all | solution.py:37
  364.8 1.0 subtract_add_fusion
  (190 shorter events, 37.0 us)
Async XLA Ops:
  2.6 23.4 %copy-start.31 = (bf16[1,128,1024]{2,1,0:T(8,128)(2,1)S(1)}, bf16[1,128,1024]{2,1,0:T(8,128)(2,1)}, u32[]{:S(2)}) copy-start(bf16[1,128,1024]{2,1,0:T(8,128)(2,1)} %param.7) | copy-start | bytes 786436
  2.7 28.7 %all-to-all-start = ((bf16[16,128,256]{2,1,0:T(8,128)(2,1)}), bf16[16,128,256]{2,1,0:T(8,128)(2,1)S(1)}, u32[]{:S(2)}, u32[]{:S(2)}) async-start(bf16[16,128,256]{2,1,0:T(8,128)(2,1)} %broadcast_in_dim.16), calls=%async_computation | async-start | bytes 2097152 | tf_op jit(solution)/shard_map/all_to_all | solution.py:37
  10.4 16.1 %copy-start.20 = (bf16[1,128,4096]{2,1,0:T(8,128)(2,1)S(1)}, bf16[1,128,4096]{2,1,0:T(8,128)(2,1)}, u32[]{:S(2)}) copy-start(bf16[1,128,4096]{2,1,0:T(8,128)(2,1)} %param.6) | copy-start | bytes 3145732
  10.4 21.0 %collective-permute-start = (bf16[128,256]{1,0:T(8,128)(2,1)S(1)}, bf16[128,256]{1,0:T(8,128)(2,1)S(1)}, u32[]{:S(2)}, u32[]{:S(2)}) collective-permute-start(bf16[128,256]{1,0:T(8,128)(2,1)S(1)} %convert_element_type.202), channel_id=1, source_target_pairs={{0,64},{64,0},{1,65},{65,1},{2,66},{66,2},{3,67},{67,3},{4,68},{68... | collective-permute-start | bytes 196616 | tf_op jit(solution)/shard_map/ppermute | solution.py:54
  29.3 1.9 copy-start.19
  32.5 21.7 %all-to-all-start.1 = ((bf16[16,128,256]{2,1,0:T(8,128)(2,1)}), bf16[16,128,256]{2,1,0:T(8,128)(2,1)S(1)}, u32[]{:S(2)}, u32[]{:S(2)}) async-start(bf16[16,128,256]{2,1,0:T(8,128)(2,1)} %broadcast_in_dim.17), calls=%async_computation.1 | async-start | bytes 2097152 | tf_op jit(solution)/shard_map/all_to_all | solution.py:37
  54.3 1.2 copy-start.2
  55.3 1.1 copy-start
  57.7 6.7 %copy-start.13 = (f32[1,128,128]{2,1,0:T(8,128)S(1)}, f32[1,128,128]{2,1,0:T(8,128)}, u32[]{:S(2)}) copy-start(f32[1,128,128]{2,1,0:T(8,128)} %param.10) | copy-start | bytes 196612
  57.7 6.7 %copy-start.32 = (f32[1,128]{1,0:T(1,128)S(1)}, f32[1,128]{1,0:T(1,128)}, u32[]{:S(2)}) copy-start(f32[1,128]{1,0:T(1,128)} %param.9) | copy-start | bytes 1540
  57.7 17.1 %collective-permute-start.1 = (bf16[160,256]{1,0:T(8,128)(2,1)}, bf16[160,256]{1,0:T(8,128)(2,1)}, u32[]{:S(2)}, u32[]{:S(2)}) collective-permute-start(bf16[160,256]{1,0:T(8,128)(2,1)} %pad_maximum_fusion.12), channel_id=1, source_target_pairs={{0,64},{64,0},{1,65},{65,1},{2,66},{66,2},{3,67},{67,3},{4,68},{68... | collective-permute-start | bytes 245768 | tf_op jit(solution)/shard_map/ppermute | solution.py:54
  64.5 1.8 copy-start.22
  66.2 9.4 %all-to-all-start.2 = ((bf16[4,128,256]{2,1,0:T(8,128)(2,1)}), bf16[4,128,256]{2,1,0:T(8,128)(2,1)S(1)}, u32[]{:S(2)}, u32[]{:S(2)}) async-start(bf16[4,128,256]{2,1,0:T(8,128)(2,1)} %broadcast_in_dim.18), calls=%async_computation.2 | async-start | bytes 524288 | tf_op jit(solution)/shard_map/all_to_all | solution.py:37
  71.1 20.3 %copy-start.1 = (bf16[16,8,4,512]{3,1,2,0:T(8,128)(2,1)S(1)}, bf16[16,8,4,512]{3,1,2,0:T(8,128)(2,1)}, u32[]{:S(2)}) copy-start(bf16[16,8,4,512]{3,1,2,0:T(8,128)(2,1)} %copy.120) | copy-start | bytes 1572868
  71.1 20.3 %copy-start.3 = (bf16[16,8,4,512]{3,1,2,0:T(8,128)(2,1)S(1)}, bf16[16,8,4,512]{3,1,2,0:T(8,128)(2,1)}, u32[]{:S(2)}) copy-start(bf16[16,8,4,512]{3,1,2,0:T(8,128)(2,1)} %copy.119) | copy-start | bytes 1572868
  75.7 15.1 %copy-start.29 = (bf16[128,256]{1,0:T(8,128)(2,1)}, bf16[128,256]{1,0:T(8,128)(2,1)S(1)}, u32[]{:S(2)}) copy-start(bf16[128,256]{1,0:T(8,128)(2,1)S(1)} %slice.344) | copy-start | bytes 196612
  76.7 31.2 %all-to-all-start.3 = ((bf16[16,16,512]{2,1,0:T(8,128)(2,1)}), bf16[16,16,512]{2,1,0:T(8,128)(2,1)}, u32[]{:S(2)}, u32[]{:S(2)}) async-start(bf16[16,16,512]{2,1,0:T(8,128)(2,1)} %bitcast.10), calls=%async_computation.3 | async-start | bytes 524288 | tf_op jit(solution)/shard_map/all_to_all | solution.py:37
  90.8 1.0 copy-start.12
  91.8 1.5 copy-start.10
  91.8 1.6 copy-start.11
  109.6 22.4 %all-to-all-start.4 = ((bf16[16,16,512]{2,1,0:T(8,128)(2,1)}), bf16[16,16,512]{2,1,0:T(8,128)(2,1)}, u32[]{:S(2)}, u32[]{:S(2)}) async-start(bf16[16,16,512]{2,1,0:T(8,128)(2,1)} %broadcast_in_dim.19), calls=%async_computation.4 | async-start | bytes 524288 | tf_op jit(solution)/shard_map/all_to_all | solution.py:37
  115.1 1.0 copy-start.7
  115.1 1.2 copy-start.8
  116.3 15.7 %copy-start.30 = (bf16[128,256]{1,0:T(8,128)(2,1)S(1)}, bf16[128,256]{1,0:T(8,128)(2,1)}, u32[]{:S(2)}) copy-start(bf16[128,256]{1,0:T(8,128)(2,1)} %copy-done.29) | copy-start | bytes 196612
  135.1 0.7 copy-start.21
  135.8 19.8 %copy-start.5 = (bf16[256,2048]{1,0:T(8,128)(2,1)S(1)}, bf16[256,2048]{1,0:T(8,128)(2,1)}, u32[]{:S(2)}) copy-start(bf16[256,2048]{1,0:T(8,128)(2,1)} %get-tuple-element.42) | copy-start | bytes 3145732
  135.9 16.4 %collective-permute-start.2 = (bf16[128,256]{1,0:T(8,128)(2,1)S(1)}, bf16[128,256]{1,0:T(8,128)(2,1)S(1)}, u32[]{:S(2)}, u32[]{:S(2)}) collective-permute-start(bf16[128,256]{1,0:T(8,128)(2,1)S(1)} %slice.497), channel_id=1, source_target_pairs={{0,64},{64,0},{1,65},{65,1},{2,66},{66,2},{3,67},{67,3},{4,68},{68... | collective-permute-start | bytes 196616 | tf_op jit(solution)/shard_map/ppermute | solution.py:54
  142.4 10.7 %all-to-all-start.5 = ((bf16[4,128,256]{2,1,0:T(8,128)(2,1)}), bf16[4,128,256]{2,1,0:T(8,128)(2,1)S(1)}, u32[]{:S(2)}, u32[]{:S(2)}) async-start(bf16[4,128,256]{2,1,0:T(8,128)(2,1)} %bitcast.203), calls=%async_computation.5 | async-start | bytes 524288 | tf_op jit(solution)/shard_map/all_to_all | solution.py:37
  157.2 21.0 %all-to-all-start.6 = ((bf16[16,132,256]{2,1,0:T(8,128)(2,1)}), bf16[16,132,256]{2,1,0:T(8,128)(2,1)S(1)}, u32[]{:S(2)}, u32[]{:S(2)}) async-start(bf16[16,132,256]{2,1,0:T(8,128)(2,1)} %pad_maximum_fusion), calls=%async_computation.6 | async-start | bytes 2228224 | tf_op jit(solution)/shard_map/all_to_all | solution.py:37
  178.2 1.0 copy-start.4
  179.2 21.8 %all-to-all-start.7 = ((bf16[16,132,256]{2,1,0:T(8,128)(2,1)}), bf16[16,132,256]{2,1,0:T(8,128)(2,1)S(1)}, u32[]{:S(2)}, u32[]{:S(2)}) async-start(bf16[16,132,256]{2,1,0:T(8,128)(2,1)} %pad_maximum_fusion.1), calls=%async_computation.7 | async-start | bytes 2228224 | tf_op jit(solution)/shard_map/all_to_all | solution.py:37
  185.2 16.0 %collective-permute-start.3 = (bf16[144,256]{1,0:T(8,128)(2,1)S(1)}, bf16[144,256]{1,0:T(8,128)(2,1)S(1)}, u32[]{:S(2)}, u32[]{:S(2)}) collective-permute-start(bf16[144,256]{1,0:T(8,128)(2,1)S(1)} %maximum_maximum_fusion.2), channel_id=1, source_target_pairs={{0,64},{64,0},{1,65},{65,1},{2,66},{66,2},{3,67},{67,3},{4,68},{68... | collective-permute-start | bytes 221192 | tf_op jit(solution)/shard_map/ppermute | solution.py:54
  201.7 3.8 %collective-permute-start.4 = (bf16[2048,128]{1,0:T(8,128)(2,1)S(1)}, bf16[2048,128]{1,0:T(8,128)(2,1)S(1)}, u32[]{:S(2)}, u32[]{:S(2)}) collective-permute-start(bf16[2048,128]{1,0:T(8,128)(2,1)S(1)} %fusion.1), channel_id=1, source_target_pairs={{0,1},{1,0},{2,3},{3,2},{4,5},{5,4},{6,7},{7,6},{8,9},{9,8},{10,11... | collective-permute-start | bytes 1572872 | tf_op jit(solution)/shard_map/ppermute | solution.py:54
  206.0 10.1 %collective-permute-start.5 = (bf16[1024,128]{1,0:T(8,128)(2,1)S(1)}, bf16[1024,128]{1,0:T(8,128)(2,1)S(1)}, u32[]{:S(2)}, u32[]{:S(2)}) collective-permute-start(bf16[1024,128]{1,0:T(8,128)(2,1)S(1)} %slice.496), channel_id=1, source_target_pairs={{0,2},{2,0},{1,3},{3,1},{4,6},{6,4},{5,7},{7,5},{8,10},{10,8},{9,1... | collective-permute-start | bytes 786440 | tf_op jit(solution)/shard_map/ppermute | solution.py:54
  216.8 24.8 %all-to-all-start.8 = ((bf16[4,256,128]{2,1,0:T(8,128)(2,1)}), bf16[4,256,128]{2,1,0:T(8,128)(2,1)S(1)}, u32[]{:S(2)}, u32[]{:S(2)}) async-start(bf16[4,256,128]{2,1,0:T(8,128)(2,1)} %bitcast.199), calls=%async_computation.8 | async-start | bytes 524288 | tf_op jit(solution)/shard_map/all_to_all | solution.py:37
  241.6 6.5 %collective-permute-start.6 = (bf16[256,128]{1,0:T(8,128)(2,1)S(1)}, bf16[256,128]{1,0:T(8,128)(2,1)S(1)}, u32[]{:S(2)}, u32[]{:S(2)}) collective-permute-start(bf16[256,128]{1,0:T(8,128)(2,1)S(1)} %convert_element_type.233), channel_id=1, source_target_pairs={{0,0},{1,33},{2,66},{3,99},{4,132},{5,165},{6,198},{7,231},{8,264}... | collective-permute-start | bytes 196616 | tf_op jit(solution)/shard_map/ppermute | solution.py:224
  248.2 4.7 %collective-permute-start.7 = (bf16[128,128]{1,0:T(8,128)(2,1)S(1)}, bf16[128,128]{1,0:T(8,128)(2,1)S(1)}, u32[]{:S(2)}, u32[]{:S(2)}) collective-permute-start(bf16[128,128]{1,0:T(8,128)(2,1)S(1)} %get-tuple-element.99), channel_id=1, source_target_pairs={{0,16},{16,0},{32,48},{48,32},{1,17},{17,1},{33,49},{49,33},{2,18}... | collective-permute-start | bytes 98312 | tf_op jit(solution)/shard_map/ppermute | solution.py:54
  255.9 14.6 %all-to-all-start.9 = ((bf16[4,296,128]{2,1,0:T(8,128)(2,1)}), bf16[4,296,128]{2,1,0:T(8,128)(2,1)S(1)}, u32[]{:S(2)}, u32[]{:S(2)}) async-start(bf16[4,296,128]{2,1,0:T(8,128)(2,1)} %broadcast_in_dim.20), calls=%async_computation.9 | async-start | bytes 606208 | tf_op jit(solution)/shard_map/all_to_all | solution.py:37
  270.6 23.7 %collective-permute-start.8 = (bf16[4,296,128]{2,1,0:T(8,128)(2,1)S(1)}, bf16[4,296,128]{2,1,0:T(8,128)(2,1)S(1)}, u32[]{:S(2)}, u32[]{:S(2)}) collective-permute-start(bf16[4,296,128]{2,1,0:T(8,128)(2,1)S(1)} %all-to-all-done.9), channel_id=1, source_target_pairs={{0,1},{1,0},{2,3},{3,2},{4,5},{5,4},{6,7},{7,6},{8,9},{9,8},{10,11... | collective-permute-start | bytes 909320 | tf_op jit(solution)/shard_map/ppermute | solution.py:54
  276.4 24.1 %collective-permute-start.9 = (bf16[4,296,128]{2,1,0:T(8,128)(2,1)S(1)}, bf16[4,296,128]{2,1,0:T(8,128)(2,1)S(1)}, u32[]{:S(2)}, u32[]{:S(2)}) collective-permute-start(bf16[4,296,128]{2,1,0:T(8,128)(2,1)S(1)} %all-to-all-done.9), channel_id=1, source_target_pairs={{0,2},{2,0},{1,3},{3,1},{4,6},{6,4},{5,7},{7,5},{8,10},{10,8},{9,1... | collective-permute-start | bytes 909320 | tf_op jit(solution)/shard_map/ppermute | solution.py:54
  294.4 1.1 copy-start.6
  300.5 6.8 %copy-start.15 = (bf16[4,296,128]{2,1,0:T(8,128)(2,1)}, bf16[4,296,128]{2,1,0:T(8,128)(2,1)S(1)}, u32[]{:S(2)}) copy-start(bf16[4,296,128]{2,1,0:T(8,128)(2,1)S(1)} %collective-permute-done.9) | copy-start | bytes 909316
  300.5 3.7 %collective-permute-start.10 = (bf16[4,296,128]{2,1,0:T(8,128)(2,1)S(1)}, bf16[4,296,128]{2,1,0:T(8,128)(2,1)S(1)}, u32[]{:S(2)}, u32[]{:S(2)}) collective-permute-start(bf16[4,296,128]{2,1,0:T(8,128)(2,1)S(1)} %collective-permute-done.9), channel_id=1, source_target_pairs={{0,1},{1,0},{2,3},{3,2},{4,5},{5,4},{6,7},{7,6},{8,9},{9,8},{10,11... | collective-permute-start | bytes 909320 | tf_op jit(solution)/shard_map/ppermute | solution.py:54
  304.2 4.3 %copy-start.17 = (bf16[4,296,128]{2,1,0:T(8,128)(2,1)}, bf16[4,296,128]{2,1,0:T(8,128)(2,1)S(1)}, u32[]{:S(2)}) copy-start(bf16[4,296,128]{2,1,0:T(8,128)(2,1)S(1)} %collective-permute-done.10) | copy-start | bytes 909316
  308.6 26.0 %all-to-all-start.10 = ((bf16[16,152,256]{2,1,0:T(8,128)(2,1)}), bf16[16,152,256]{2,1,0:T(8,128)(2,1)S(1)}, u32[]{:S(2)}, u32[]{:S(2)}) async-start(bf16[16,152,256]{2,1,0:T(8,128)(2,1)} %broadcast_in_dim.21), calls=%async_computation.10 | async-start | bytes 2490368 | tf_op jit(solution)/shard_map/all_to_all | solution.py:37
  313.9 1.0 copy-start.16
  314.0 8.3 %copy-start.18 = (bf16[4,296,128]{2,1,0:T(8,128)(2,1)S(1)}, bf16[4,296,128]{2,1,0:T(8,128)(2,1)}, u32[]{:S(2)}) copy-start(bf16[4,296,128]{2,1,0:T(8,128)(2,1)} %copy-done.17) | copy-start | bytes 909316
  315.7 18.8 %collective-permute-start.11 = (bf16[152,256]{1,0:T(8,128)(2,1)S(1)}, bf16[152,256]{1,0:T(8,128)(2,1)S(1)}, u32[]{:S(2)}, u32[]{:S(2)}) collective-permute-start(bf16[152,256]{1,0:T(8,128)(2,1)S(1)} %maximum_maximum_fusion), channel_id=1, source_target_pairs={{0,64},{64,0},{1,65},{65,1},{2,66},{66,2},{3,67},{67,3},{4,68},{68... | collective-permute-start | bytes 233480 | tf_op jit(solution)/shard_map/ppermute | solution.py:54
  335.7 24.2 %all-to-all-start.11 = ((bf16[16,152,256]{2,1,0:T(8,128)(2,1)}), bf16[16,152,256]{2,1,0:T(8,128)(2,1)S(1)}, u32[]{:S(2)}, u32[]{:S(2)}) async-start(bf16[16,152,256]{2,1,0:T(8,128)(2,1)} %broadcast_in_dim.22), calls=%async_computation.11 | async-start | bytes 2490368 | tf_op jit(solution)/shard_map/all_to_all | solution.py:37
  342.3 1.3 copy-start.23
  342.3 1.3 copy-start.24
  342.4 1.3 copy-start.25
  342.4 1.3 copy-start.26
  345.7 14.3 %copy-start.14 = (f32[1,128,128]{2,1,0:T(8,128)S(1)}, f32[1,128,128]{2,1,0:T(8,128)}, u32[]{:S(2)}) copy-start(f32[1,128,128]{2,1,0:T(8,128)} %param.10) | copy-start | bytes 196612
  361.2 3.5 copy-start.9
  361.2 3.5 copy-start.27
  361.2 3.5 copy-start.28
